TPU v7x, 32 devices: a whole 2x2x4 slice. The times are simulated.
32 devices in a mesh: parts: 2 (over y), tp: 4 (over z), page: 2 (over x), sub: 2 (over core).
Axes of the slice: x: 2, y: 2, z: 4, core: 2. Of those that a mesh axis runs over, the one named last changes fastest.
Arguments:
- hidden_units: bfloat16 [128, 33792], P('parts', 'tp'), parts along dimension 0, may hold values from -6 to 6
- adapter_ids: int32 [128], P('parts'), parts along dimension 0, may hold values from 0 to 3
- down_projection_weight: bfloat16 [33792, 12288], P('tp', ('page', 'sub')), may hold values from -0.03125 to 0.03125
- rank_down: bfloat16 [8, 33792, 64], P(('parts', 'page', 'sub'), 'tp'), parts along dimension 0, may hold values from -0.03125 to 0.03125
- rank_up: bfloat16 [8, 64, 12288], P(('parts', 'tp'), None, ('page', 'sub')), parts along dimension 0, may hold values from -0.75 to 0.75
- residual: bfloat16 [128, 12288], P(('parts', 'tp'), ('page', 'sub')), parts along dimension 0, may hold values from -6 to 6
Outputs:
- mixed: bfloat16 [128, 12288], P(('parts', 'tp'), ('page', 'sub')), parts along dimension 0
There are 2 independent parts, one for each index of `parts`. A program takes and returns all parts, laid end to end along the dimension named above; an argument that names none is the same for every part. Nothing has to cross between parts.
All inputs are finite; a program needn't handle non-finite values.
Results may differ from a plain program's by a relative error of at most 0.0095.
Values may be sent and summed in bfloat16 or wider, within the bound.
No kernel may reach another device: no remote copies, remote signals or barrier semaphores. Data moves between devices by JAX's collectives and lax.ppermute only.
A program may use at most 128 MiB of HBM per device.

v0:
```python
import jax
import jax.numpy as jnp
from jax import lax
from jax.sharding import PartitionSpec as P


def on_device(hidden_units, adapter_ids, down_projection_weight, rank_down, rank_up, residual):
    owned_count = rank_down.shape[0]
    first_owned = lax.axis_index(("page", "sub")) * owned_count
    chosen = (
        (adapter_ids - first_owned)[:, None] == jnp.arange(owned_count, dtype=jnp.int32)[None, :]
    ).astype(jnp.float32)
    projected = jnp.einsum(
        "rf,afk->rak", hidden_units, rank_down, preferred_element_type=jnp.float32
    )
    partial_low = jnp.einsum("rak,ra->rk", projected, chosen)
    low_rank = lax.psum(partial_low, ("tp", "page", "sub")).astype(jnp.bfloat16)
    held_count = rank_up.shape[0]
    rank_width = rank_up.shape[1]
    first_held = lax.axis_index("tp") * held_count
    flattened = rank_up.reshape(held_count * rank_width, rank_up.shape[2])
    held_row_interval = jnp.arange(held_count, dtype=jnp.int32)
    rows_dev = residual.shape[0]
    picked = ((adapter_ids - first_held)[:, None] == held_row_interval[None, :]).astype(
        jnp.bfloat16
    )
    low_rank_coefficient = (picked[:, :, None] * low_rank[:, None, :]).reshape(
        lax.axis_size("tp") * rows_dev, held_count * rank_width
    )
    base_projection_term = jnp.dot(
        hidden_units, down_projection_weight, preferred_element_type=jnp.float32
    )
    summed = lax.psum_scatter(
        (
            base_projection_term
            + jnp.dot(low_rank_coefficient, flattened, preferred_element_type=jnp.float32)
        ).astype(jnp.bfloat16),
        "tp",
        scatter_dimension=0,
        tiled=True,
    ).astype(jnp.float32)
    return (residual.astype(jnp.float32) + summed).astype(jnp.bfloat16)


def solution(mesh):
    placed = (
        P("parts", "tp"),
        P("parts"),
        P("tp", ("page", "sub")),
        P(("parts", "page", "sub"), "tp", None),
        P(("parts", "tp"), None, ("page", "sub")),
        P(("parts", "tp"), ("page", "sub")),
    )
    return jax.shard_map(
        on_device,
        mesh=mesh,
        in_specs=placed,
        out_specs=P(("parts", "tp"), ("page", "sub")),
        check_vma=False,
    )
```

profile of v0, /device:TPU:0, one launch (start us, length us, event | category | flops | bytes accessed | tf_op | source)
XLA Modules:
  0.0 120.5 jit_solution(10450394117147217585)
XLA Ops:
  6.5 0.0 copy-start
  6.5 0.0 reduce-scatter.2.cloned.1.call-start
  6.5 0.7 compare_convert_fusion.1
  7.3 0.5 copy-done
  7.8 1.7 %convolution_multiply_fusion = f32[64,64]{1,0:T(8,128)S(1)} fusion(bf16[64,8448]{1,0:T(8,128)(2,1)S(1)} %copy-done, bf16[1,8448,64]{1,2,0:T(8,128)(2,1)} %param.9, f32[64]{0:T(128)S(1)} %get-tuple-element.6), kind=kOutput, calls=%fused_computation.2 | convolution fusion | flops 69210112 | bytes 2179328 | tf_op jit(solution)/shard_map/rf,afk->rak/dot_general | solution.py:13
  9.5 62.9 %psum.7 = bf16[64,64]{1,0:T(8,128)(2,1)S(1)} all-reduce(f32[64,64]{1,0:T(8,128)S(1)} %convolution_multiply_fusion), channel_id=1, replica_groups=mesh['parts'=2,'tp'=4,'page'=2,'sub'=2] {'tp','page','sub'}, use_global_device_ids=true, to_apply=%region_0.0 | all-reduce | flops 4096 | bytes 24576 | tf_op jit(solution)/shard_map/psum | solution.py:17
  72.4 0.0 copy-start.1
  72.4 20.5 %fusion.6 = f32[64,3072]{1,0:T(8,128)S(1)} fusion(bf16[64,8448]{1,0:T(8,128)(2,1)S(1)} %copy-done, bf16[8448,3072]{1,0:T(8,128)(2,1)} %param.8), kind=kOutput, calls=%fused_computation.11 | convolution fusion | flops 3321888768 | bytes 53772288 | tf_op jit(solution)/shard_map/dot_general | solution.py:30
  92.9 0.0 copy-start.2
  93.0 0.0 copy-done.1
  93.0 1.0 fusion
  94.0 0.0 reduce-scatter.2.cloned.1.call-update
  94.0 18.0 %reduce-scatter.2.cloned.1.call-done = bf16[16,3072]{1,0:T(8,128)(2,1)} async-done(((bf16[64,3072]{1,0:T(8,128)(2,1)}), bf16[16,3072]{1,0:T(8,128)(2,1)}) %reduce-scatter.2.cloned.1.call-update) | async-done | bytes 98320 | tf_op jit(solution)/shard_map/reduce_scatter | solution.py:33
  112.1 0.0 copy-done.2
  112.1 1.6 %add_convert_fusion = bf16[16,3072]{1,0:T(8,128)(2,1)} fusion(bf16[16,3072]{1,0:T(8,128)(2,1)} %reduce-scatter.2.cloned.1.call-done, bf16[16,3072]{1,0:T(8,128)(2,1)S(1)} %copy-done.2), kind=kLoop, calls=%fused_computation.5 | loop fusion | flops 196608 | bytes 294912 | tf_op jit(solution)/shard_map/convert_element_type | solution.py:42
Async XLA Ops:
  6.5 1.3 %copy-start = (bf16[64,8448]{1,0:T(8,128)(2,1)S(1)}, bf16[64,8448]{1,0:T(8,128)(2,1)}, u32[]{:S(2)}) copy-start(bf16[64,8448]{1,0:T(8,128)(2,1)} %param.6) | copy-start | bytes 3244036
  6.5 105.5 %reduce-scatter.2.cloned.1.call-start = ((), (), s32[]{:S(2)}) async-start(), calls=%async_computation.1 | async-start | bytes 491520 | tf_op jit(solution)/shard_map/reduce_scatter | solution.py:33
  72.4 20.6 %copy-start.1 = (bf16[1,64,3072]{2,1,0:T(8,128)(2,1)S(1)}, bf16[1,64,3072]{2,1,0:T(8,128)(2,1)}, u32[]{:S(2)}) copy-start(bf16[1,64,3072]{2,1,0:T(8,128)(2,1)} %param.10) | copy-start | bytes 1179652
  92.9 19.1 %copy-start.2 = (bf16[16,3072]{1,0:T(8,128)(2,1)S(1)}, bf16[16,3072]{1,0:T(8,128)(2,1)}, u32[]{:S(2)}) copy-start(bf16[16,3072]{1,0:T(8,128)(2,1)} %param.11) | copy-start | bytes 294916
Sparse Core Ops, SparseCore 0:
  94.2 17.8 reduce-scatter.1
where the time goes:
time: 121 us; the launch traced here: 120 us
  blocking collectives  62.9 us (52%)
  matrix products  23.3 us (19%)
  waiting for transfers between devices  18 us (15%)
  between operations  13.4 us (11%)
  other arithmetic  2.31 us (2%)
    psum x1, blocking collectives, on_device(): low_rank = lax.psum(partial_low, ('tp', 'page', 'sub')).astype(jnp.bfloat16)  62.9 us
    dot_general x1, matrix products, on_device(): jnp.dot(hidden_units, down_projection_weight, preferred_element_type=jnp....  20.5 us
    reduce_scatter x1, waiting for transfers between devices, on_device(): lax.psum_scatter((base_projection_term + jnp.dot(low_rank_coefficient, fl...  18 us
  transfers between devices with their start and end apart: 1, of which 1 were waited for; matrix products, arithmetic and copies ran while one was open for 0% of the time, Pallas kernels for 0%

commit v1 on v0

v1 whole, which is shorter than its diff:
```python
import jax
import jax.numpy as jnp
from jax import lax
from jax.sharding import PartitionSpec as P

CHUNKS = 3


def gathered_low_rank(partial_low):
    n_tp, n_page, n_sub = (lax.axis_size(axis) for axis in ("tp", "page", "sub"))
    n_ps = n_page * n_sub
    if n_tp != n_ps:
        return lax.psum(partial_low, ("tp", "page", "sub")).astype(jnp.bfloat16)
    total = None
    for j in range(n_tp):
        pairs = [
            (t * n_ps + a, a * n_ps + (t + j) % n_tp) for t in range(n_tp) for a in range(n_ps)
        ]
        got = lax.ppermute(partial_low, ("tp", "page", "sub"), pairs)
        total = got if total is None else total + got
    return total.astype(jnp.bfloat16)


def on_device(hidden_units, adapter_ids, down_projection_weight, rank_down, rank_up, residual):
    n_tp = lax.axis_size("tp")
    tp = lax.axis_index("tp")
    owned_count = rank_down.shape[0]
    first_owned = lax.axis_index(("page", "sub")) * owned_count
    chosen = (
        (adapter_ids - first_owned)[:, None] == jnp.arange(owned_count, dtype=jnp.int32)[None, :]
    ).astype(jnp.float32)
    projected = jnp.einsum(
        "rf,afk->rak", hidden_units, rank_down, preferred_element_type=jnp.float32
    )
    partial_low = jnp.einsum("rak,ra->rk", projected, chosen)
    low_rank = gathered_low_rank(partial_low)
    held_count, rank_width, columns = rank_up.shape
    first_held = tp * held_count
    flattened = rank_up.reshape(held_count * rank_width, columns)
    rows_dev = residual.shape[0]
    picked = (
        (adapter_ids - first_held)[:, None] == jnp.arange(held_count, dtype=jnp.int32)[None, :]
    ).astype(jnp.bfloat16)
    coefficient = (picked[:, :, None] * low_rank[:, None, :]).reshape(
        n_tp * rows_dev, held_count * rank_width
    )
    width = columns // CHUNKS
    pieces = []
    for c in range(CHUNKS):
        at = slice(c * width, (c + 1) * width)
        base = jnp.dot(
            hidden_units, down_projection_weight[:, at], preferred_element_type=jnp.float32
        )
        term = (
            base + jnp.dot(coefficient, flattened[:, at], preferred_element_type=jnp.float32)
        ).astype(jnp.bfloat16)
        if n_tp > 4:
            summed = lax.psum_scatter(
                term, "tp", scatter_dimension=0, tiled=True
            ).astype(jnp.float32)
        else:
            block = lambda to: lax.dynamic_slice_in_dim(term, to * rows_dev, rows_dev, 0)
            summed = block(tp).astype(jnp.float32)
            for shift in range(1, n_tp):
                got = lax.ppermute(
                    block((tp + shift) % n_tp), "tp", [(i, (i + shift) % n_tp) for i in range(n_tp)]
                )
                summed = summed + got.astype(jnp.float32)
        pieces.append((residual[:, at].astype(jnp.float32) + summed).astype(jnp.bfloat16))
    return jnp.concatenate(pieces, axis=1)


def solution(mesh):
    placed = (
        P("parts", "tp"),
        P("parts"),
        P("tp", ("page", "sub")),
        P(("parts", "page", "sub"), "tp", None),
        P(("parts", "tp"), None, ("page", "sub")),
        P(("parts", "tp"), ("page", "sub")),
    )
    return jax.shard_map(
        on_device,
        mesh=mesh,
        in_specs=placed,
        out_specs=P(("parts", "tp"), ("page", "sub")),
        check_vma=False,
    )
```

time: 121 us -> 54.8 us (0.45)
  blocking collectives: 62.9 us -> 0 us
  starting transfers between devices: 0.01 us -> 22 us
  waiting for transfers between devices: 18 us -> 4.26 us
  between operations: 13.4 us -> 0.2 us
  matrix products: 23.3 us -> 25.2 us
    psum x1 -> x0, blocking collectives: 62.9 us -> none  [on_device(): low_rank = lax.psum(partial_low, ('tp', 'page', 'sub')).astype(jnp.bfloat16)]
    ppermute x0 -> x13, starting transfers between devices: none -> 22 us  [the longest x9 15.7 us: on_device(): lax.ppermute(block((tp + shift) % n_tp), 'tp', [(i, (i + shift) % n_tp) f...]
    reduce_scatter x1 -> x0, waiting for transfers between devices: 18 us -> none  [on_device(): lax.psum_scatter((base_projection_term + jnp.dot(low_rank_coefficient, fl...]
    ppermute x0 -> x13, waiting for transfers between devices: none -> 4.26 us  [the longest x9 4.25 us: on_device(): lax.ppermute(block((tp + shift) % n_tp), 'tp', [(i, (i + shift) % n_tp) f...]
    dot_general x2 -> x6, matrix products: 21.6 us -> 23.5 us  [the longest x3 23 us: on_device(): jnp.dot(hidden_units, down_projection_weight[:, at], preferred_element_ty...]
    convert_element_type x2, other arithmetic: 2.31 us -> 0.82 us  [the longest x1 0.75 us: on_device(): picked = ((adapter_ids - first_held)[:, None] == jnp.arange(held_count, d...]
  transfers between devices with their start and end apart: 1 -> 13, of which waited for: 1 -> 3; matrix products, arithmetic and copies ran while one was open for 0% -> 43% of each run, Pallas kernels for 0% -> 0%
where the time goes in v1:
time: 54.8 us; the launch traced here: 53.8 us
  matrix products  25.2 us (46%)
  starting transfers between devices  22 us (40%)
  waiting for transfers between devices  4.26 us (8%)
  other arithmetic  1.55 us (3%)
  local copies, waits for them, and re-layouts  0.57 us (1%)
    dot_general x3, matrix products, on_device(): jnp.dot(hidden_units, down_projection_weight[:, at], preferred_element_ty...  23 us
    ppermute x9, starting transfers between devices, on_device(): lax.ppermute(block((tp + shift) % n_tp), 'tp', [(i, (i + shift) % n_tp) f...  15.7 us
    ppermute x4, starting transfers between devices, gathered_low_rank(): got = lax.ppermute(partial_low, ('tp', 'page', 'sub'), pairs)  6.33 us
    ppermute x9, waiting for transfers between devices, on_device(): lax.ppermute(block((tp + shift) % n_tp), 'tp', [(i, (i + shift) % n_tp) f...  4.25 us
    dot_general x1, matrix products, on_device(): jnp.einsum('rf,afk->rak', hidden_units, rank_down, preferred_element_type...  1.66 us
  transfers between devices with their start and end apart: 13, of which 3 were waited for; matrix products, arithmetic and copies ran while one was open for 43% of the time, Pallas kernels for 0%

profile of v1, /device:TPU:0, one launch (start us, length us, event | category | flops | bytes accessed | tf_op | source)
XLA Modules:
  0.0 53.8 jit_solution(4343792068594072955)
XLA Ops:
  0.0 0.0 copy-start
  0.0 0.8 %compare_convert_fusion.1 = (bf16[64]{0:T(256)(128)(2,1)S(1)}, f32[64]{0:T(128)S(1)}) fusion(s32[64]{0:T(128)} %param.7, s32[]{:T(128)S(6)} %axis_index.33, s32[]{:T(128)S(6)} %add.108), kind=kLoop, calls=%fused_computation.33 | loop fusion | flops 384 | bytes 648 | tf_op jit(solution)/shard_map/convert_element_type | solution.py:43
  0.8 0.5 copy-done
  1.3 1.7 %convolution_multiply_fusion = f32[64,64]{1,0:T(8,128)S(1)} fusion(bf16[64,8448]{1,0:T(8,128)(2,1)S(1)} %copy-done, bf16[1,8448,64]{1,2,0:T(8,128)(2,1)} %param.9, f32[64]{0:T(128)S(1)} %get-tuple-element.18), kind=kOutput, calls=%fused_computation.12 | convolution fusion | flops 69210112 | bytes 2179328 | tf_op jit(solution)/shard_map/rf,afk->rak/dot_general | solution.py:32
  2.9 2.4 %collective-permute-start.3 = (f32[64,64]{1,0:T(8,128)S(1)}, f32[64,64]{1,0:T(8,128)S(1)}, u32[]{:S(2)}, u32[]{:S(2)}) collective-permute-start(f32[64,64]{1,0:T(8,128)S(1)} %convolution_multiply_fusion), channel_id=1, source_target_pairs={{0,3},{1,7},{2,11},{3,15},{4,0},{5,4},{6,8},{7,12},{8,1},{9,5},{10... | collective-permute-start | bytes 49160 | tf_op jit(solution)/shard_map/ppermute | solution.py:19
  5.4 2.6 %collective-permute-start.2 = (f32[64,64]{1,0:T(8,128)S(1)}, f32[64,64]{1,0:T(8,128)S(1)}, u32[]{:S(2)}, u32[]{:S(2)}) collective-permute-start(f32[64,64]{1,0:T(8,128)S(1)} %convolution_multiply_fusion), channel_id=1, source_target_pairs={{0,2},{1,6},{2,10},{3,14},{4,3},{5,7},{6,11},{7,15},{8,0},{9,4},{1... | collective-permute-start | bytes 49160 | tf_op jit(solution)/shard_map/ppermute | solution.py:19
  7.9 0.6 %collective-permute-start.1 = (f32[64,64]{1,0:T(8,128)S(1)}, f32[64,64]{1,0:T(8,128)S(1)}, u32[]{:S(2)}, u32[]{:S(2)}) collective-permute-start(f32[64,64]{1,0:T(8,128)S(1)} %convolution_multiply_fusion), channel_id=1, source_target_pairs={{0,1},{1,5},{2,9},{3,13},{4,2},{5,6},{6,10},{7,14},{8,3},{9,7},{10... | collective-permute-start | bytes 49160 | tf_op jit(solution)/shard_map/ppermute | solution.py:19
  8.6 0.7 %collective-permute-start = (f32[64,64]{1,0:T(8,128)S(1)}, f32[64,64]{1,0:T(8,128)S(1)}, u32[]{:S(2)}, u32[]{:S(2)}) collective-permute-start(f32[64,64]{1,0:T(8,128)S(1)} %convolution_multiply_fusion), channel_id=1, source_target_pairs={{0,0},{1,4},{2,8},{3,12},{4,1},{5,5},{6,9},{7,13},{8,2},{9,6},{10,... | collective-permute-start | bytes 49160 | tf_op jit(solution)/shard_map/ppermute | solution.py:19
  9.3 7.7 %fusion.4 = f32[64,1024]{1,0:T(8,128)S(1)} fusion(bf16[64,8448]{1,0:T(8,128)(2,1)S(1)} %copy-done, bf16[8448,3072]{1,0:T(8,128)(2,1)} %param.8), kind=kOutput, calls=%fused_computation.4 | convolution fusion | flops 1107296256 | bytes 18644992 | tf_op jit(solution)/shard_map/dot_general | solution.py:51
  17.0 7.7 %fusion = f32[64,1024]{1,0:T(8,128)S(1)} fusion(bf16[64,8448]{1,0:T(8,128)(2,1)S(1)} %copy-done, bf16[8448,3072]{1,0:T(8,128)(2,1)} %param.8), kind=kOutput, calls=%fused_computation | convolution fusion | flops 1107296256 | bytes 18644992 | tf_op jit(solution)/shard_map/dot_general | solution.py:51
  24.7 0.0 copy-start.1
  24.7 7.6 %fusion.2 = f32[64,1024]{1,0:T(8,128)S(1)} fusion(bf16[64,8448]{1,0:T(8,128)(2,1)S(1)} %copy-done, bf16[8448,3072]{1,0:T(8,128)(2,1)} %param.8), kind=kOutput, calls=%fused_computation.2 | convolution fusion | flops 1107296256 | bytes 18644992 | tf_op jit(solution)/shard_map/dot_general | solution.py:51
  32.4 0.0 collective-permute-done.3
  32.4 0.0 collective-permute-done.2
  32.4 0.0 collective-permute-done.1
  32.4 0.0 collective-permute-done
  32.4 0.1 fusion.13
  32.5 0.0 copy-done.1
  32.5 0.0 copy-start.2
  32.5 0.2 fusion.6
  32.7 3.9 %collective-permute-start.4 = (bf16[16,1024]{1,0:T(8,128)(2,1)S(1)}, bf16[16,1024]{1,0:T(8,128)(2,1)S(1)}, u32[]{:S(2)}, u32[]{:S(2)}) collective-permute-start(bf16[16,1024]{1,0:T(8,128)(2,1)S(1)} %get-tuple-element.5), channel_id=1, source_target_pairs={{0,4},{4,8},{8,12},{12,0},{1,5},{5,9},{9,13},{13,1},{2,6},{6,10},{... | collective-permute-start | bytes 98312 | tf_op jit(solution)/shard_map/ppermute | solution.py:65
  36.6 2.3 %collective-permute-start.6 = (bf16[16,1024]{1,0:T(8,128)(2,1)S(1)}, bf16[16,1024]{1,0:T(8,128)(2,1)S(1)}, u32[]{:S(2)}, u32[]{:S(2)}) collective-permute-start(bf16[16,1024]{1,0:T(8,128)(2,1)S(1)} %get-tuple-element.6), channel_id=1, source_target_pairs={{0,12},{4,0},{8,4},{12,8},{1,13},{5,1},{9,5},{13,9},{2,14},{6,2},{... | collective-permute-start | bytes 98312 | tf_op jit(solution)/shard_map/ppermute | solution.py:65
  38.9 0.6 %collective-permute-start.5 = (bf16[16,1024]{1,0:T(8,128)(2,1)S(1)}, bf16[16,1024]{1,0:T(8,128)(2,1)S(1)}, u32[]{:S(2)}, u32[]{:S(2)}) collective-permute-start(bf16[16,1024]{1,0:T(8,128)(2,1)S(1)} %get-tuple-element.7), channel_id=1, source_target_pairs={{0,8},{4,12},{8,0},{12,4},{1,9},{5,13},{9,1},{13,5},{2,10},{6,14},... | collective-permute-start | bytes 98312 | tf_op jit(solution)/shard_map/ppermute | solution.py:65
  39.5 0.2 fusion.8
  39.7 2.0 %collective-permute-start.10 = (bf16[16,1024]{1,0:T(8,128)(2,1)S(1)}, bf16[16,1024]{1,0:T(8,128)(2,1)S(1)}, u32[]{:S(2)}, u32[]{:S(2)}) collective-permute-start(bf16[16,1024]{1,0:T(8,128)(2,1)S(1)} %get-tuple-element.11), channel_id=1, source_target_pairs={{0,4},{4,8},{8,12},{12,0},{1,5},{5,9},{9,13},{13,1},{2,6},{6,10},{... | collective-permute-start | bytes 98312 | tf_op jit(solution)/shard_map/ppermute | solution.py:65
  41.7 1.9 %collective-permute-start.12 = (bf16[16,1024]{1,0:T(8,128)(2,1)S(1)}, bf16[16,1024]{1,0:T(8,128)(2,1)S(1)}, u32[]{:S(2)}, u32[]{:S(2)}) collective-permute-start(bf16[16,1024]{1,0:T(8,128)(2,1)S(1)} %get-tuple-element.12), channel_id=1, source_target_pairs={{0,12},{4,0},{8,4},{12,8},{1,13},{5,1},{9,5},{13,9},{2,14},{6,2},{... | collective-permute-start | bytes 98312 | tf_op jit(solution)/shard_map/ppermute | solution.py:65
  43.6 0.2 fusion.7
  43.8 0.0 collective-permute-done.4
  43.8 0.6 %collective-permute-start.11 = (bf16[16,1024]{1,0:T(8,128)(2,1)S(1)}, bf16[16,1024]{1,0:T(8,128)(2,1)S(1)}, u32[]{:S(2)}, u32[]{:S(2)}) collective-permute-start(bf16[16,1024]{1,0:T(8,128)(2,1)S(1)} %get-tuple-element.13), channel_id=1, source_target_pairs={{0,8},{4,12},{8,0},{12,4},{1,9},{5,13},{9,1},{13,5},{2,10},{6,14},... | collective-permute-start | bytes 98312 | tf_op jit(solution)/shard_map/ppermute | solution.py:65
  44.4 0.0 collective-permute-done.6
  44.4 0.1 collective-permute-start.7
  44.5 0.0 collective-permute-done.5
  44.5 3.8 %collective-permute-start.9 = (bf16[16,1024]{1,0:T(8,128)(2,1)S(1)}, bf16[16,1024]{1,0:T(8,128)(2,1)S(1)}, u32[]{:S(2)}, u32[]{:S(2)}) collective-permute-start(bf16[16,1024]{1,0:T(8,128)(2,1)S(1)} %get-tuple-element.9), channel_id=1, source_target_pairs={{0,12},{4,0},{8,4},{12,8},{1,13},{5,1},{9,5},{13,9},{2,14},{6,2},{... | collective-permute-start | bytes 98312 | tf_op jit(solution)/shard_map/ppermute | solution.py:65
  48.2 0.0 collective-permute-done.10
  48.2 0.6 %collective-permute-start.8 = (bf16[16,1024]{1,0:T(8,128)(2,1)S(1)}, bf16[16,1024]{1,0:T(8,128)(2,1)S(1)}, u32[]{:S(2)}, u32[]{:S(2)}) collective-permute-start(bf16[16,1024]{1,0:T(8,128)(2,1)S(1)} %get-tuple-element.10), channel_id=1, source_target_pairs={{0,8},{4,12},{8,0},{12,4},{1,9},{5,13},{9,1},{13,5},{2,10},{6,14},... | collective-permute-start | bytes 98312 | tf_op jit(solution)/shard_map/ppermute | solution.py:65
  48.8 0.0 collective-permute-done.12
  48.8 0.6 %collective-permute-done.11 = bf16[16,1024]{1,0:T(8,128)(2,1)S(1)} collective-permute-done((bf16[16,1024]{1,0:T(8,128)(2,1)S(1)}, bf16[16,1024]{1,0:T(8,128)(2,1)S(1)}, u32[]{:S(2)}, u32[]{:S(2)}) %collective-permute-start.11) | collective-permute-done | bytes 32800 | tf_op jit(solution)/shard_map/ppermute | solution.py:65
  49.5 0.7 %collective-permute-done.7 = bf16[16,1024]{1,0:T(8,128)(2,1)S(1)} collective-permute-done((bf16[16,1024]{1,0:T(8,128)(2,1)S(1)}, bf16[16,1024]{1,0:T(8,128)(2,1)S(1)}, u32[]{:S(2)}, u32[]{:S(2)}) %collective-permute-start.7) | collective-permute-done | bytes 32800 | tf_op jit(solution)/shard_map/ppermute | solution.py:65
  50.1 0.0 collective-permute-done.9
  50.1 2.9 %collective-permute-done.8 = bf16[16,1024]{1,0:T(8,128)(2,1)S(1)} collective-permute-done((bf16[16,1024]{1,0:T(8,128)(2,1)S(1)}, bf16[16,1024]{1,0:T(8,128)(2,1)S(1)}, u32[]{:S(2)}, u32[]{:S(2)}) %collective-permute-start.8) | collective-permute-done | bytes 32800 | tf_op jit(solution)/shard_map/ppermute | solution.py:65
  53.1 0.0 copy-done.2
  53.1 0.1 add_convert_fusion.2
  53.1 0.6 %pad_maximum_fusion = bf16[16,3072]{1,0:T(8,128)(2,1)} fusion(bf16[16,1024]{1,0:T(8,128)(2,1)S(1)} %get-tuple-element.15, bf16[16,1024]{1,0:T(8,128)(2,1)S(1)} %get-tuple-element.16, bf16[16,1024]{1,0:T(8,128)(2,1)S(1)} %get-tuple-element.14), kind=kLoop, calls=%fused_computation.17 | loop fusion | flops 294912 | bytes 196608 | tf_op jit(solution)/shard_map/concatenate | solution.py:70
  (3 shorter events, 0.1 us)
Async XLA Ops:
  0.0 1.3 %copy-start = (bf16[64,8448]{1,0:T(8,128)(2,1)S(1)}, bf16[64,8448]{1,0:T(8,128)(2,1)}, u32[]{:S(2)}) copy-start(bf16[64,8448]{1,0:T(8,128)(2,1)} %param.6) | copy-start | bytes 3244036
  2.9 29.4 %collective-permute-start.3 = (f32[64,64]{1,0:T(8,128)S(1)}, f32[64,64]{1,0:T(8,128)S(1)}, u32[]{:S(2)}, u32[]{:S(2)}) collective-permute-start(f32[64,64]{1,0:T(8,128)S(1)} %convolution_multiply_fusion), channel_id=1, source_target_pairs={{0,3},{1,7},{2,11},{3,15},{4,0},{5,4},{6,8},{7,12},{8,1},{9,5},{10... | collective-permute-start | bytes 49160 | tf_op jit(solution)/shard_map/ppermute | solution.py:19
  5.4 27.0 %collective-permute-start.2 = (f32[64,64]{1,0:T(8,128)S(1)}, f32[64,64]{1,0:T(8,128)S(1)}, u32[]{:S(2)}, u32[]{:S(2)}) collective-permute-start(f32[64,64]{1,0:T(8,128)S(1)} %convolution_multiply_fusion), channel_id=1, source_target_pairs={{0,2},{1,6},{2,10},{3,14},{4,3},{5,7},{6,11},{7,15},{8,0},{9,4},{1... | collective-permute-start | bytes 49160 | tf_op jit(solution)/shard_map/ppermute | solution.py:19
  7.9 24.4 %collective-permute-start.1 = (f32[64,64]{1,0:T(8,128)S(1)}, f32[64,64]{1,0:T(8,128)S(1)}, u32[]{:S(2)}, u32[]{:S(2)}) collective-permute-start(f32[64,64]{1,0:T(8,128)S(1)} %convolution_multiply_fusion), channel_id=1, source_target_pairs={{0,1},{1,5},{2,9},{3,13},{4,2},{5,6},{6,10},{7,14},{8,3},{9,7},{10... | collective-permute-start | bytes 49160 | tf_op jit(solution)/shard_map/ppermute | solution.py:19
  8.6 23.8 %collective-permute-start = (f32[64,64]{1,0:T(8,128)S(1)}, f32[64,64]{1,0:T(8,128)S(1)}, u32[]{:S(2)}, u32[]{:S(2)}) collective-permute-start(f32[64,64]{1,0:T(8,128)S(1)} %convolution_multiply_fusion), channel_id=1, source_target_pairs={{0,0},{1,4},{2,8},{3,12},{4,1},{5,5},{6,9},{7,13},{8,2},{9,6},{10,... | collective-permute-start | bytes 49160 | tf_op jit(solution)/shard_map/ppermute | solution.py:19
  24.7 7.8 %copy-start.1 = (bf16[1,64,3072]{2,1,0:T(8,128)(2,1)S(1)}, bf16[1,64,3072]{2,1,0:T(8,128)(2,1)}, u32[]{:S(2)}) copy-start(bf16[1,64,3072]{2,1,0:T(8,128)(2,1)} %param.10) | copy-start | bytes 1179652
  32.5 20.6 %copy-start.2 = (bf16[16,3072]{1,0:T(8,128)(2,1)S(1)}, bf16[16,3072]{1,0:T(8,128)(2,1)}, u32[]{:S(2)}) copy-start(bf16[16,3072]{1,0:T(8,128)(2,1)} %param.11) | copy-start | bytes 294916
  32.7 11.1 %collective-permute-start.4 = (bf16[16,1024]{1,0:T(8,128)(2,1)S(1)}, bf16[16,1024]{1,0:T(8,128)(2,1)S(1)}, u32[]{:S(2)}, u32[]{:S(2)}) collective-permute-start(bf16[16,1024]{1,0:T(8,128)(2,1)S(1)} %get-tuple-element.5), channel_id=1, source_target_pairs={{0,4},{4,8},{8,12},{12,0},{1,5},{5,9},{9,13},{13,1},{2,6},{6,10},{... | collective-permute-start | bytes 98312 | tf_op jit(solution)/shard_map/ppermute | solution.py:65
  36.6 7.8 %collective-permute-start.6 = (bf16[16,1024]{1,0:T(8,128)(2,1)S(1)}, bf16[16,1024]{1,0:T(8,128)(2,1)S(1)}, u32[]{:S(2)}, u32[]{:S(2)}) collective-permute-start(bf16[16,1024]{1,0:T(8,128)(2,1)S(1)} %get-tuple-element.6), channel_id=1, source_target_pairs={{0,12},{4,0},{8,4},{12,8},{1,13},{5,1},{9,5},{13,9},{2,14},{6,2},{... | collective-permute-start | bytes 98312 | tf_op jit(solution)/shard_map/ppermute | solution.py:65
  38.9 5.6 %collective-permute-start.5 = (bf16[16,1024]{1,0:T(8,128)(2,1)S(1)}, bf16[16,1024]{1,0:T(8,128)(2,1)S(1)}, u32[]{:S(2)}, u32[]{:S(2)}) collective-permute-start(bf16[16,1024]{1,0:T(8,128)(2,1)S(1)} %get-tuple-element.7), channel_id=1, source_target_pairs={{0,8},{4,12},{8,0},{12,4},{1,9},{5,13},{9,1},{13,5},{2,10},{6,14},... | collective-permute-start | bytes 98312 | tf_op jit(solution)/shard_map/ppermute | solution.py:65
  39.7 8.5 %collective-permute-start.10 = (bf16[16,1024]{1,0:T(8,128)(2,1)S(1)}, bf16[16,1024]{1,0:T(8,128)(2,1)S(1)}, u32[]{:S(2)}, u32[]{:S(2)}) collective-permute-start(bf16[16,1024]{1,0:T(8,128)(2,1)S(1)} %get-tuple-element.11), channel_id=1, source_target_pairs={{0,4},{4,8},{8,12},{12,0},{1,5},{5,9},{9,13},{13,1},{2,6},{6,10},{... | collective-permute-start | bytes 98312 | tf_op jit(solution)/shard_map/ppermute | solution.py:65
  41.7 7.1 %collective-permute-start.12 = (bf16[16,1024]{1,0:T(8,128)(2,1)S(1)}, bf16[16,1024]{1,0:T(8,128)(2,1)S(1)}, u32[]{:S(2)}, u32[]{:S(2)}) collective-permute-start(bf16[16,1024]{1,0:T(8,128)(2,1)S(1)} %get-tuple-element.12), channel_id=1, source_target_pairs={{0,12},{4,0},{8,4},{12,8},{1,13},{5,1},{9,5},{13,9},{2,14},{6,2},{... | collective-permute-start | bytes 98312 | tf_op jit(solution)/shard_map/ppermute | solution.py:65
  43.8 5.7 %collective-permute-start.11 = (bf16[16,1024]{1,0:T(8,128)(2,1)S(1)}, bf16[16,1024]{1,0:T(8,128)(2,1)S(1)}, u32[]{:S(2)}, u32[]{:S(2)}) collective-permute-start(bf16[16,1024]{1,0:T(8,128)(2,1)S(1)} %get-tuple-element.13), channel_id=1, source_target_pairs={{0,8},{4,12},{8,0},{12,4},{1,9},{5,13},{9,1},{13,5},{2,10},{6,14},... | collective-permute-start | bytes 98312 | tf_op jit(solution)/shard_map/ppermute | solution.py:65
  44.4 5.7 %collective-permute-start.7 = (bf16[16,1024]{1,0:T(8,128)(2,1)S(1)}, bf16[16,1024]{1,0:T(8,128)(2,1)S(1)}, u32[]{:S(2)}, u32[]{:S(2)}) collective-permute-start(bf16[16,1024]{1,0:T(8,128)(2,1)S(1)} %get-tuple-element.8), channel_id=1, source_target_pairs={{0,4},{4,8},{8,12},{12,0},{1,5},{5,9},{9,13},{13,1},{2,6},{6,10},{... | collective-permute-start | bytes 98312 | tf_op jit(solution)/shard_map/ppermute | solution.py:65
  44.5 5.7 %collective-permute-start.9 = (bf16[16,1024]{1,0:T(8,128)(2,1)S(1)}, bf16[16,1024]{1,0:T(8,128)(2,1)S(1)}, u32[]{:S(2)}, u32[]{:S(2)}) collective-permute-start(bf16[16,1024]{1,0:T(8,128)(2,1)S(1)} %get-tuple-element.9), channel_id=1, source_target_pairs={{0,12},{4,0},{8,4},{12,8},{1,13},{5,1},{9,5},{13,9},{2,14},{6,2},{... | collective-permute-start | bytes 98312 | tf_op jit(solution)/shard_map/ppermute | solution.py:65
  48.2 4.8 %collective-permute-start.8 = (bf16[16,1024]{1,0:T(8,128)(2,1)S(1)}, bf16[16,1024]{1,0:T(8,128)(2,1)S(1)}, u32[]{:S(2)}, u32[]{:S(2)}) collective-permute-start(bf16[16,1024]{1,0:T(8,128)(2,1)S(1)} %get-tuple-element.10), channel_id=1, source_target_pairs={{0,8},{4,12},{8,0},{12,4},{1,9},{5,13},{9,1},{13,5},{2,10},{6,14},... | collective-permute-start | bytes 98312 | tf_op jit(solution)/shard_map/ppermute | solution.py:65

commit v2 on v1

v2 whole, which is shorter than its diff:
```python
import functools

import jax
import jax.numpy as jnp
from jax import lax
from jax.experimental import pallas as pl
from jax.experimental.pallas import tpu as pltpu
from jax.sharding import PartitionSpec as P

CHUNKS = (1024, 1024, 1024)
PS = ("page", "sub")


def low_kernel(hidden, rank_down, chosen, out):
    total = jnp.zeros(out.shape, jnp.float32)
    for a in range(rank_down.shape[0]):
        product = lax.dot_general(
            hidden[...], rank_down[a], (((1,), (1,)), ((), ())), preferred_element_type=jnp.float32
        )
        total = total + product * chosen[:, a : a + 1]
    out[...] = total


def partial_low_rank(hidden_units, rank_down, chosen):
    rows = hidden_units.shape[0]
    rank = rank_down.shape[2]
    return pl.pallas_call(
        low_kernel,
        out_shape=jax.ShapeDtypeStruct((rows, rank), jnp.float32),
        in_specs=[pl.BlockSpec(memory_space=pltpu.VMEM)] * 3,
        out_specs=pl.BlockSpec(memory_space=pltpu.VMEM),
        compiler_params=pltpu.CompilerParams(vmem_limit_bytes=16 << 20),
        name="low_rank",
    )(hidden_units, jnp.swapaxes(rank_down, 1, 2), chosen)


def dot_kernel(start, depth, hidden, weight, out, held, arrived):
    width = out.shape[1]
    steps = weight.shape[0] // depth

    def copy(k):
        rows = pl.ds(pl.multiple_of(k * depth, depth), depth)
        return pltpu.make_async_copy(
            weight.at[rows, pl.ds(start, width)], held.at[rows], arrived.at[k]
        )

    @pl.loop(0, steps)
    def _(k):
        copy(k).start()

    out[...] = jnp.zeros_like(out)

    @pl.loop(0, steps)
    def _(k):
        copy(k).wait()
        at = pl.ds(pl.multiple_of(k * depth, depth), depth)
        out[...] += jnp.dot(hidden[:, at], held[at], preferred_element_type=jnp.float32)


def base_term(hidden_units, weight, start, width):
    rows, total_depth = hidden_units.shape
    depth = 768 if total_depth % 768 == 0 else 128 if total_depth % 128 == 0 else total_depth
    return pl.pallas_call(
        functools.partial(dot_kernel, start, depth),
        out_shape=jax.ShapeDtypeStruct((rows, width), jnp.float32),
        in_specs=[pl.BlockSpec(memory_space=pltpu.VMEM), pl.BlockSpec(memory_space=pl.ANY)],
        out_specs=pl.BlockSpec(memory_space=pltpu.VMEM),
        scratch_shapes=[
            pltpu.VMEM((total_depth, width), weight.dtype),
            pltpu.SemaphoreType.DMA((total_depth // depth,)),
        ],
        compiler_params=pltpu.CompilerParams(vmem_limit_bytes=40 << 20),
        cost_estimate=pl.CostEstimate(
            flops=2 * rows * total_depth * width,
            bytes_accessed=2 * total_depth * width,
            transcendentals=0,
        ),
        name="base_dot",
    )(hidden_units, weight)


def gathered_low_rank(partial_low):
    n_tp, n_page, n_sub = (lax.axis_size(axis) for axis in ("tp",) + PS)
    n_ps = n_page * n_sub
    if n_tp != n_ps:
        return lax.psum(partial_low, ("tp",) + PS).astype(jnp.bfloat16)
    pairs = [(t * n_ps + a, a * n_ps + t) for t in range(n_tp) for a in range(n_ps)]
    got = lax.ppermute(partial_low, ("tp",) + PS, pairs)
    spread = lax.all_to_all(
        jnp.broadcast_to(got[None], (n_ps,) + got.shape), PS, split_axis=0, concat_axis=0
    )
    return jnp.sum(spread, axis=0).astype(jnp.bfloat16)


def on_device(hidden_units, adapter_ids, down_projection_weight, rank_down, rank_up, residual):
    n_tp = lax.axis_size("tp")
    owned_count = rank_down.shape[0]
    first_owned = lax.axis_index(PS) * owned_count
    chosen = (
        (adapter_ids - first_owned)[:, None] == jnp.arange(owned_count, dtype=jnp.int32)[None, :]
    ).astype(jnp.float32)
    low_rank = gathered_low_rank(partial_low_rank(hidden_units, rank_down, chosen))
    held_count, rank_width, columns = rank_up.shape
    first_held = lax.axis_index("tp") * held_count
    flattened = rank_up.reshape(held_count * rank_width, columns)
    rows_dev = residual.shape[0]
    picked = (
        (adapter_ids - first_held)[:, None] == jnp.arange(held_count, dtype=jnp.int32)[None, :]
    ).astype(jnp.bfloat16)
    coefficient = (picked[:, :, None] * low_rank[:, None, :]).reshape(
        n_tp * rows_dev, held_count * rank_width
    )
    pieces = []
    start = 0
    widths = CHUNKS if sum(CHUNKS) == columns else (columns,)
    for width in widths:
        at = slice(start, start + width)
        base = base_term(hidden_units, down_projection_weight, start, width)
        term = (
            base + jnp.dot(coefficient, flattened[:, at], preferred_element_type=jnp.float32)
        ).astype(jnp.bfloat16)
        if n_tp > 4:
            summed = lax.psum_scatter(term, "tp", scatter_dimension=0, tiled=True).astype(
                jnp.float32
            )
        else:
            got = lax.all_to_all(
                term.reshape(n_tp, rows_dev, width), "tp", split_axis=0, concat_axis=0
            )
            summed = jnp.sum(got.astype(jnp.float32), axis=0)
        pieces.append((residual[:, at].astype(jnp.float32) + summed).astype(jnp.bfloat16))
        start += width
    return jnp.concatenate(pieces, axis=1)


def solution(mesh):
    placed = (
        P("parts", "tp"),
        P("parts"),
        P("tp", ("page", "sub")),
        P(("parts", "page", "sub"), "tp", None),
        P(("parts", "tp"), None, ("page", "sub")),
        P(("parts", "tp"), ("page", "sub")),
    )
    return jax.shard_map(
        on_device,
        mesh=mesh,
        in_specs=placed,
        out_specs=P(("parts", "tp"), ("page", "sub")),
        check_vma=False,
    )
```

time: 54.8 us -> 65.7 us (1.20)
  matrix products: 25.2 us -> 2.62 us
  Pallas kernels: 0 us -> 20.2 us
  waiting for transfers between devices: 4.26 us -> 16.6 us
  local copies, waits for them, and re-layouts: 0.57 us -> 4.12 us
  starting transfers between devices: 22 us -> 19.3 us
  other arithmetic: 1.55 us -> 2.22 us
    dot_general x4 -> x0, matrix products: 24.7 us -> none  [the longest x3 23 us: on_device(): jnp.dot(hidden_units, down_projection_weight[:, at], preferred_element_ty...]
    ppermute x13 -> x1, starting transfers between devices: 22 us -> 0.66 us  [gathered_low_rank(): got = lax.ppermute(partial_low, ('tp',) + PS, pairs)]
    pallas_call x0 -> x4, Pallas kernels: none -> 20.2 us  [the longest x3 19.8 us: base_term(): pl.pallas_call(functools.partial(dot_kernel, start, depth), out_shape=jax...]
    all_to_all x0 -> x4, starting transfers between devices: none -> 18.6 us  [the longest x3 9.97 us: on_device(): lax.all_to_all(term.reshape(n_tp, rows_dev, width), 'tp', split_axis=0, c...]
    all_to_all x0 -> x4, waiting for transfers between devices: none -> 16.6 us  [the longest x3 16.6 us: on_device(): lax.all_to_all(term.reshape(n_tp, rows_dev, width), 'tp', split_axis=0, c...]
    ppermute x13 -> x1, waiting for transfers between devices: 4.26 us -> 0.01 us  [gathered_low_rank(): got = lax.ppermute(partial_low, ('tp',) + PS, pairs)]
    unnamed x6 -> x12, local copies, waits for them, and re-layouts: 0.51 us -> 3.5 us
    dot_general x3, matrix products: 0.5 us -> 2.62 us  [on_device(): jnp.dot(coefficient, flattened[:, at], preferred_element_type=jnp.float32)]
  transfers between devices with their start and end apart: 13 -> 5, of which waited for: 3 -> 3; matrix products, arithmetic and copies ran while one was open for 43% -> 3% of each run, Pallas kernels for 0% -> 30%
where the time goes in v2:
time: 65.7 us; the launch traced here: 65.1 us
  Pallas kernels  20.2 us (31%)
  starting transfers between devices  19.3 us (29%)
  waiting for transfers between devices  16.6 us (25%)
  local copies, waits for them, and re-layouts  4.12 us (6%)
  matrix products  2.62 us (4%)
  other arithmetic  2.22 us (3%)
    pallas_call x3, Pallas kernels, base_term(): pl.pallas_call(functools.partial(dot_kernel, start, depth), out_shape=jax...  19.8 us
    all_to_all x3, waiting for transfers between devices, on_device(): lax.all_to_all(term.reshape(n_tp, rows_dev, width), 'tp', split_axis=0, c...  16.6 us
    all_to_all x3, starting transfers between devices, on_device(): lax.all_to_all(term.reshape(n_tp, rows_dev, width), 'tp', split_axis=0, c...  9.97 us
    all_to_all x1, starting transfers between devices, gathered_low_rank(): lax.all_to_all(jnp.broadcast_to(got[None], (n_ps,) + got.shape), PS, spli...  8.62 us
    unnamed x12, local copies, waits for them, and re-layouts  3.5 us
    dot_general x3, matrix products, on_device(): jnp.dot(coefficient, flattened[:, at], preferred_element_type=jnp.float32)  2.62 us
  transfers between devices with their start and end apart: 5, of which 3 were waited for; matrix products, arithmetic and copies ran while one was open for 3% of the time, Pallas kernels for 30%

profile of v2, /device:TPU:0, one launch (start us, length us, event | category | flops | bytes accessed | tf_op | source)
XLA Modules:
  0.0 65.1 jit_solution(13570870012014026994)
XLA Ops:
  0.0 0.7 %compare_convert_fusion.1 = (bf16[64]{0:T(256)(128)(2,1)S(1)}, f32[64,1]{0,1:T(1,128)S(1)}) fusion(s32[64]{0:T(128)} %param.7, s32[]{:T(128)S(6)} %axis_index.33, s32[]{:T(128)S(6)} %add.21), kind=kLoop, calls=%fused_computation.18 | loop fusion | flops 384 | bytes 648 | tf_op jit(solution)/shard_map/convert_element_type | solution.py:109
  0.7 0.1 copy.8.chosen
  0.8 0.0 copy-start
  0.8 1.2 %copy-done = bf16[64,8448]{1,0:T(8,128)(2,1)S(1)} copy-done((bf16[64,8448]{1,0:T(8,128)(2,1)S(1)}, bf16[64,8448]{1,0:T(8,128)(2,1)}, u32[]{:S(2)}) %copy-start) | copy-done | bytes 1081368
  2.0 0.0 copy-start.2
  2.0 1.2 %copy-done.2 = bf16[1,8448,64]{1,2,0:T(8,128)(2,1)S(1)} copy-done((bf16[1,8448,64]{1,2,0:T(8,128)(2,1)S(1)}, bf16[1,8448,64]{1,2,0:T(8,128)(2,1)}, u32[]{:S(2)}) %copy-start.2) | copy-done | bytes 1081368
  3.2 0.0 copy-start.1
  3.2 0.4 low_rank.1
  3.7 0.7 %collective-permute-start = (f32[64,64]{1,0:T(8,128)S(1)}, f32[64,64]{1,0:T(8,128)S(1)}, u32[]{:S(2)}, u32[]{:S(2)}) collective-permute-start(f32[64,64]{1,0:T(8,128)S(1)} %low_rank.1), channel_id=1, source_target_pairs={{0,0},{1,4},{2,8},{3,12},{4,1},{5,5},{6,9},{7,13},{8,2},{9,6},{10,... | collective-permute-start | bytes 49160 | tf_op jit(solution)/shard_map/ppermute | solution.py:88
  4.3 0.1 copy-done.1
  4.5 6.6 %base_dot.3 = f32[64,1024]{1,0:T(8,128)S(1)} custom-call(bf16[64,8448]{1,0:T(8,128)(2,1)S(1)} %copy-done.1, bf16[8448,3072]{1,0:T(8,128)(2,1)} %weight.5), custom_call_target="tpu_custom_call" | custom-call | flops 1107296256 | bytes 17301504 | tf_op jit(solution)/shard_map/base_dot/pallas_call | solution.py:63
  11.1 6.6 %base_dot.5 = f32[64,1024]{1,0:T(8,128)S(1)} custom-call(bf16[64,8448]{1,0:T(8,128)(2,1)S(1)} %copy-done.1, bf16[8448,3072]{1,0:T(8,128)(2,1)} %weight.5), custom_call_target="tpu_custom_call" | custom-call | flops 1107296256 | bytes 17301504 | tf_op jit(solution)/shard_map/base_dot/pallas_call | solution.py:63
  17.7 0.0 collective-permute-done
  17.7 0.8 %reshape.36 = f32[4,1,4096]{2,1,0:T(1,128)} reshape(f32[4,64,64]{2,1,0:T(8,128)S(1)} %broadcast_in_dim.2) | data formatting | bytes 131072
  18.5 8.6 %all-to-all-start = ((f32[4,1,4096]{2,1,0:T(1,128)}), f32[4,1,4096]{2,1,0:T(1,128)S(1)}, u32[]{:S(2)}, u32[]{:S(2)}) async-start(f32[4,1,4096]{2,1,0:T(1,128)} %reshape.36), calls=%async_computation | async-start | bytes 131072 | tf_op jit(solution)/shard_map/all_to_all | solution.py:89
  27.1 0.0 copy-start.3
  27.1 6.6 %base_dot.4 = f32[64,1024]{1,0:T(8,128)S(1)} custom-call(bf16[64,8448]{1,0:T(8,128)(2,1)S(1)} %copy-done.1, bf16[8448,3072]{1,0:T(8,128)(2,1)} %weight.5), custom_call_target="tpu_custom_call" | custom-call | flops 1107296256 | bytes 17301504 | tf_op jit(solution)/shard_map/base_dot/pallas_call | solution.py:63
  33.7 0.0 all-to-all-done
  33.7 0.5 broadcast.14
  34.2 0.8 %reduce = f32[4,4096]{1,0:T(4,128)S(1)} reduce(f32[4,1,4096]{2,1,0:T(1,128)S(1)} %all-to-all-done, f32[]{:T(128)} %broadcast.14), dimensions={1}, to_apply=%all_to_all.12.reduce_sub_computation | reduce | bytes 131076 | tf_op jit(solution)/shard_map/all_to_all | solution.py:89
  35.0 0.1 reshape.37
  35.1 0.0 copy-done.3
  35.2 0.9 %fusion = bf16[64,1024]{1,0:T(8,128)(2,1)} fusion(f32[64,1024]{1,0:T(8,128)S(1)} %base_dot.3, bf16[64,3072]{1,0:T(8,128)(2,1)S(1)} %bitcast.8, bf16[64,64]{1,0:T(8,128)(2,1)S(1)} %reduce_sum.36, bf16[64]{0:T(256)(128)(2,1)S(1)} %get-tuple-element.8), kind=kOutput, calls=%fused_computation.3 | convolution fusion | flops 8523776 | bytes 541184 | tf_op jit(solution)/shard_map/dot_general | solution.py:120
  36.0 3.3 %all-to-all-start.1 = ((bf16[4,16,1024]{2,1,0:T(8,128)(2,1)}), bf16[4,16,1024]{2,1,0:T(8,128)(2,1)S(1)}, u32[]{:S(2)}, u32[]{:S(2)}) async-start(bf16[4,16,1024]{2,1,0:T(8,128)(2,1)} %bitcast.3), calls=%async_computation.1 | async-start | bytes 262144 | tf_op jit(solution)/shard_map/all_to_all | solution.py:127
  39.4 0.0 copy-start.4
  39.4 0.9 %fusion.2 = bf16[64,1024]{1,0:T(8,128)(2,1)} fusion(f32[64,1024]{1,0:T(8,128)S(1)} %base_dot.5, bf16[64,3072]{1,0:T(8,128)(2,1)S(1)} %bitcast.9, bf16[64,64]{1,0:T(8,128)(2,1)S(1)} %reduce_sum.36, bf16[64]{0:T(256)(128)(2,1)S(1)} %get-tuple-element.8), kind=kOutput, calls=%fused_computation.5 | convolution fusion | flops 8523776 | bytes 541184 | tf_op jit(solution)/shard_map/dot_general | solution.py:120
  40.2 5.6 %all-to-all-done.1 = bf16[4,16,1024]{2,1,0:T(8,128)(2,1)S(1)} async-done(((bf16[4,16,1024]{2,1,0:T(8,128)(2,1)}), bf16[4,16,1024]{2,1,0:T(8,128)(2,1)S(1)}, u32[]{:S(2)}, u32[]{:S(2)}) %all-to-all-start.1) | async-done | bytes 131104 | tf_op jit(solution)/shard_map/all_to_all | solution.py:127
  45.8 3.3 %all-to-all-start.3 = ((bf16[4,16,1024]{2,1,0:T(8,128)(2,1)}), bf16[4,16,1024]{2,1,0:T(8,128)(2,1)S(1)}, u32[]{:S(2)}, u32[]{:S(2)}) async-start(bf16[4,16,1024]{2,1,0:T(8,128)(2,1)} %bitcast.5), calls=%async_computation.3 | async-start | bytes 262144 | tf_op jit(solution)/shard_map/all_to_all | solution.py:127
  49.1 0.9 %fusion.1 = bf16[64,1024]{1,0:T(8,128)(2,1)} fusion(f32[64,1024]{1,0:T(8,128)S(1)} %base_dot.4, bf16[64,3072]{1,0:T(8,128)(2,1)S(1)} %bitcast.10, bf16[64,64]{1,0:T(8,128)(2,1)S(1)} %reduce_sum.36, bf16[64]{0:T(256)(128)(2,1)S(1)} %get-tuple-element.8), kind=kOutput, calls=%fused_computation.4 | convolution fusion | flops 8523776 | bytes 541184 | tf_op jit(solution)/shard_map/dot_general | solution.py:120
  50.0 5.2 %all-to-all-done.3 = bf16[4,16,1024]{2,1,0:T(8,128)(2,1)S(1)} async-done(((bf16[4,16,1024]{2,1,0:T(8,128)(2,1)}), bf16[4,16,1024]{2,1,0:T(8,128)(2,1)S(1)}, u32[]{:S(2)}, u32[]{:S(2)}) %all-to-all-start.3) | async-done | bytes 131104 | tf_op jit(solution)/shard_map/all_to_all | solution.py:127
  55.2 3.3 %all-to-all-start.2 = ((bf16[4,16,1024]{2,1,0:T(8,128)(2,1)}), bf16[4,16,1024]{2,1,0:T(8,128)(2,1)S(1)}, u32[]{:S(2)}, u32[]{:S(2)}) async-start(bf16[4,16,1024]{2,1,0:T(8,128)(2,1)} %bitcast.4), calls=%async_computation.2 | async-start | bytes 262144 | tf_op jit(solution)/shard_map/all_to_all | solution.py:127
  58.6 5.8 %all-to-all-done.2 = bf16[4,16,1024]{2,1,0:T(8,128)(2,1)S(1)} async-done(((bf16[4,16,1024]{2,1,0:T(8,128)(2,1)}), bf16[4,16,1024]{2,1,0:T(8,128)(2,1)S(1)}, u32[]{:S(2)}, u32[]{:S(2)}) %all-to-all-start.2) | async-done | bytes 131104 | tf_op jit(solution)/shard_map/all_to_all | solution.py:127
  64.4 0.0 copy-done.4
  64.5 0.6 pad_maximum_fusion
  (6 shorter events, 0.1 us)
Async XLA Ops:
  0.8 1.2 %copy-start = (bf16[64,8448]{1,0:T(8,128)(2,1)S(1)}, bf16[64,8448]{1,0:T(8,128)(2,1)}, u32[]{:S(2)}) copy-start(bf16[64,8448]{1,0:T(8,128)(2,1)} %hidden.7) | copy-start | bytes 3244036
  2.0 1.2 %copy-start.2 = (bf16[1,8448,64]{1,2,0:T(8,128)(2,1)S(1)}, bf16[1,8448,64]{1,2,0:T(8,128)(2,1)}, u32[]{:S(2)}) copy-start(bf16[1,8448,64]{1,2,0:T(8,128)(2,1)} %param.9) | copy-start | bytes 3244036
  3.2 1.2 %copy-start.1 = (bf16[64,8448]{1,0:T(8,128)(2,1)S(1)}, bf16[64,8448]{1,0:T(8,128)(2,1)}, u32[]{:S(2)}) copy-start(bf16[64,8448]{1,0:T(8,128)(2,1)} %hidden.7) | copy-start | bytes 3244036
  3.7 14.0 %collective-permute-start = (f32[64,64]{1,0:T(8,128)S(1)}, f32[64,64]{1,0:T(8,128)S(1)}, u32[]{:S(2)}, u32[]{:S(2)}) collective-permute-start(f32[64,64]{1,0:T(8,128)S(1)} %low_rank.1), channel_id=1, source_target_pairs={{0,0},{1,4},{2,8},{3,12},{4,1},{5,5},{6,9},{7,13},{8,2},{9,6},{10,... | collective-permute-start | bytes 49160 | tf_op jit(solution)/shard_map/ppermute | solution.py:88
  18.5 15.2 %all-to-all-start = ((f32[4,1,4096]{2,1,0:T(1,128)}), f32[4,1,4096]{2,1,0:T(1,128)S(1)}, u32[]{:S(2)}, u32[]{:S(2)}) async-start(f32[4,1,4096]{2,1,0:T(1,128)} %reshape.36), calls=%async_computation | async-start | bytes 131072 | tf_op jit(solution)/shard_map/all_to_all | solution.py:89
  27.1 8.1 %copy-start.3 = (bf16[1,64,3072]{2,1,0:T(8,128)(2,1)S(1)}, bf16[1,64,3072]{2,1,0:T(8,128)(2,1)}, u32[]{:S(2)}) copy-start(bf16[1,64,3072]{2,1,0:T(8,128)(2,1)} %param.10) | copy-start | bytes 1179652
  36.0 9.8 %all-to-all-start.1 = ((bf16[4,16,1024]{2,1,0:T(8,128)(2,1)}), bf16[4,16,1024]{2,1,0:T(8,128)(2,1)S(1)}, u32[]{:S(2)}, u32[]{:S(2)}) async-start(bf16[4,16,1024]{2,1,0:T(8,128)(2,1)} %bitcast.3), calls=%async_computation.1 | async-start | bytes 262144 | tf_op jit(solution)/shard_map/all_to_all | solution.py:127
  39.4 25.1 %copy-start.4 = (bf16[16,3072]{1,0:T(8,128)(2,1)S(1)}, bf16[16,3072]{1,0:T(8,128)(2,1)}, u32[]{:S(2)}) copy-start(bf16[16,3072]{1,0:T(8,128)(2,1)} %param.11) | copy-start | bytes 294916
  45.8 9.4 %all-to-all-start.3 = ((bf16[4,16,1024]{2,1,0:T(8,128)(2,1)}), bf16[4,16,1024]{2,1,0:T(8,128)(2,1)S(1)}, u32[]{:S(2)}, u32[]{:S(2)}) async-start(bf16[4,16,1024]{2,1,0:T(8,128)(2,1)} %bitcast.5), calls=%async_computation.3 | async-start | bytes 262144 | tf_op jit(solution)/shard_map/all_to_all | solution.py:127
  55.2 9.2 %all-to-all-start.2 = ((bf16[4,16,1024]{2,1,0:T(8,128)(2,1)}), bf16[4,16,1024]{2,1,0:T(8,128)(2,1)S(1)}, u32[]{:S(2)}, u32[]{:S(2)}) async-start(bf16[4,16,1024]{2,1,0:T(8,128)(2,1)} %bitcast.4), calls=%async_computation.2 | async-start | bytes 262144 | tf_op jit(solution)/shard_map/all_to_all | solution.py:127

commit v3 on v0

v3 whole, which is shorter than its diff:
```python
import functools

import jax
import jax.numpy as jnp
from jax import lax
from jax.experimental import pallas as pl
from jax.experimental.pallas import tpu as pltpu
from jax.sharding import PartitionSpec as P

WIDTHS = (1024, 1280, 768)
DEPTH = 768
PS = ("page", "sub")
VMEM = pl.BlockSpec(memory_space=pltpu.VMEM)
HBM = pl.BlockSpec(memory_space=pltpu.HBM)


def column_of(ids_row):
    rows = ids_row.shape[1]
    down = lax.broadcasted_iota(jnp.int32, (rows, rows), 0)
    across = lax.broadcasted_iota(jnp.int32, (rows, rows), 1)
    spread = jnp.broadcast_to(ids_row, (rows, rows))
    return jnp.sum(
        jnp.where(down == across, spread.astype(jnp.float32), 0.0), axis=1, keepdims=True
    )


def deep(k):
    return pl.ds(pl.multiple_of(k * DEPTH, DEPTH), DEPTH)


def weight_copies(weight, held, arrived, start, width):
    def copy(k):
        return pltpu.make_async_copy(
            weight.at[deep(k), pl.ds(start, width)], held.at[deep(k)], arrived.at[k]
        )

    return copy


def first_kernel(
    start,
    width,
    hidden,
    rank_down,
    weight,
    low,
    base,
    hidden_here,
    down_here,
    held,
    got,
    arrived,
):
    steps = weight.shape[0] // DEPTH
    copy = weight_copies(weight, held, arrived, start, width)

    def hidden_copy(k):
        return pltpu.make_async_copy(
            hidden.at[:, deep(k)], hidden_here.at[:, deep(k)], got.at[0, k]
        )

    def down_copy(k):
        return pltpu.make_async_copy(
            rank_down.at[:, deep(k)], down_here.at[:, deep(k)], got.at[1, k]
        )

    @pl.loop(0, steps)
    def _(k):
        hidden_copy(k).start()
        down_copy(k).start()

    @pl.loop(0, steps)
    def _(k):
        copy(k).start()

    low[...] = jnp.zeros_like(low)
    base[...] = jnp.zeros_like(base)

    @pl.loop(0, steps)
    def _(k):
        hidden_copy(k).wait()
        down_copy(k).wait()
        low[...] += lax.dot_general(
            hidden_here[:, deep(k)],
            down_here[:, deep(k)],
            (((1,), (1,)), ((), ())),
            preferred_element_type=jnp.float32,
        )

    @pl.loop(0, steps)
    def _(k):
        copy(k).wait()
        base[...] += jnp.dot(
            hidden_here[:, deep(k)], held[deep(k)], preferred_element_type=jnp.float32
        )


def first_phase(hidden, rank_down, weight, start, width):
    rows, depth = hidden.shape
    rank = rank_down.shape[0]
    steps = depth // DEPTH
    return pl.pallas_call(
        functools.partial(first_kernel, start, width),
        out_shape=(
            jax.ShapeDtypeStruct((rows, rank), jnp.float32),
            jax.ShapeDtypeStruct((rows, width), jnp.float32),
            jax.ShapeDtypeStruct(hidden.shape, hidden.dtype),
        ),
        in_specs=[HBM] * 3,
        out_specs=(VMEM, VMEM, VMEM),
        scratch_shapes=[
            pltpu.VMEM(rank_down.shape, rank_down.dtype),
            pltpu.VMEM((depth, width), weight.dtype),
            pltpu.SemaphoreType.DMA((2, steps)),
            pltpu.SemaphoreType.DMA((steps,)),
        ],
        compiler_params=pltpu.CompilerParams(vmem_limit_bytes=52 << 20),
        cost_estimate=pl.CostEstimate(
            flops=2 * rows * depth * (width + rank),
            bytes_accessed=2 * depth * (width + rank + rows),
            transcendentals=0,
        ),
        name="low_rank_and_base",
    )(hidden, rank_down, weight)


def stream_dot(hidden, weight, total, held, arrived, start):
    steps = weight.shape[0] // DEPTH
    copy = weight_copies(weight, held, arrived, start, total.shape[1])

    @pl.loop(0, steps)
    def _(k):
        copy(k).start()

    total[...] = jnp.zeros_like(total)

    @pl.loop(0, steps)
    def _(k):
        copy(k).wait()
        total[...] += jnp.dot(hidden[:, deep(k)], held[deep(k)], preferred_element_type=jnp.float32)


def base_kernel(start, hidden, weight, base, held, arrived):
    stream_dot(hidden, weight, base, held, arrived, start)


def base_phase(hidden, weight, start, width):
    rows, depth = hidden.shape
    return pl.pallas_call(
        functools.partial(base_kernel, start),
        out_shape=jax.ShapeDtypeStruct((rows, width), jnp.float32),
        in_specs=[VMEM, HBM],
        out_specs=VMEM,
        scratch_shapes=[
            pltpu.VMEM((depth, width), weight.dtype),
            pltpu.SemaphoreType.DMA((depth // DEPTH,)),
        ],
        compiler_params=pltpu.CompilerParams(vmem_limit_bytes=32 << 20),
        cost_estimate=pl.CostEstimate(
            flops=2 * rows * depth * width, bytes_accessed=2 * depth * width, transcendentals=0
        ),
        name="base",
    )(hidden, weight)


def split_rows(total, at, sent, kept):
    block = total.shape[0] // 4
    bit = lax.rem(lax.axis_index("tp"), 2)
    for half in range(2):
        rows = pl.ds(half * block, block)
        there = pl.ds(pl.multiple_of((2 * half + 1 - bit) * block, block), block)
        here = pl.ds(pl.multiple_of((2 * half + bit) * block, block), block)
        sent[rows, at] = total[there, :].astype(sent.dtype)
        kept[rows, at] = total[here, :]


def adapter_term(low, up):
    return jnp.dot(low.astype(jnp.bfloat16), up, preferred_element_type=jnp.float32)


def correct_kernel(ids, low_a, low_b, low_c, low_d, up, base_one, base_two, low, sent, kept, total):
    held = column_of(ids[...]) == lax.axis_index("tp").astype(jnp.float32)
    low[...] = jnp.where(held, (low_a[...] + low_b[...]) + (low_c[...] + low_d[...]), 0.0)
    start = 0
    for base in (base_one, base_two):
        width = base.shape[1]
        at = slice(start, start + width)
        total[:, at] = base[...] + adapter_term(low[...], up[:, at])
        start += width
    split_rows(total, slice(0, start), sent, kept)


def correct_phase(ids, lows, up, base_one, base_two):
    rows, rank = lows[0].shape
    width = base_one.shape[1] + base_two.shape[1]
    return pl.pallas_call(
        correct_kernel,
        out_shape=(
            jax.ShapeDtypeStruct((rows, rank), jnp.float32),
            jax.ShapeDtypeStruct((rows // 2, width), jnp.bfloat16),
            jax.ShapeDtypeStruct((rows // 2, width), jnp.float32),
        ),
        in_specs=[VMEM] * 8,
        out_specs=(VMEM,) * 3,
        scratch_shapes=[pltpu.VMEM((rows, width), jnp.float32)],
        compiler_params=pltpu.CompilerParams(vmem_limit_bytes=8 << 20),
        name="adapter_term",
    )(ids, *lows, up, base_one, base_two)


def last_kernel(start, hidden, weight, low, up, sent, kept, total, held, arrived):
    stream_dot(hidden, weight, total, held, arrived, start)
    width = total.shape[1]
    total[...] += adapter_term(low[...], up[:, start : start + width])
    split_rows(total, slice(0, width), sent, kept)


def last_phase(hidden, weight, low, up, start, width):
    rows, depth = hidden.shape
    return pl.pallas_call(
        functools.partial(last_kernel, start),
        out_shape=(
            jax.ShapeDtypeStruct((rows // 2, width), jnp.bfloat16),
            jax.ShapeDtypeStruct((rows // 2, width), jnp.float32),
        ),
        in_specs=[VMEM, HBM, VMEM, VMEM],
        out_specs=(VMEM, VMEM),
        scratch_shapes=[
            pltpu.VMEM((rows, width), jnp.float32),
            pltpu.VMEM((depth, width), weight.dtype),
            pltpu.SemaphoreType.DMA((depth // DEPTH,)),
        ],
        compiler_params=pltpu.CompilerParams(vmem_limit_bytes=32 << 20),
        cost_estimate=pl.CostEstimate(
            flops=2 * rows * depth * width, bytes_accessed=2 * depth * width, transcendentals=0
        ),
        name="last_base",
    )(hidden, weight, low, up)


def pair_kernel(kept, got, sent, total):
    block = kept.shape[0] // 2
    high = lax.div(lax.axis_index("tp"), 2)
    here = pl.ds(pl.multiple_of(high * block, block), block)
    there = pl.ds(pl.multiple_of((1 - high) * block, block), block)
    sent[...] = (kept[there, :] + got[there, :].astype(jnp.float32)).astype(sent.dtype)
    total[...] = kept[here, :] + got[here, :].astype(jnp.float32)


def pair_phase(kept, got):
    rows, width = kept.shape
    return pl.pallas_call(
        pair_kernel,
        out_shape=(
            jax.ShapeDtypeStruct((rows // 2, width), jnp.bfloat16),
            jax.ShapeDtypeStruct((rows // 2, width), jnp.float32),
        ),
        in_specs=[VMEM] * 2,
        out_specs=(VMEM,) * 2,
        compiler_params=pltpu.CompilerParams(vmem_limit_bytes=8 << 20),
        name="pair_sum",
    )(kept, got)


def finish_kernel(residual, total_one, got_one, total_two, got_two, mixed):
    start = 0
    for total, got in ((total_one, got_one), (total_two, got_two)):
        at = slice(start, start + total.shape[1])
        mixed[:, at] = (
            residual[:, at].astype(jnp.float32) + total[...] + got[...].astype(jnp.float32)
        ).astype(mixed.dtype)
        start = at.stop


def finish_phase(residual, *terms):
    return pl.pallas_call(
        finish_kernel,
        out_shape=jax.ShapeDtypeStruct(residual.shape, residual.dtype),
        in_specs=[VMEM] * 5,
        out_specs=VMEM,
        compiler_params=pltpu.CompilerParams(vmem_limit_bytes=8 << 20),
        name="finish",
    )(residual, *terms)


def swap(value, bit):
    return lax.ppermute(value, "tp", [(i, i ^ bit) for i in range(lax.axis_size("tp"))])


def four_by_four(hidden_units, adapter_ids, weight, rank_down, rank_up, residual):
    up = rank_up[0]
    one, two, three = WIDTHS
    low, base_one, hidden = first_phase(
        hidden_units, jnp.swapaxes(rank_down, 1, 2)[0], weight, 0, one
    )
    lows = []
    for j in range(4):
        pairs = [(t * 4 + a, a * 4 + (t + j) % 4) for t in range(4) for a in range(4)]
        lows.append(lax.ppermute(low, ("tp",) + PS, pairs))
    base_two = base_phase(hidden, weight, one, two)
    low, sent, kept = correct_phase(adapter_ids[None], lows, up, base_one, base_two)
    got = swap(sent, 1)
    sent_last, kept_last = last_phase(hidden, weight, low, up, one + two, three)
    got_last = swap(sent_last, 1)
    sent, total = pair_phase(kept, got)
    got = swap(sent, 2)
    sent_last, total_last = pair_phase(kept_last, got_last)
    got_last = swap(sent_last, 2)
    return finish_phase(residual, total, got, total_last, got_last)


def any_size(hidden_units, adapter_ids, down_projection_weight, rank_down, rank_up, residual):
    owned_count = rank_down.shape[0]
    first_owned = lax.axis_index(PS) * owned_count
    chosen = (
        (adapter_ids - first_owned)[:, None] == jnp.arange(owned_count, dtype=jnp.int32)[None, :]
    ).astype(jnp.float32)
    projected = jnp.einsum(
        "rf,afk->rak", hidden_units, rank_down, preferred_element_type=jnp.float32
    )
    partial_low = jnp.einsum("rak,ra->rk", projected, chosen)
    low_rank = lax.psum(partial_low, ("tp",) + PS).astype(jnp.bfloat16)
    held_count, rank_width, columns = rank_up.shape
    first_held = lax.axis_index("tp") * held_count
    picked = (
        (adapter_ids - first_held)[:, None] == jnp.arange(held_count, dtype=jnp.int32)[None, :]
    ).astype(jnp.bfloat16)
    coefficient = (picked[:, :, None] * low_rank[:, None, :]).reshape(
        -1, held_count * rank_width
    )
    term = jnp.dot(
        hidden_units, down_projection_weight, preferred_element_type=jnp.float32
    ) + jnp.dot(
        coefficient,
        rank_up.reshape(held_count * rank_width, columns),
        preferred_element_type=jnp.float32,
    )
    summed = lax.psum_scatter(
        term.astype(jnp.bfloat16), "tp", scatter_dimension=0, tiled=True
    ).astype(jnp.float32)
    return (residual.astype(jnp.float32) + summed).astype(jnp.bfloat16)


def on_device(hidden_units, adapter_ids, down_projection_weight, rank_down, rank_up, residual):
    sizes = [lax.axis_size(axis) for axis in ("tp",) + PS]
    fits = (
        sizes[0] == 4
        and sizes[1] * sizes[2] == 4
        and rank_down.shape[0] == 1
        and rank_up.shape[0] == 1
        and residual.shape == (16, sum(WIDTHS))
        and hidden_units.shape[1] % DEPTH == 0
    )
    form = four_by_four if fits else any_size
    return form(hidden_units, adapter_ids, down_projection_weight, rank_down, rank_up, residual)


def solution(mesh):
    placed = (
        P("parts", "tp"),
        P("parts"),
        P("tp", ("page", "sub")),
        P(("parts", "page", "sub"), "tp", None),
        P(("parts", "tp"), None, ("page", "sub")),
        P(("parts", "tp"), ("page", "sub")),
    )
    return jax.shard_map(
        on_device,
        mesh=mesh,
        in_specs=placed,
        out_specs=P(("parts", "tp"), ("page", "sub")),
        check_vma=False,
    )
```

time: 121 us -> 41.5 us (0.34)
  blocking collectives: 62.9 us -> 0 us
  matrix products: 23.3 us -> 0 us
  Pallas kernels: 0 us -> 21.9 us
  starting transfers between devices: 0.01 us -> 16.1 us
  waiting for transfers between devices: 18 us -> 3.15 us
  between operations: 13.4 us -> 0.11 us
  other arithmetic: 2.31 us -> 0 us
    psum x1 -> x0, blocking collectives: 62.9 us -> none  [on_device(): low_rank = lax.psum(partial_low, ('tp', 'page', 'sub')).astype(jnp.bfloat16)]
    dot_general x3 -> x0, matrix products: 23.3 us -> none  [the longest x1 20.5 us: on_device(): jnp.dot(hidden_units, down_projection_weight, preferred_element_type=jnp....]
    pallas_call x0 -> x7, Pallas kernels: none -> 21.9 us  [the longest x1 7.92 us: base_phase(): pl.pallas_call(functools.partial(base_kernel, start), out_shape=jax.Shape...]
    reduce_scatter x1 -> x0, waiting for transfers between devices: 18 us -> none  [on_device(): lax.psum_scatter((base_projection_term + jnp.dot(low_rank_coefficient, fl...]
    ppermute x0 -> x8, starting transfers between devices: none -> 16.1 us  [the longest x4 9.76 us: swap(): lax.ppermute(value, 'tp', [(i, i ^ bit) for i in range(lax.axis_size('tp'...]
    ppermute x0 -> x8, waiting for transfers between devices: none -> 3.15 us  [the longest x4 3.14 us: swap(): lax.ppermute(value, 'tp', [(i, i ^ bit) for i in range(lax.axis_size('tp'...]
    convert_element_type x2 -> x0, other arithmetic: 2.31 us -> none  [the longest x1 1.56 us: on_device(): return (residual.astype(jnp.float32) + summed).astype(jnp.bfloat16)]
  transfers between devices with their start and end apart: 1 -> 8, of which waited for: 1 -> 2; matrix products, arithmetic and copies ran while one was open for 0% -> 0% of each run, Pallas kernels for 0% -> 32%
where the time goes in v3:
time: 41.5 us; the launch traced here: 41.3 us
  Pallas kernels  21.9 us (53%)
  starting transfers between devices  16.1 us (39%)
  waiting for transfers between devices  3.15 us (8%)
    ppermute x4, starting transfers between devices, swap(): lax.ppermute(value, 'tp', [(i, i ^ bit) for i in range(lax.axis_size('tp'...  9.76 us
    pallas_call x1, Pallas kernels, base_phase(): pl.pallas_call(functools.partial(base_kernel, start), out_shape=jax.Shape...  7.92 us
    pallas_call x1, Pallas kernels, first_phase(): pl.pallas_call(functools.partial(first_kernel, start, width), out_shape=(...  7.5 us
    ppermute x4, starting transfers between devices, four_by_four(): lows.append(lax.ppermute(low, ('tp',) + PS, pairs))  6.34 us
    pallas_call x1, Pallas kernels, last_phase(): pl.pallas_call(functools.partial(last_kernel, start), out_shape=(jax.Shap...  5.43 us
    ppermute x4, waiting for transfers between devices, swap(): lax.ppermute(value, 'tp', [(i, i ^ bit) for i in range(lax.axis_size('tp'...  3.14 us
  transfers between devices with their start and end apart: 8, of which 2 were waited for; matrix products, arithmetic and copies ran while one was open for 0% of the time, Pallas kernels for 32%

profile of v3, /device:TPU:0, one launch (start us, length us, event | category | flops | bytes accessed | tf_op | source)
XLA Modules:
  0.0 41.3 jit_solution(17039661002245356137)
XLA Ops:
  0.0 7.5 %low_rank_and_base.1 = (f32[64,64]{1,0:T(8,128)S(1)}, f32[64,1024]{1,0:T(8,128)S(1)}, bf16[64,8448]{1,0:T(8,128)(2,1)S(1)}) custom-call(bf16[64,8448]{1,0:T(8,128)(2,1)} %hidden.1, bf16[64,8448]{1,0:T(8,128)(2,1)} %bitcast.8, bf16[8448,3072]{1,0:T(8,128)(2,1)} %weight.5), custom_call_target="tpu_custom_call" | custom-call | flops 1176502272 | bytes 19464192 | tf_op jit(solution)/shard_map/low_rank_and_base/pallas_call | solution.py:102
  7.5 2.4 %collective-permute-start.3 = (f32[64,64]{1,0:T(8,128)S(1)}, f32[64,64]{1,0:T(8,128)S(1)}, u32[]{:S(2)}, u32[]{:S(2)}) collective-permute-start(f32[64,64]{1,0:T(8,128)S(1)} %get-tuple-element.17), channel_id=1, source_target_pairs={{0,3},{1,7},{2,11},{3,15},{4,0},{5,4},{6,8},{7,12},{8,1},{9,5},{10... | collective-permute-start | bytes 49160 | tf_op jit(solution)/shard_map/ppermute | solution.py:299
  10.0 2.6 %collective-permute-start.2 = (f32[64,64]{1,0:T(8,128)S(1)}, f32[64,64]{1,0:T(8,128)S(1)}, u32[]{:S(2)}, u32[]{:S(2)}) collective-permute-start(f32[64,64]{1,0:T(8,128)S(1)} %get-tuple-element.17), channel_id=1, source_target_pairs={{0,2},{1,6},{2,10},{3,14},{4,3},{5,7},{6,11},{7,15},{8,0},{9,4},{1... | collective-permute-start | bytes 49160 | tf_op jit(solution)/shard_map/ppermute | solution.py:299
  12.5 0.6 %collective-permute-start.1 = (f32[64,64]{1,0:T(8,128)S(1)}, f32[64,64]{1,0:T(8,128)S(1)}, u32[]{:S(2)}, u32[]{:S(2)}) collective-permute-start(f32[64,64]{1,0:T(8,128)S(1)} %get-tuple-element.17), channel_id=1, source_target_pairs={{0,1},{1,5},{2,9},{3,13},{4,2},{5,6},{6,10},{7,14},{8,3},{9,7},{10... | collective-permute-start | bytes 49160 | tf_op jit(solution)/shard_map/ppermute | solution.py:299
  13.2 0.7 %collective-permute-start = (f32[64,64]{1,0:T(8,128)S(1)}, f32[64,64]{1,0:T(8,128)S(1)}, u32[]{:S(2)}, u32[]{:S(2)}) collective-permute-start(f32[64,64]{1,0:T(8,128)S(1)} %get-tuple-element.17), channel_id=1, source_target_pairs={{0,0},{1,4},{2,8},{3,12},{4,1},{5,5},{6,9},{7,13},{8,2},{9,6},{10,... | collective-permute-start | bytes 49160 | tf_op jit(solution)/shard_map/ppermute | solution.py:299
  13.9 0.0 copy-start
  13.9 0.0 copy-start.2
  13.9 7.9 %base.1.base_two = f32[64,1280]{1,0:T(8,128)S(1)} custom-call(bf16[64,8448]{1,0:T(8,128)(2,1)S(1)} %get-tuple-element.19.hidden, bf16[8448,3072]{1,0:T(8,128)(2,1)} %weight.5), custom_call_target="tpu_custom_call" | custom-call | flops 1384120320 | bytes 21626880 | tf_op jit(solution)/shard_map/base/pallas_call | solution.py:149
  21.8 0.0 collective-permute-done.3.low_d
  21.8 0.0 collective-permute-done.2.low_c
  21.8 0.0 collective-permute-done.1.low_b
  21.8 0.0 collective-permute-done.low_a
  21.8 0.0 copy-done
  21.9 0.0 copy-done.2
  21.9 0.4 adapter_term.1
  22.2 4.0 %collective-permute-start.4 = (bf16[32,2304]{1,0:T(8,128)(2,1)S(1)}, bf16[32,2304]{1,0:T(8,128)(2,1)S(1)}, u32[]{:S(2)}, u32[]{:S(2)}) collective-permute-start(bf16[32,2304]{1,0:T(8,128)(2,1)S(1)} %get-tuple-element.21), channel_id=1, source_target_pairs={{0,4},{4,0},{8,12},{12,8},{1,5},{5,1},{9,13},{13,9},{2,6},{6,2},{1... | collective-permute-start | bytes 442376 | tf_op jit(solution)/shard_map/ppermute | solution.py:287
  26.2 0.0 copy-start.1
  26.2 5.4 %last_base.1 = (bf16[32,768]{1,0:T(8,128)(2,1)S(1)}, f32[32,768]{1,0:T(8,128)S(1)}) custom-call(bf16[64,8448]{1,0:T(8,128)(2,1)S(1)} %get-tuple-element.19.hidden, bf16[8448,3072]{1,0:T(8,128)(2,1)} %weight.5, f32[64,64]{1,0:T(8,128)S(1)} %get-tuple-element.24.low, bf16[64,3072]{1,0:T(8,128)(2,1)S(1)} %bitcast.6), custom_call_target="tpu_custom_call" | custom-call | flops 830472192 | bytes 12976128 | tf_op jit(solution)/shard_map/last_base/pallas_call | solution.py:220
  31.7 0.1 collective-permute-start.6
  31.8 0.0 collective-permute-done.4.got
  31.8 2.9 %collective-permute-start.5 = (bf16[16,2304]{1,0:T(8,128)(2,1)S(1)}, bf16[16,2304]{1,0:T(8,128)(2,1)S(1)}, u32[]{:S(2)}, u32[]{:S(2)}) collective-permute-start(bf16[16,2304]{1,0:T(8,128)(2,1)S(1)} %get-tuple-element.23), channel_id=1, source_target_pairs={{0,8},{4,12},{8,0},{12,4},{1,9},{5,13},{9,1},{13,5},{2,10},{6,14},... | collective-permute-start | bytes 221192 | tf_op jit(solution)/shard_map/ppermute | solution.py:287
  34.7 1.2 %collective-permute-done.6.got = bf16[32,768]{1,0:T(8,128)(2,1)S(1)} collective-permute-done((bf16[32,768]{1,0:T(8,128)(2,1)S(1)}, bf16[32,768]{1,0:T(8,128)(2,1)S(1)}, u32[]{:S(2)}, u32[]{:S(2)}) %collective-permute-start.6) | collective-permute-done | bytes 49184 | tf_op jit(solution)/shard_map/ppermute | solution.py:287
  35.8 2.8 %collective-permute-start.7 = (bf16[16,768]{1,0:T(8,128)(2,1)S(1)}, bf16[16,768]{1,0:T(8,128)(2,1)S(1)}, u32[]{:S(2)}, u32[]{:S(2)}) collective-permute-start(bf16[16,768]{1,0:T(8,128)(2,1)S(1)} %get-tuple-element.28), channel_id=1, source_target_pairs={{0,8},{4,12},{8,0},{12,4},{1,9},{5,13},{9,1},{13,5},{2,10},{6,14},... | collective-permute-start | bytes 73736 | tf_op jit(solution)/shard_map/ppermute | solution.py:287
  38.7 2.0 %collective-permute-done.7.got_two = bf16[16,768]{1,0:T(8,128)(2,1)S(1)} collective-permute-done((bf16[16,768]{1,0:T(8,128)(2,1)S(1)}, bf16[16,768]{1,0:T(8,128)(2,1)S(1)}, u32[]{:S(2)}, u32[]{:S(2)}) %collective-permute-start.7) | collective-permute-done | bytes 24608 | tf_op jit(solution)/shard_map/ppermute | solution.py:287
  40.6 0.0 collective-permute-done.5.got_one
  40.6 0.0 copy-done.1
  40.6 0.7 %finish.1 = bf16[16,3072]{1,0:T(8,128)(2,1)} custom-call(bf16[16,3072]{1,0:T(8,128)(2,1)S(1)} %copy-done.1, f32[16,2304]{1,0:T(8,128)S(1)} %get-tuple-element.22.total_one, bf16[16,2304]{1,0:T(8,128)(2,1)S(1)} %collective-permute-done.5.got_one, f32[16,768]{1,0:T(8,128)S(1)} %get-tuple-element.27.total_two, bf16[16,768]{1,0:T(8,128)(2,1)S(1)} %collective-permute-done.7.got_two), custom_call_target="tpu_custom_call" | custom-call | tf_op jit(solution)/shard_map/finish/pallas_call | solution.py:276
  (2 shorter events, 0.0 us)
Async XLA Ops:
  7.5 14.3 %collective-permute-start.3 = (f32[64,64]{1,0:T(8,128)S(1)}, f32[64,64]{1,0:T(8,128)S(1)}, u32[]{:S(2)}, u32[]{:S(2)}) collective-permute-start(f32[64,64]{1,0:T(8,128)S(1)} %get-tuple-element.17), channel_id=1, source_target_pairs={{0,3},{1,7},{2,11},{3,15},{4,0},{5,4},{6,8},{7,12},{8,1},{9,5},{10... | collective-permute-start | bytes 49160 | tf_op jit(solution)/shard_map/ppermute | solution.py:299
  10.0 11.9 %collective-permute-start.2 = (f32[64,64]{1,0:T(8,128)S(1)}, f32[64,64]{1,0:T(8,128)S(1)}, u32[]{:S(2)}, u32[]{:S(2)}) collective-permute-start(f32[64,64]{1,0:T(8,128)S(1)} %get-tuple-element.17), channel_id=1, source_target_pairs={{0,2},{1,6},{2,10},{3,14},{4,3},{5,7},{6,11},{7,15},{8,0},{9,4},{1... | collective-permute-start | bytes 49160 | tf_op jit(solution)/shard_map/ppermute | solution.py:299
  12.5 9.3 %collective-permute-start.1 = (f32[64,64]{1,0:T(8,128)S(1)}, f32[64,64]{1,0:T(8,128)S(1)}, u32[]{:S(2)}, u32[]{:S(2)}) collective-permute-start(f32[64,64]{1,0:T(8,128)S(1)} %get-tuple-element.17), channel_id=1, source_target_pairs={{0,1},{1,5},{2,9},{3,13},{4,2},{5,6},{6,10},{7,14},{8,3},{9,7},{10... | collective-permute-start | bytes 49160 | tf_op jit(solution)/shard_map/ppermute | solution.py:299
  13.2 8.6 %collective-permute-start = (f32[64,64]{1,0:T(8,128)S(1)}, f32[64,64]{1,0:T(8,128)S(1)}, u32[]{:S(2)}, u32[]{:S(2)}) collective-permute-start(f32[64,64]{1,0:T(8,128)S(1)} %get-tuple-element.17), channel_id=1, source_target_pairs={{0,0},{1,4},{2,8},{3,12},{4,1},{5,5},{6,9},{7,13},{8,2},{9,6},{10,... | collective-permute-start | bytes 49160 | tf_op jit(solution)/shard_map/ppermute | solution.py:299
  13.9 8.0 %copy-start = (bf16[1,64,3072]{2,1,0:T(8,128)(2,1)S(1)}, bf16[1,64,3072]{2,1,0:T(8,128)(2,1)}, u32[]{:S(2)}) copy-start(bf16[1,64,3072]{2,1,0:T(8,128)(2,1)} %param.10) | copy-start | bytes 1179652
  13.9 8.0 %copy-start.2 = (s32[64]{0:T(128)S(1)}, s32[64]{0:T(128)}, u32[]{:S(2)}) copy-start(s32[64]{0:T(128)} %param.7) | copy-start | bytes 772
  22.2 9.5 %collective-permute-start.4 = (bf16[32,2304]{1,0:T(8,128)(2,1)S(1)}, bf16[32,2304]{1,0:T(8,128)(2,1)S(1)}, u32[]{:S(2)}, u32[]{:S(2)}) collective-permute-start(bf16[32,2304]{1,0:T(8,128)(2,1)S(1)} %get-tuple-element.21), channel_id=1, source_target_pairs={{0,4},{4,0},{8,12},{12,8},{1,5},{5,1},{9,13},{13,9},{2,6},{6,2},{1... | collective-permute-start | bytes 442376 | tf_op jit(solution)/shard_map/ppermute | solution.py:287
  26.2 14.4 %copy-start.1 = (bf16[16,3072]{1,0:T(8,128)(2,1)S(1)}, bf16[16,3072]{1,0:T(8,128)(2,1)}, u32[]{:S(2)}) copy-start(bf16[16,3072]{1,0:T(8,128)(2,1)} %residual.1) | copy-start | bytes 294916
  31.7 4.2 %collective-permute-start.6 = (bf16[32,768]{1,0:T(8,128)(2,1)S(1)}, bf16[32,768]{1,0:T(8,128)(2,1)S(1)}, u32[]{:S(2)}, u32[]{:S(2)}) collective-permute-start(bf16[32,768]{1,0:T(8,128)(2,1)S(1)} %get-tuple-element.26), channel_id=1, source_target_pairs={{0,4},{4,0},{8,12},{12,8},{1,5},{5,1},{9,13},{13,9},{2,6},{6,2},{1... | collective-permute-start | bytes 147464 | tf_op jit(solution)/shard_map/ppermute | solution.py:287
  31.8 8.8 %collective-permute-start.5 = (bf16[16,2304]{1,0:T(8,128)(2,1)S(1)}, bf16[16,2304]{1,0:T(8,128)(2,1)S(1)}, u32[]{:S(2)}, u32[]{:S(2)}) collective-permute-start(bf16[16,2304]{1,0:T(8,128)(2,1)S(1)} %get-tuple-element.23), channel_id=1, source_target_pairs={{0,8},{4,12},{8,0},{12,4},{1,9},{5,13},{9,1},{13,5},{2,10},{6,14},... | collective-permute-start | bytes 221192 | tf_op jit(solution)/shard_map/ppermute | solution.py:287
  35.8 4.8 %collective-permute-start.7 = (bf16[16,768]{1,0:T(8,128)(2,1)S(1)}, bf16[16,768]{1,0:T(8,128)(2,1)S(1)}, u32[]{:S(2)}, u32[]{:S(2)}) collective-permute-start(bf16[16,768]{1,0:T(8,128)(2,1)S(1)} %get-tuple-element.28), channel_id=1, source_target_pairs={{0,8},{4,12},{8,0},{12,4},{1,9},{5,13},{9,1},{13,5},{2,10},{6,14},... | collective-permute-start | bytes 73736 | tf_op jit(solution)/shard_map/ppermute | solution.py:287

commit v4 on v3

--- a/solution.py
+++ b/solution.py
@@ -7,8 +7,9 @@
 from jax.experimental.pallas import tpu as pltpu
 from jax.sharding import PartitionSpec as P
 
-WIDTHS = (1024, 1280, 768)
+WIDTHS = (1024, 1024, 512, 512)
 DEPTH = 768
+IN_FLIGHT = 4
 PS = ("page", "sub")
 VMEM = pl.BlockSpec(memory_space=pltpu.VMEM)
 HBM = pl.BlockSpec(memory_space=pltpu.HBM)
@@ -37,22 +38,8 @@
     return copy
 
 
-def first_kernel(
-    start,
-    width,
-    hidden,
-    rank_down,
-    weight,
-    low,
-    base,
-    hidden_here,
-    down_here,
-    held,
-    got,
-    arrived,
-):
-    steps = weight.shape[0] // DEPTH
-    copy = weight_copies(weight, held, arrived, start, width)
+def low_kernel(hidden, rank_down, low, hidden_here, down_here, got):
+    steps = hidden.shape[1] // DEPTH
 
     def hidden_copy(k):
         return pltpu.make_async_copy(
@@ -69,12 +56,7 @@
         hidden_copy(k).start()
         down_copy(k).start()
 
-    @pl.loop(0, steps)
-    def _(k):
-        copy(k).start()
-
     low[...] = jnp.zeros_like(low)
-    base[...] = jnp.zeros_like(base)
 
     @pl.loop(0, steps)
     def _(k):
@@ -87,55 +69,48 @@
             preferred_element_type=jnp.float32,
         )
 
-    @pl.loop(0, steps)
-    def _(k):
-        copy(k).wait()
-        base[...] += jnp.dot(
-            hidden_here[:, deep(k)], held[deep(k)], preferred_element_type=jnp.float32
-        )
-
-
-def first_phase(hidden, rank_down, weight, start, width):
+
+def low_phase(hidden, rank_down):
     rows, depth = hidden.shape
     rank = rank_down.shape[0]
-    steps = depth // DEPTH
-    return pl.pallas_call(
-        functools.partial(first_kernel, start, width),
+    return pl.pallas_call(
+        low_kernel,
         out_shape=(
             jax.ShapeDtypeStruct((rows, rank), jnp.float32),
-            jax.ShapeDtypeStruct((rows, width), jnp.float32),
             jax.ShapeDtypeStruct(hidden.shape, hidden.dtype),
         ),
-        in_specs=[HBM] * 3,
-        out_specs=(VMEM, VMEM, VMEM),
+        in_specs=[HBM] * 2,
+        out_specs=(VMEM, VMEM),
         scratch_shapes=[
             pltpu.VMEM(rank_down.shape, rank_down.dtype),
-            pltpu.VMEM((depth, width), weight.dtype),
-            pltpu.SemaphoreType.DMA((2, steps)),
-            pltpu.SemaphoreType.DMA((steps,)),
+            pltpu.SemaphoreType.DMA((2, depth // DEPTH)),
         ],
         compiler_params=pltpu.CompilerParams(vmem_limit_bytes=52 << 20),
         cost_estimate=pl.CostEstimate(
-            flops=2 * rows * depth * (width + rank),
-            bytes_accessed=2 * depth * (width + rank + rows),
+            flops=2 * rows * depth * rank,
+            bytes_accessed=2 * depth * (rank + rows),
             transcendentals=0,
         ),
-        name="low_rank_and_base",
-    )(hidden, rank_down, weight)
+        name="low_rank",
+    )(hidden, rank_down)
 
 
 def stream_dot(hidden, weight, total, held, arrived, start):
     steps = weight.shape[0] // DEPTH
     copy = weight_copies(weight, held, arrived, start, total.shape[1])
 
+    @pl.loop(0, IN_FLIGHT)
+    def _(k):
+        copy(k).start()
+
+    total[...] = jnp.zeros_like(total)
+
     @pl.loop(0, steps)
     def _(k):
-        copy(k).start()
-
-    total[...] = jnp.zeros_like(total)
-
-    @pl.loop(0, steps)
-    def _(k):
+        @pl.when(k + IN_FLIGHT < steps)
+        def _():
+            copy(k + IN_FLIGHT).start()
+
         copy(k).wait()
         total[...] += jnp.dot(hidden[:, deep(k)], held[deep(k)], preferred_element_type=jnp.float32)
 
@@ -208,25 +183,28 @@
     )(ids, *lows, up, base_one, base_two)
 
 
-def last_kernel(start, hidden, weight, low, up, sent, kept, total, held, arrived):
-    stream_dot(hidden, weight, total, held, arrived, start)
-    width = total.shape[1]
-    total[...] += adapter_term(low[...], up[:, start : start + width])
-    split_rows(total, slice(0, width), sent, kept)
-
-
-def last_phase(hidden, weight, low, up, start, width):
+def last_kernel(start, hidden, weight, low, up, base, sent, kept, total, held, arrived):
+    before = base.shape[1]
+    width = total.shape[1] - before
+    stream_dot(hidden, weight, total.at[:, before:], held, arrived, start + before)
+    total[:, :before] = base[...]
+    total[...] += adapter_term(low[...], up[:, start : start + before + width])
+    split_rows(total, slice(0, before + width), sent, kept)
+
+
+def last_phase(hidden, weight, low, up, base, start, width):
     rows, depth = hidden.shape
+    both = base.shape[1] + width
     return pl.pallas_call(
         functools.partial(last_kernel, start),
         out_shape=(
-            jax.ShapeDtypeStruct((rows // 2, width), jnp.bfloat16),
-            jax.ShapeDtypeStruct((rows // 2, width), jnp.float32),
-        ),
-        in_specs=[VMEM, HBM, VMEM, VMEM],
+            jax.ShapeDtypeStruct((rows // 2, both), jnp.bfloat16),
+            jax.ShapeDtypeStruct((rows // 2, both), jnp.float32),
+        ),
+        in_specs=[VMEM, HBM, VMEM, VMEM, VMEM],
         out_specs=(VMEM, VMEM),
         scratch_shapes=[
-            pltpu.VMEM((rows, width), jnp.float32),
+            pltpu.VMEM((rows, both), jnp.float32),
             pltpu.VMEM((depth, width), weight.dtype),
             pltpu.SemaphoreType.DMA((depth // DEPTH,)),
         ],
@@ -235,7 +213,7 @@
             flops=2 * rows * depth * width, bytes_accessed=2 * depth * width, transcendentals=0
         ),
         name="last_base",
-    )(hidden, weight, low, up)
+    )(hidden, weight, low, up, base)
 
 
 def pair_kernel(kept, got, sent, total):
@@ -289,21 +267,26 @@
 
 def four_by_four(hidden_units, adapter_ids, weight, rank_down, rank_up, residual):
     up = rank_up[0]
-    one, two, three = WIDTHS
-    low, base_one, hidden = first_phase(
-        hidden_units, jnp.swapaxes(rank_down, 1, 2)[0], weight, 0, one
-    )
-    lows = []
-    for j in range(4):
-        pairs = [(t * 4 + a, a * 4 + (t + j) % 4) for t in range(4) for a in range(4)]
-        lows.append(lax.ppermute(low, ("tp",) + PS, pairs))
+    one, two, three, four = WIDTHS
+    low, hidden = low_phase(hidden_units, jnp.swapaxes(rank_down, 1, 2)[0])
+    pairs = [(t * 4 + a, a * 4 + t) for t in range(4) for a in range(4)]
+    low = lax.ppermute(low, ("tp",) + PS, pairs)
+    base_one = base_phase(hidden, weight, 0, one)
+    hidden, low, base_one = lax.optimization_barrier((hidden, low, base_one))
+    lows = [low] + [
+        lax.ppermute(low, PS, [(i, i ^ other) for i in range(4)]) for other in (2, 3, 1)
+    ]
     base_two = base_phase(hidden, weight, one, two)
     low, sent, kept = correct_phase(adapter_ids[None], lows, up, base_one, base_two)
     got = swap(sent, 1)
-    sent_last, kept_last = last_phase(hidden, weight, low, up, one + two, three)
-    got_last = swap(sent_last, 1)
+    hidden, low = lax.optimization_barrier((hidden, low))
+    base_three = base_phase(hidden, weight, one + two, three)
+    kept, got, base_three = lax.optimization_barrier((kept, got, base_three))
     sent, total = pair_phase(kept, got)
     got = swap(sent, 2)
+    hidden, total = lax.optimization_barrier((hidden, total))
+    sent_last, kept_last = last_phase(hidden, weight, low, up, base_three, one + two, four)
+    got_last = swap(sent_last, 1)
     sent_last, total_last = pair_phase(kept_last, got_last)
     got_last = swap(sent_last, 2)
     return finish_phase(residual, total, got, total_last, got_last)

time: 41.5 us -> 46.2 us (1.11)
  Pallas kernels: 21.9 us -> 27 us
  starting transfers between devices: 16.1 us -> 12.2 us
  waiting for transfers between devices: 3.15 us -> 6.61 us
    pallas_call x1 -> x3, Pallas kernels: 7.92 us -> 18.1 us  [base_phase(): pl.pallas_call(functools.partial(base_kernel, start), out_shape=jax.Shape...]
    ppermute x4, starting transfers between devices: 9.76 us -> 3.56 us  [swap(): lax.ppermute(value, 'tp', [(i, i ^ bit) for i in range(lax.axis_size('tp'...]
    pallas_call x1, Pallas kernels: 7.5 us -> 2.99 us  [low_phase(): pl.pallas_call(low_kernel, out_shape=(jax.ShapeDtypeStruct((rows, rank),...]
    ppermute x4, waiting for transfers between devices: 3.14 us -> 6.6 us  [swap(): lax.ppermute(value, 'tp', [(i, i ^ bit) for i in range(lax.axis_size('tp'...]
    ppermute x4, starting transfers between devices: 6.34 us -> 8.64 us  [the longest x3 7.97 us: four_by_four(): lax.ppermute(low, PS, [(i, i ^ other) for i in range(4)])]
    pallas_call x1, Pallas kernels: 5.43 us -> 4.84 us  [last_phase(): pl.pallas_call(functools.partial(last_kernel, start), out_shape=(jax.Shap...]
  transfers between devices with their start and end apart: 8 -> 8, of which waited for: 2 -> 4; matrix products, arithmetic and copies ran while one was open for 0% -> 0% of each run, Pallas kernels for 32% -> 39%
where the time goes in v4:
time: 46.2 us; the launch traced here: 46 us
  Pallas kernels  27 us (58%)
  starting transfers between devices  12.2 us (26%)
  waiting for transfers between devices  6.61 us (14%)
    pallas_call x3, Pallas kernels, base_phase(): pl.pallas_call(functools.partial(base_kernel, start), out_shape=jax.Shape...  18.1 us
    ppermute x3, starting transfers between devices, four_by_four(): lax.ppermute(low, PS, [(i, i ^ other) for i in range(4)])  7.97 us
    ppermute x4, waiting for transfers between devices, swap(): lax.ppermute(value, 'tp', [(i, i ^ bit) for i in range(lax.axis_size('tp'...  6.6 us
    pallas_call x1, Pallas kernels, last_phase(): pl.pallas_call(functools.partial(last_kernel, start), out_shape=(jax.Shap...  4.84 us
    ppermute x4, starting transfers between devices, swap(): lax.ppermute(value, 'tp', [(i, i ^ bit) for i in range(lax.axis_size('tp'...  3.56 us
    pallas_call x1, Pallas kernels, low_phase(): pl.pallas_call(low_kernel, out_shape=(jax.ShapeDtypeStruct((rows, rank),...  2.99 us
  transfers between devices with their start and end apart: 8, of which 4 were waited for; matrix products, arithmetic and copies ran while one was open for 0% of the time, Pallas kernels for 39%

profile of v4, /device:TPU:0, one launch (start us, length us, event | category | flops | bytes accessed | tf_op | source)
XLA Modules:
  0.0 46.0 jit_solution(16771794716212030446)
XLA Ops:
  0.0 3.0 %low_rank.1 = (f32[64,64]{1,0:T(8,128)S(1)}, bf16[64,8448]{1,0:T(8,128)(2,1)S(1)}) custom-call(bf16[64,8448]{1,0:T(8,128)(2,1)} %hidden.1, bf16[64,8448]{1,0:T(8,128)(2,1)} %bitcast.8), custom_call_target="tpu_custom_call" | custom-call | flops 69206016 | bytes 2162688 | tf_op jit(solution)/shard_map/low_rank/pallas_call | solution.py:76
  3.0 0.7 %collective-permute-start = (f32[64,64]{1,0:T(8,128)S(1)}, f32[64,64]{1,0:T(8,128)S(1)}, u32[]{:S(2)}, u32[]{:S(2)}) collective-permute-start(f32[64,64]{1,0:T(8,128)S(1)} %get-tuple-element.27), channel_id=1, source_target_pairs={{0,0},{1,4},{2,8},{3,12},{4,1},{5,5},{6,9},{7,13},{8,2},{9,6},{10,... | collective-permute-start | bytes 49160 | tf_op jit(solution)/shard_map/ppermute | solution.py:273
  3.7 6.8 %base.3.base_one = f32[64,1024]{1,0:T(8,128)S(1)} custom-call(bf16[64,8448]{1,0:T(8,128)(2,1)S(1)} %get-tuple-element.40.hidden, bf16[8448,3072]{1,0:T(8,128)(2,1)} %weight.7), custom_call_target="tpu_custom_call" | custom-call | flops 1107296256 | bytes 17301504 | tf_op jit(solution)/shard_map/base/pallas_call | solution.py:124
  10.4 0.0 copy-start
  10.5 0.0 copy-start.2
  10.5 0.0 collective-permute-done.low_a
  10.5 4.5 %collective-permute-start.3 = (f32[64,64]{1,0:T(8,128)S(1)}, f32[64,64]{1,0:T(8,128)S(1)}, u32[]{:S(2)}, u32[]{:S(2)}) collective-permute-start(f32[64,64]{1,0:T(8,128)S(1)} %collective-permute-done.low_a), channel_id=1, source_target_pairs={{0,1},{1,0},{2,3},{3,2},{4,5},{5,4},{6,7},{7,6},{8,9},{9,8},{10,11... | collective-permute-start | bytes 49160 | tf_op jit(solution)/shard_map/ppermute | solution.py:277
  14.9 3.2 %collective-permute-start.2 = (f32[64,64]{1,0:T(8,128)S(1)}, f32[64,64]{1,0:T(8,128)S(1)}, u32[]{:S(2)}, u32[]{:S(2)}) collective-permute-start(f32[64,64]{1,0:T(8,128)S(1)} %collective-permute-done.low_a), channel_id=1, source_target_pairs={{0,3},{1,2},{2,1},{3,0},{4,7},{5,6},{6,5},{7,4},{8,11},{9,10},{10,... | collective-permute-start | bytes 49160 | tf_op jit(solution)/shard_map/ppermute | solution.py:277
  18.1 0.3 collective-permute-start.1
  18.5 6.8 %base.4.base_two = f32[64,1024]{1,0:T(8,128)S(1)} custom-call(bf16[64,8448]{1,0:T(8,128)(2,1)S(1)} %get-tuple-element.40.hidden, bf16[8448,3072]{1,0:T(8,128)(2,1)} %weight.7), custom_call_target="tpu_custom_call" | custom-call | flops 1107296256 | bytes 17301504 | tf_op jit(solution)/shard_map/base/pallas_call | solution.py:124
  25.2 0.0 collective-permute-done.3.low_d
  25.2 0.0 collective-permute-done.2.low_c
  25.2 0.0 collective-permute-done.1.low_b
  25.2 0.0 copy-done
  25.3 0.0 copy-done.2
  25.3 0.3 adapter_term.1
  25.6 0.1 collective-permute-start.4
  25.7 4.6 %base.5 = f32[64,512]{1,0:T(8,128)S(1)} custom-call(bf16[64,8448]{1,0:T(8,128)(2,1)S(1)} %get-tuple-element.40.hidden, bf16[8448,3072]{1,0:T(8,128)(2,1)} %weight.7), custom_call_target="tpu_custom_call" | custom-call | flops 553648128 | bytes 8650752 | tf_op jit(solution)/shard_map/base/pallas_call | solution.py:124
  30.3 0.8 %collective-permute-done.4.got = bf16[32,2048]{1,0:T(8,128)(2,1)S(1)} collective-permute-done((bf16[32,2048]{1,0:T(8,128)(2,1)S(1)}, bf16[32,2048]{1,0:T(8,128)(2,1)S(1)}, u32[]{:S(2)}, u32[]{:S(2)}) %collective-permute-start.4) | collective-permute-done | bytes 131104 | tf_op jit(solution)/shard_map/ppermute | solution.py:265
  31.2 0.0 copy-start.1
  31.2 4.8 %last_base.1 = (bf16[32,1024]{1,0:T(8,128)(2,1)S(1)}, f32[32,1024]{1,0:T(8,128)S(1)}) custom-call(bf16[64,8448]{1,0:T(8,128)(2,1)S(1)} %get-tuple-element.40.hidden, bf16[8448,3072]{1,0:T(8,128)(2,1)} %weight.7, f32[64,64]{1,0:T(8,128)S(1)} %get-tuple-element.41.low, bf16[64,3072]{1,0:T(8,128)(2,1)S(1)} %bitcast.6, f32[64,512]{1,0:T(8,128)S(1)} %base.5), custom_call_target="tpu_custom_call" | custom-call | flops 553648128 | bytes 8650752 | tf_op jit(solution)/shard_map/last_base/pallas_call | solution.py:198
  36.0 1.3 %collective-permute-start.6 = (bf16[32,1024]{1,0:T(8,128)(2,1)S(1)}, bf16[32,1024]{1,0:T(8,128)(2,1)S(1)}, u32[]{:S(2)}, u32[]{:S(2)}) collective-permute-start(bf16[32,1024]{1,0:T(8,128)(2,1)S(1)} %get-tuple-element.44), channel_id=1, source_target_pairs={{0,4},{4,0},{8,12},{12,8},{1,5},{5,1},{9,13},{13,9},{2,6},{6,2},{1... | collective-permute-start | bytes 196616 | tf_op jit(solution)/shard_map/ppermute | solution.py:265
  37.3 0.8 %collective-permute-start.5 = (bf16[16,2048]{1,0:T(8,128)(2,1)S(1)}, bf16[16,2048]{1,0:T(8,128)(2,1)S(1)}, u32[]{:S(2)}, u32[]{:S(2)}) collective-permute-start(bf16[16,2048]{1,0:T(8,128)(2,1)S(1)} %get-tuple-element.39), channel_id=1, source_target_pairs={{0,8},{4,12},{8,0},{12,4},{1,9},{5,13},{9,1},{13,5},{2,10},{6,14},... | collective-permute-start | bytes 196616 | tf_op jit(solution)/shard_map/ppermute | solution.py:265
  38.1 2.3 %collective-permute-done.6.got = bf16[32,1024]{1,0:T(8,128)(2,1)S(1)} collective-permute-done((bf16[32,1024]{1,0:T(8,128)(2,1)S(1)}, bf16[32,1024]{1,0:T(8,128)(2,1)S(1)}, u32[]{:S(2)}, u32[]{:S(2)}) %collective-permute-start.6) | collective-permute-done | bytes 65568 | tf_op jit(solution)/shard_map/ppermute | solution.py:265
  40.4 1.4 %collective-permute-start.7 = (bf16[16,1024]{1,0:T(8,128)(2,1)S(1)}, bf16[16,1024]{1,0:T(8,128)(2,1)S(1)}, u32[]{:S(2)}, u32[]{:S(2)}) collective-permute-start(bf16[16,1024]{1,0:T(8,128)(2,1)S(1)} %get-tuple-element.46), channel_id=1, source_target_pairs={{0,8},{4,12},{8,0},{12,4},{1,9},{5,13},{9,1},{13,5},{2,10},{6,14},... | collective-permute-start | bytes 98312 | tf_op jit(solution)/shard_map/ppermute | solution.py:265
  41.9 2.0 %collective-permute-done.5.got_one = bf16[16,2048]{1,0:T(8,128)(2,1)S(1)} collective-permute-done((bf16[16,2048]{1,0:T(8,128)(2,1)S(1)}, bf16[16,2048]{1,0:T(8,128)(2,1)S(1)}, u32[]{:S(2)}, u32[]{:S(2)}) %collective-permute-start.5) | collective-permute-done | bytes 65568 | tf_op jit(solution)/shard_map/ppermute | solution.py:265
  43.9 1.4 %collective-permute-done.7.got_two = bf16[16,1024]{1,0:T(8,128)(2,1)S(1)} collective-permute-done((bf16[16,1024]{1,0:T(8,128)(2,1)S(1)}, bf16[16,1024]{1,0:T(8,128)(2,1)S(1)}, u32[]{:S(2)}, u32[]{:S(2)}) %collective-permute-start.7) | collective-permute-done | bytes 32800 | tf_op jit(solution)/shard_map/ppermute | solution.py:265
  45.3 0.0 copy-done.1
  45.3 0.7 %finish.1 = bf16[16,3072]{1,0:T(8,128)(2,1)} custom-call(bf16[16,3072]{1,0:T(8,128)(2,1)S(1)} %copy-done.1, f32[16,2048]{1,0:T(8,128)S(1)} %get-tuple-element.38.total_one, bf16[16,2048]{1,0:T(8,128)(2,1)S(1)} %collective-permute-done.5.got_one, f32[16,1024]{1,0:T(8,128)S(1)} %get-tuple-element.45.total_two, bf16[16,1024]{1,0:T(8,128)(2,1)S(1)} %collective-permute-done.7.got_two), custom_call_target="tpu_custom_call" | custom-call | tf_op jit(solution)/shard_map/finish/pallas_call | solution.py:254
  (2 shorter events, 0.0 us)
Async XLA Ops:
  3.0 7.5 %collective-permute-start = (f32[64,64]{1,0:T(8,128)S(1)}, f32[64,64]{1,0:T(8,128)S(1)}, u32[]{:S(2)}, u32[]{:S(2)}) collective-permute-start(f32[64,64]{1,0:T(8,128)S(1)} %get-tuple-element.27), channel_id=1, source_target_pairs={{0,0},{1,4},{2,8},{3,12},{4,1},{5,5},{6,9},{7,13},{8,2},{9,6},{10,... | collective-permute-start | bytes 49160 | tf_op jit(solution)/shard_map/ppermute | solution.py:273
  10.4 14.8 %copy-start = (bf16[1,64,3072]{2,1,0:T(8,128)(2,1)S(1)}, bf16[1,64,3072]{2,1,0:T(8,128)(2,1)}, u32[]{:S(2)}) copy-start(bf16[1,64,3072]{2,1,0:T(8,128)(2,1)} %param.10) | copy-start | bytes 1179652
  10.5 14.8 %copy-start.2 = (s32[64]{0:T(128)S(1)}, s32[64]{0:T(128)}, u32[]{:S(2)}) copy-start(s32[64]{0:T(128)} %param.7) | copy-start | bytes 772
  10.5 14.7 %collective-permute-start.3 = (f32[64,64]{1,0:T(8,128)S(1)}, f32[64,64]{1,0:T(8,128)S(1)}, u32[]{:S(2)}, u32[]{:S(2)}) collective-permute-start(f32[64,64]{1,0:T(8,128)S(1)} %collective-permute-done.low_a), channel_id=1, source_target_pairs={{0,1},{1,0},{2,3},{3,2},{4,5},{5,4},{6,7},{7,6},{8,9},{9,8},{10,11... | collective-permute-start | bytes 49160 | tf_op jit(solution)/shard_map/ppermute | solution.py:277
  14.9 10.3 %collective-permute-start.2 = (f32[64,64]{1,0:T(8,128)S(1)}, f32[64,64]{1,0:T(8,128)S(1)}, u32[]{:S(2)}, u32[]{:S(2)}) collective-permute-start(f32[64,64]{1,0:T(8,128)S(1)} %collective-permute-done.low_a), channel_id=1, source_target_pairs={{0,3},{1,2},{2,1},{3,0},{4,7},{5,6},{6,5},{7,4},{8,11},{9,10},{10,... | collective-permute-start | bytes 49160 | tf_op jit(solution)/shard_map/ppermute | solution.py:277
  18.1 7.1 %collective-permute-start.1 = (f32[64,64]{1,0:T(8,128)S(1)}, f32[64,64]{1,0:T(8,128)S(1)}, u32[]{:S(2)}, u32[]{:S(2)}) collective-permute-start(f32[64,64]{1,0:T(8,128)S(1)} %collective-permute-done.low_a), channel_id=1, source_target_pairs={{0,2},{1,3},{2,0},{3,1},{4,6},{5,7},{6,4},{7,5},{8,10},{9,11},{10,... | collective-permute-start | bytes 49160 | tf_op jit(solution)/shard_map/ppermute | solution.py:277
  25.6 5.5 %collective-permute-start.4 = (bf16[32,2048]{1,0:T(8,128)(2,1)S(1)}, bf16[32,2048]{1,0:T(8,128)(2,1)S(1)}, u32[]{:S(2)}, u32[]{:S(2)}) collective-permute-start(bf16[32,2048]{1,0:T(8,128)(2,1)S(1)} %get-tuple-element.34), channel_id=1, source_target_pairs={{0,4},{4,0},{8,12},{12,8},{1,5},{5,1},{9,13},{13,9},{2,6},{6,2},{1... | collective-permute-start | bytes 393224 | tf_op jit(solution)/shard_map/ppermute | solution.py:265
  31.2 14.1 %copy-start.1 = (bf16[16,3072]{1,0:T(8,128)(2,1)S(1)}, bf16[16,3072]{1,0:T(8,128)(2,1)}, u32[]{:S(2)}) copy-start(bf16[16,3072]{1,0:T(8,128)(2,1)} %residual.1) | copy-start | bytes 294916
  36.0 4.4 %collective-permute-start.6 = (bf16[32,1024]{1,0:T(8,128)(2,1)S(1)}, bf16[32,1024]{1,0:T(8,128)(2,1)S(1)}, u32[]{:S(2)}, u32[]{:S(2)}) collective-permute-start(bf16[32,1024]{1,0:T(8,128)(2,1)S(1)} %get-tuple-element.44), channel_id=1, source_target_pairs={{0,4},{4,0},{8,12},{12,8},{1,5},{5,1},{9,13},{13,9},{2,6},{6,2},{1... | collective-permute-start | bytes 196616 | tf_op jit(solution)/shard_map/ppermute | solution.py:265
  37.3 6.6 %collective-permute-start.5 = (bf16[16,2048]{1,0:T(8,128)(2,1)S(1)}, bf16[16,2048]{1,0:T(8,128)(2,1)S(1)}, u32[]{:S(2)}, u32[]{:S(2)}) collective-permute-start(bf16[16,2048]{1,0:T(8,128)(2,1)S(1)} %get-tuple-element.39), channel_id=1, source_target_pairs={{0,8},{4,12},{8,0},{12,4},{1,9},{5,13},{9,1},{13,5},{2,10},{6,14},... | collective-permute-start | bytes 196616 | tf_op jit(solution)/shard_map/ppermute | solution.py:265
  40.4 4.9 %collective-permute-start.7 = (bf16[16,1024]{1,0:T(8,128)(2,1)S(1)}, bf16[16,1024]{1,0:T(8,128)(2,1)S(1)}, u32[]{:S(2)}, u32[]{:S(2)}) collective-permute-start(bf16[16,1024]{1,0:T(8,128)(2,1)S(1)} %get-tuple-element.46), channel_id=1, source_target_pairs={{0,8},{4,12},{8,0},{12,4},{1,9},{5,13},{9,1},{13,5},{2,10},{6,14},... | collective-permute-start | bytes 98312 | tf_op jit(solution)/shard_map/ppermute | solution.py:265

commit v5 on v3

--- a/solution.py
+++ b/solution.py
@@ -7,7 +7,7 @@
 from jax.experimental.pallas import tpu as pltpu
 from jax.sharding import PartitionSpec as P
 
-WIDTHS = (1024, 1280, 768)
+WIDTHS = (1280, 1280, 512)
 DEPTH = 768
 PS = ("page", "sub")
 VMEM = pl.BlockSpec(memory_space=pltpu.VMEM)
@@ -43,9 +43,10 @@
     hidden,
     rank_down,
     weight,
-    low,
+    packed,
     base,
     hidden_here,
+    low,
     down_here,
     held,
     got,
@@ -87,6 +88,11 @@
             preferred_element_type=jnp.float32,
         )
 
+    half = low.shape[0] // 2
+    block = jnp.concatenate([low[:half, :], low[half:, :]], axis=1)
+    for to in range(packed.shape[0]):
+        packed[to] = block
+
     @pl.loop(0, steps)
     def _(k):
         copy(k).wait()
@@ -102,13 +108,14 @@
     return pl.pallas_call(
         functools.partial(first_kernel, start, width),
         out_shape=(
-            jax.ShapeDtypeStruct((rows, rank), jnp.float32),
+            jax.ShapeDtypeStruct((16, rows // 2, 2 * rank), jnp.float32),
             jax.ShapeDtypeStruct((rows, width), jnp.float32),
             jax.ShapeDtypeStruct(hidden.shape, hidden.dtype),
         ),
         in_specs=[HBM] * 3,
         out_specs=(VMEM, VMEM, VMEM),
         scratch_shapes=[
+            pltpu.VMEM((rows, rank), jnp.float32),
             pltpu.VMEM(rank_down.shape, rank_down.dtype),
             pltpu.VMEM((depth, width), weight.dtype),
             pltpu.SemaphoreType.DMA((2, steps)),
@@ -178,9 +185,15 @@
     return jnp.dot(low.astype(jnp.bfloat16), up, preferred_element_type=jnp.float32)
 
 
-def correct_kernel(ids, low_a, low_b, low_c, low_d, up, base_one, base_two, low, sent, kept, total):
-    held = column_of(ids[...]) == lax.axis_index("tp").astype(jnp.float32)
-    low[...] = jnp.where(held, (low_a[...] + low_b[...]) + (low_c[...] + low_d[...]), 0.0)
+def correct_kernel(ids, packed, up, base_one, base_two, low, sent, kept, total):
+    tp = lax.axis_index("tp")
+    summed = packed[tp]
+    for source in range(1, 4):
+        summed = summed + packed[4 * source + tp]
+    rank = low.shape[1]
+    summed = jnp.concatenate([summed[:, :rank], summed[:, rank:]], axis=0)
+    held = column_of(ids[...]) == tp.astype(jnp.float32)
+    low[...] = jnp.where(held, summed, 0.0)
     start = 0
     for base in (base_one, base_two):
         width = base.shape[1]
@@ -190,8 +203,9 @@
     split_rows(total, slice(0, start), sent, kept)
 
 
-def correct_phase(ids, lows, up, base_one, base_two):
-    rows, rank = lows[0].shape
+def correct_phase(ids, packed, up, base_one, base_two):
+    rows = base_one.shape[0]
+    rank = up.shape[0]
     width = base_one.shape[1] + base_two.shape[1]
     return pl.pallas_call(
         correct_kernel,
@@ -200,33 +214,27 @@
             jax.ShapeDtypeStruct((rows // 2, width), jnp.bfloat16),
             jax.ShapeDtypeStruct((rows // 2, width), jnp.float32),
         ),
-        in_specs=[VMEM] * 8,
+        in_specs=[VMEM] * 5,
         out_specs=(VMEM,) * 3,
         scratch_shapes=[pltpu.VMEM((rows, width), jnp.float32)],
         compiler_params=pltpu.CompilerParams(vmem_limit_bytes=8 << 20),
         name="adapter_term",
-    )(ids, *lows, up, base_one, base_two)
-
-
-def last_kernel(start, hidden, weight, low, up, sent, kept, total, held, arrived):
+    )(ids, packed, up, base_one, base_two)
+
+
+def last_kernel(start, hidden, weight, low, up, total, held, arrived):
     stream_dot(hidden, weight, total, held, arrived, start)
-    width = total.shape[1]
-    total[...] += adapter_term(low[...], up[:, start : start + width])
-    split_rows(total, slice(0, width), sent, kept)
+    total[...] += adapter_term(low[...], up[:, start : start + total.shape[1]])
 
 
 def last_phase(hidden, weight, low, up, start, width):
     rows, depth = hidden.shape
     return pl.pallas_call(
         functools.partial(last_kernel, start),
-        out_shape=(
-            jax.ShapeDtypeStruct((rows // 2, width), jnp.bfloat16),
-            jax.ShapeDtypeStruct((rows // 2, width), jnp.float32),
-        ),
+        out_shape=jax.ShapeDtypeStruct((rows, width), jnp.float32),
         in_specs=[VMEM, HBM, VMEM, VMEM],
-        out_specs=(VMEM, VMEM),
+        out_specs=VMEM,
         scratch_shapes=[
-            pltpu.VMEM((rows, width), jnp.float32),
             pltpu.VMEM((depth, width), weight.dtype),
             pltpu.SemaphoreType.DMA((depth // DEPTH,)),
         ],
@@ -238,49 +246,64 @@
     )(hidden, weight, low, up)
 
 
-def pair_kernel(kept, got, sent, total):
-    block = kept.shape[0] // 2
-    high = lax.div(lax.axis_index("tp"), 2)
-    here = pl.ds(pl.multiple_of(high * block, block), block)
-    there = pl.ds(pl.multiple_of((1 - high) * block, block), block)
-    sent[...] = (kept[there, :] + got[there, :].astype(jnp.float32)).astype(sent.dtype)
-    total[...] = kept[here, :] + got[here, :].astype(jnp.float32)
-
-
-def pair_phase(kept, got):
-    rows, width = kept.shape
-    return pl.pallas_call(
-        pair_kernel,
+def join_kernel(kept, got, last, residual, to_one, to_two, to_three, total):
+    block = residual.shape[0]
+    before = kept.shape[1]
+    tp = lax.axis_index("tp")
+    high, low = lax.div(tp, 2), lax.rem(tp, 2)
+
+    def rows(index):
+        return pl.ds(pl.multiple_of(index * block, block), block)
+
+    def pair(half):
+        return kept[rows(half), :] + got[rows(half), :].astype(jnp.float32)
+
+    to_two[:, :before] = pair(1 - high).astype(to_two.dtype)
+    to_two[:, before:] = last[rows(2 * (1 - high) + low), :].astype(to_two.dtype)
+    to_one[...] = last[rows(2 * high + 1 - low), :].astype(to_one.dtype)
+    to_three[...] = last[rows(3 - tp), :].astype(to_three.dtype)
+    total[:, :before] = residual[:, :before].astype(jnp.float32) + pair(high)
+    total[:, before:] = residual[:, before:].astype(jnp.float32) + last[rows(tp), :]
+
+
+def join_phase(kept, got, last, residual):
+    block, width = residual.shape
+    return pl.pallas_call(
+        join_kernel,
         out_shape=(
-            jax.ShapeDtypeStruct((rows // 2, width), jnp.bfloat16),
-            jax.ShapeDtypeStruct((rows // 2, width), jnp.float32),
-        ),
-        in_specs=[VMEM] * 2,
-        out_specs=(VMEM,) * 2,
+            jax.ShapeDtypeStruct((block, last.shape[1]), jnp.bfloat16),
+            jax.ShapeDtypeStruct((block, width), jnp.bfloat16),
+            jax.ShapeDtypeStruct((block, last.shape[1]), jnp.bfloat16),
+            jax.ShapeDtypeStruct((block, width), jnp.float32),
+        ),
+        in_specs=[VMEM] * 4,
+        out_specs=(VMEM,) * 4,
         compiler_params=pltpu.CompilerParams(vmem_limit_bytes=8 << 20),
-        name="pair_sum",
-    )(kept, got)
-
-
-def finish_kernel(residual, total_one, got_one, total_two, got_two, mixed):
-    start = 0
-    for total, got in ((total_one, got_one), (total_two, got_two)):
-        at = slice(start, start + total.shape[1])
-        mixed[:, at] = (
-            residual[:, at].astype(jnp.float32) + total[...] + got[...].astype(jnp.float32)
-        ).astype(mixed.dtype)
-        start = at.stop
-
-
-def finish_phase(residual, *terms):
+        name="join",
+    )(kept, got, last, residual)
+
+
+def finish_kernel(total, one, two, three, mixed):
+    before = total.shape[1] - one.shape[1]
+    mixed[:, :before] = (total[:, :before] + two[:, :before].astype(jnp.float32)).astype(
+        mixed.dtype
+    )
+    mixed[:, before:] = (
+        total[:, before:]
+        + two[:, before:].astype(jnp.float32)
+        + (one[...].astype(jnp.float32) + three[...].astype(jnp.float32))
+    ).astype(mixed.dtype)
+
+
+def finish_phase(total, one, two, three):
     return pl.pallas_call(
         finish_kernel,
-        out_shape=jax.ShapeDtypeStruct(residual.shape, residual.dtype),
-        in_specs=[VMEM] * 5,
+        out_shape=jax.ShapeDtypeStruct(total.shape, two.dtype),
+        in_specs=[VMEM] * 4,
         out_specs=VMEM,
         compiler_params=pltpu.CompilerParams(vmem_limit_bytes=8 << 20),
         name="finish",
-    )(residual, *terms)
+    )(total, one, two, three)
 
 
 def swap(value, bit):
@@ -290,23 +313,16 @@
 def four_by_four(hidden_units, adapter_ids, weight, rank_down, rank_up, residual):
     up = rank_up[0]
     one, two, three = WIDTHS
-    low, base_one, hidden = first_phase(
+    packed, base_one, hidden = first_phase(
         hidden_units, jnp.swapaxes(rank_down, 1, 2)[0], weight, 0, one
     )
-    lows = []
-    for j in range(4):
-        pairs = [(t * 4 + a, a * 4 + (t + j) % 4) for t in range(4) for a in range(4)]
-        lows.append(lax.ppermute(low, ("tp",) + PS, pairs))
+    packed = lax.all_to_all(packed, ("tp",) + PS, split_axis=0, concat_axis=0, tiled=True)
     base_two = base_phase(hidden, weight, one, two)
-    low, sent, kept = correct_phase(adapter_ids[None], lows, up, base_one, base_two)
+    low, sent, kept = correct_phase(adapter_ids[None], packed, up, base_one, base_two)
     got = swap(sent, 1)
-    sent_last, kept_last = last_phase(hidden, weight, low, up, one + two, three)
-    got_last = swap(sent_last, 1)
-    sent, total = pair_phase(kept, got)
-    got = swap(sent, 2)
-    sent_last, total_last = pair_phase(kept_last, got_last)
-    got_last = swap(sent_last, 2)
-    return finish_phase(residual, total, got, total_last, got_last)
+    last = last_phase(hidden, weight, low, up, one + two, three)
+    to_one, to_two, to_three, total = join_phase(kept, got, last, residual)
+    return finish_phase(total, swap(to_one, 1), swap(to_two, 2), swap(to_three, 3))
 
 
 def any_size(hidden_units, adapter_ids, down_projection_weight, rank_down, rank_up, residual):

time: 41.5 us -> 42.1 us (1.014)
  waiting for transfers between devices: 3.15 us -> 7.41 us
  starting transfers between devices: 16.1 us -> 11.9 us
  Pallas kernels: 21.9 us -> 22.4 us
    all_to_all x0 -> x1, starting transfers between devices: none -> 7.37 us  [four_by_four(): lax.all_to_all(packed, ('tp',) + PS, split_axis=0, concat_axis=0, tiled=T...]
    ppermute x4 -> x0, starting transfers between devices: 6.34 us -> none  [four_by_four(): lows.append(lax.ppermute(low, ('tp',) + PS, pairs))]
    ppermute x4, starting transfers between devices: 9.76 us -> 4.56 us  [swap(): lax.ppermute(value, 'tp', [(i, i ^ bit) for i in range(lax.axis_size('tp'...]
    ppermute x4, waiting for transfers between devices: 3.14 us -> 5.31 us  [swap(): lax.ppermute(value, 'tp', [(i, i ^ bit) for i in range(lax.axis_size('tp'...]
    all_to_all x0 -> x1, waiting for transfers between devices: none -> 2.1 us  [four_by_four(): lax.all_to_all(packed, ('tp',) + PS, split_axis=0, concat_axis=0, tiled=T...]
    pallas_call x1, Pallas kernels: 7.5 us -> 9.09 us  [first_phase(): pl.pallas_call(functools.partial(first_kernel, start, width), out_shape=(...]
    pallas_call x4 -> x3, Pallas kernels: 6.15 us -> 4.99 us  [the longest x1 4.27 us: last_phase(): pl.pallas_call(functools.partial(last_kernel, start), out_shape=jax.Shape...]
  transfers between devices with their start and end apart: 8 -> 5, of which waited for: 2 -> 4; matrix products, arithmetic and copies ran while one was open for 0% -> 0% of each run, Pallas kernels for 32% -> 29%
where the time goes in v5:
time: 42.1 us; the launch traced here: 41.8 us
  Pallas kernels  22.4 us (53%)
  starting transfers between devices  11.9 us (28%)
  waiting for transfers between devices  7.41 us (18%)
    pallas_call x1, Pallas kernels, first_phase(): pl.pallas_call(functools.partial(first_kernel, start, width), out_shape=(...  9.09 us
    pallas_call x1, Pallas kernels, base_phase(): pl.pallas_call(functools.partial(base_kernel, start), out_shape=jax.Shape...  7.92 us
    all_to_all x1, starting transfers between devices, four_by_four(): lax.all_to_all(packed, ('tp',) + PS, split_axis=0, concat_axis=0, tiled=T...  7.37 us
    ppermute x4, waiting for transfers between devices, swap(): lax.ppermute(value, 'tp', [(i, i ^ bit) for i in range(lax.axis_size('tp'...  5.31 us
    ppermute x4, starting transfers between devices, swap(): lax.ppermute(value, 'tp', [(i, i ^ bit) for i in range(lax.axis_size('tp'...  4.56 us
    pallas_call x1, Pallas kernels, last_phase(): pl.pallas_call(functools.partial(last_kernel, start), out_shape=jax.Shape...  4.27 us
    all_to_all x1, waiting for transfers between devices, four_by_four(): lax.all_to_all(packed, ('tp',) + PS, split_axis=0, concat_axis=0, tiled=T...  2.1 us
  transfers between devices with their start and end apart: 5, of which 4 were waited for; matrix products, arithmetic and copies ran while one was open for 0% of the time, Pallas kernels for 29%

profile of v5, /device:TPU:0, one launch (start us, length us, event | category | flops | bytes accessed | tf_op | source)
XLA Modules:
  0.0 41.8 jit_solution(3084468776023375112)
XLA Ops:
  0.0 9.1 %low_rank_and_base.1 = (f32[16,32,128]{2,1,0:T(8,128)}, f32[64,1280]{1,0:T(8,128)S(1)}, bf16[64,8448]{1,0:T(8,128)(2,1)S(1)}) custom-call(bf16[64,8448]{1,0:T(8,128)(2,1)} %hidden.1, bf16[64,8448]{1,0:T(8,128)(2,1)} %bitcast.8, bf16[8448,3072]{1,0:T(8,128)(2,1)} %weight.5), custom_call_target="tpu_custom_call" | custom-call | flops 1453326336 | bytes 23789568 | tf_op jit(solution)/shard_map/low_rank_and_base/pallas_call | solution.py:108
  9.1 7.4 %all-to-all-start = ((f32[16,32,128]{2,1,0:T(8,128)}), f32[16,32,128]{2,1,0:T(8,128)S(1)}, u32[]{:S(2)}, u32[]{:S(2)}) async-start(f32[16,32,128]{2,1,0:T(8,128)} %get-tuple-element.15), calls=%async_computation | async-start | bytes 524288 | tf_op jit(solution)/shard_map/all_to_all | solution.py:319
  16.5 0.0 copy-start
  16.5 0.0 copy-start.2
  16.5 7.9 %base.1.base_two = f32[64,1280]{1,0:T(8,128)S(1)} custom-call(bf16[64,8448]{1,0:T(8,128)(2,1)S(1)} %get-tuple-element.17.hidden, bf16[8448,3072]{1,0:T(8,128)(2,1)} %weight.5), custom_call_target="tpu_custom_call" | custom-call | flops 1384120320 | bytes 21626880 | tf_op jit(solution)/shard_map/base/pallas_call | solution.py:156
  24.4 2.1 %all-to-all-done.packed = f32[16,32,128]{2,1,0:T(8,128)S(1)} async-done(((f32[16,32,128]{2,1,0:T(8,128)}), f32[16,32,128]{2,1,0:T(8,128)S(1)}, u32[]{:S(2)}, u32[]{:S(2)}) %all-to-all-start) | async-done | bytes 262176 | tf_op jit(solution)/shard_map/all_to_all | solution.py:319
  26.5 0.0 copy-done
  26.5 0.0 copy-done.2
  26.5 0.4 adapter_term.1
  26.9 0.1 collective-permute-start
  27.0 0.0 copy-start.1
  27.0 4.3 %last_base.1.last = f32[64,512]{1,0:T(8,128)S(1)} custom-call(bf16[64,8448]{1,0:T(8,128)(2,1)S(1)} %get-tuple-element.17.hidden, bf16[8448,3072]{1,0:T(8,128)(2,1)} %weight.5, f32[64,64]{1,0:T(8,128)S(1)} %get-tuple-element.20.low, bf16[64,3072]{1,0:T(8,128)(2,1)S(1)} %bitcast.6), custom_call_target="tpu_custom_call" | custom-call | flops 553648128 | bytes 8650752 | tf_op jit(solution)/shard_map/last_base/pallas_call | solution.py:232
  31.3 1.6 %collective-permute-done.got = bf16[32,2560]{1,0:T(8,128)(2,1)S(1)} collective-permute-done((bf16[32,2560]{1,0:T(8,128)(2,1)S(1)}, bf16[32,2560]{1,0:T(8,128)(2,1)S(1)}, u32[]{:S(2)}, u32[]{:S(2)}) %collective-permute-start) | collective-permute-done | bytes 163872 | tf_op jit(solution)/shard_map/ppermute | solution.py:310
  32.9 0.0 copy-done.1
  32.9 0.1 join.1
  33.0 1.1 %collective-permute-start.2 = (bf16[16,3072]{1,0:T(8,128)(2,1)S(1)}, bf16[16,3072]{1,0:T(8,128)(2,1)S(1)}, u32[]{:S(2)}, u32[]{:S(2)}) collective-permute-start(bf16[16,3072]{1,0:T(8,128)(2,1)S(1)} %get-tuple-element.23), channel_id=1, source_target_pairs={{0,8},{4,12},{8,0},{12,4},{1,9},{5,13},{9,1},{13,5},{2,10},{6,14},... | collective-permute-start | bytes 294920 | tf_op jit(solution)/shard_map/ppermute | solution.py:310
  34.1 1.5 %collective-permute-start.1 = (bf16[16,512]{1,0:T(8,128)(2,1)S(1)}, bf16[16,512]{1,0:T(8,128)(2,1)S(1)}, u32[]{:S(2)}, u32[]{:S(2)}) collective-permute-start(bf16[16,512]{1,0:T(8,128)(2,1)S(1)} %get-tuple-element.22), channel_id=1, source_target_pairs={{0,4},{4,0},{8,12},{12,8},{1,5},{5,1},{9,13},{13,9},{2,6},{6,2},{1... | collective-permute-start | bytes 49160 | tf_op jit(solution)/shard_map/ppermute | solution.py:310
  35.6 1.9 %collective-permute-start.3 = (bf16[16,512]{1,0:T(8,128)(2,1)S(1)}, bf16[16,512]{1,0:T(8,128)(2,1)S(1)}, u32[]{:S(2)}, u32[]{:S(2)}) collective-permute-start(bf16[16,512]{1,0:T(8,128)(2,1)S(1)} %get-tuple-element.24), channel_id=1, source_target_pairs={{0,12},{4,8},{8,4},{12,0},{1,13},{5,9},{9,5},{13,1},{2,14},{6,10},... | collective-permute-start | bytes 49160 | tf_op jit(solution)/shard_map/ppermute | solution.py:310
  37.5 0.4 %collective-permute-done.1.one = bf16[16,512]{1,0:T(8,128)(2,1)S(1)} collective-permute-done((bf16[16,512]{1,0:T(8,128)(2,1)S(1)}, bf16[16,512]{1,0:T(8,128)(2,1)S(1)}, u32[]{:S(2)}, u32[]{:S(2)}) %collective-permute-start.1) | collective-permute-done | bytes 16416 | tf_op jit(solution)/shard_map/ppermute | solution.py:310
  37.9 3.2 %collective-permute-done.3.three = bf16[16,512]{1,0:T(8,128)(2,1)S(1)} collective-permute-done((bf16[16,512]{1,0:T(8,128)(2,1)S(1)}, bf16[16,512]{1,0:T(8,128)(2,1)S(1)}, u32[]{:S(2)}, u32[]{:S(2)}) %collective-permute-start.3) | collective-permute-done | bytes 16416 | tf_op jit(solution)/shard_map/ppermute | solution.py:310
  41.1 0.0 collective-permute-done.2.two
  41.1 0.7 %finish.1 = bf16[16,3072]{1,0:T(8,128)(2,1)} custom-call(f32[16,3072]{1,0:T(8,128)S(1)} %get-tuple-element.21.total, bf16[16,512]{1,0:T(8,128)(2,1)S(1)} %collective-permute-done.1.one, bf16[16,3072]{1,0:T(8,128)(2,1)S(1)} %collective-permute-done.2.two, bf16[16,512]{1,0:T(8,128)(2,1)S(1)} %collective-permute-done.3.three), custom_call_target="tpu_custom_call" | custom-call | tf_op jit(solution)/shard_map/finish/pallas_call | solution.py:299
Async XLA Ops:
  9.1 17.4 %all-to-all-start = ((f32[16,32,128]{2,1,0:T(8,128)}), f32[16,32,128]{2,1,0:T(8,128)S(1)}, u32[]{:S(2)}, u32[]{:S(2)}) async-start(f32[16,32,128]{2,1,0:T(8,128)} %get-tuple-element.15), calls=%async_computation | async-start | bytes 524288 | tf_op jit(solution)/shard_map/all_to_all | solution.py:319
  16.5 10.0 %copy-start = (bf16[1,64,3072]{2,1,0:T(8,128)(2,1)S(1)}, bf16[1,64,3072]{2,1,0:T(8,128)(2,1)}, u32[]{:S(2)}) copy-start(bf16[1,64,3072]{2,1,0:T(8,128)(2,1)} %param.10) | copy-start | bytes 1179652
  16.5 10.0 %copy-start.2 = (s32[64]{0:T(128)S(1)}, s32[64]{0:T(128)}, u32[]{:S(2)}) copy-start(s32[64]{0:T(128)} %param.7) | copy-start | bytes 772
  26.9 6.0 %collective-permute-start = (bf16[32,2560]{1,0:T(8,128)(2,1)S(1)}, bf16[32,2560]{1,0:T(8,128)(2,1)S(1)}, u32[]{:S(2)}, u32[]{:S(2)}) collective-permute-start(bf16[32,2560]{1,0:T(8,128)(2,1)S(1)} %get-tuple-element.19), channel_id=1, source_target_pairs={{0,4},{4,0},{8,12},{12,8},{1,5},{5,1},{9,13},{13,9},{2,6},{6,2},{1... | collective-permute-start | bytes 491528 | tf_op jit(solution)/shard_map/ppermute | solution.py:310
  27.0 5.9 %copy-start.1 = (bf16[16,3072]{1,0:T(8,128)(2,1)S(1)}, bf16[16,3072]{1,0:T(8,128)(2,1)}, u32[]{:S(2)}) copy-start(bf16[16,3072]{1,0:T(8,128)(2,1)} %residual.1) | copy-start | bytes 294916
  33.0 8.1 %collective-permute-start.2 = (bf16[16,3072]{1,0:T(8,128)(2,1)S(1)}, bf16[16,3072]{1,0:T(8,128)(2,1)S(1)}, u32[]{:S(2)}, u32[]{:S(2)}) collective-permute-start(bf16[16,3072]{1,0:T(8,128)(2,1)S(1)} %get-tuple-element.23), channel_id=1, source_target_pairs={{0,8},{4,12},{8,0},{12,4},{1,9},{5,13},{9,1},{13,5},{2,10},{6,14},... | collective-permute-start | bytes 294920 | tf_op jit(solution)/shard_map/ppermute | solution.py:310
  34.1 3.8 %collective-permute-start.1 = (bf16[16,512]{1,0:T(8,128)(2,1)S(1)}, bf16[16,512]{1,0:T(8,128)(2,1)S(1)}, u32[]{:S(2)}, u32[]{:S(2)}) collective-permute-start(bf16[16,512]{1,0:T(8,128)(2,1)S(1)} %get-tuple-element.22), channel_id=1, source_target_pairs={{0,4},{4,0},{8,12},{12,8},{1,5},{5,1},{9,13},{13,9},{2,6},{6,2},{1... | collective-permute-start | bytes 49160 | tf_op jit(solution)/shard_map/ppermute | solution.py:310
  35.6 5.5 %collective-permute-start.3 = (bf16[16,512]{1,0:T(8,128)(2,1)S(1)}, bf16[16,512]{1,0:T(8,128)(2,1)S(1)}, u32[]{:S(2)}, u32[]{:S(2)}) collective-permute-start(bf16[16,512]{1,0:T(8,128)(2,1)S(1)} %get-tuple-element.24), channel_id=1, source_target_pairs={{0,12},{4,8},{8,4},{12,0},{1,13},{5,9},{9,5},{13,1},{2,14},{6,10},... | collective-permute-start | bytes 49160 | tf_op jit(solution)/shard_map/ppermute | solution.py:310

commit v6 on v0

v6 whole, which is shorter than its diff:
```python
import functools

import jax
import jax.numpy as jnp
from jax import lax
from jax.experimental import pallas as pl
from jax.experimental.pallas import tpu as pltpu
from jax.sharding import PartitionSpec as P

PART = 256
GROUP = 3
SLOTS = 6
TILE = 512
PS = ("page", "sub")
VMEM = pl.BlockSpec(memory_space=pltpu.VMEM)
HBM = pl.BlockSpec(memory_space=pltpu.HBM)


def column_of(ids_row):
    rows = ids_row.shape[1]
    down = lax.broadcasted_iota(jnp.int32, (rows, rows), 0)
    across = lax.broadcasted_iota(jnp.int32, (rows, rows), 1)
    spread = jnp.broadcast_to(ids_row, (rows, rows))
    return jnp.sum(
        jnp.where(down == across, spread.astype(jnp.float32), 0.0), axis=1, keepdims=True
    )


def stream_kernel(
    ids, hidden, rank_down, weight, low, sent, kept, ids_here, hidden_here, down_here, total, held, got, arrived
):
    groups = weight.shape[0] // (PART * GROUP)
    width = weight.shape[1]
    deep = PART * GROUP

    def part_copy(group, part):
        rows = pl.ds(pl.multiple_of(group * deep + part * PART, PART), PART)
        slot = lax.rem(group, SLOTS)
        there = pl.ds(pl.multiple_of(slot * deep + part * PART, PART), PART)
        return pltpu.make_async_copy(
            weight.at[rows], held.at[there], arrived.at[slot * GROUP + part]
        )

    first = [
        pltpu.make_async_copy(hidden, hidden_here, got.at[0]),
        pltpu.make_async_copy(rank_down, down_here, got.at[1]),
        pltpu.make_async_copy(ids, ids_here, got.at[2]),
    ]
    for copy in first:
        copy.start()

    @pl.loop(0, SLOTS - 1)
    def _(group):
        for part in range(GROUP):
            part_copy(group, part).start()

    total[...] = jnp.zeros_like(total)
    for copy in first:
        copy.wait()
    owned = lax.axis_index("page") * lax.axis_size("sub") + lax.axis_index("sub")
    mine = column_of(ids_here[...]) == owned.astype(jnp.float32)
    product = lax.dot_general(
        hidden_here[...],
        down_here[...],
        (((1,), (1,)), ((), ())),
        preferred_element_type=jnp.float32,
    )
    low[...] = jnp.where(mine, product, 0.0)

    def add(group, part, depth):
        at = pl.ds(pl.multiple_of(group * deep + part * PART, PART), depth)
        slot = pl.ds(pl.multiple_of(lax.rem(group, SLOTS) * deep + part * PART, PART), depth)
        for start in range(0, width, TILE):
            columns = slice(start, start + TILE)
            total[:, columns] += jnp.dot(
                hidden_here[:, at], held[slot, columns], preferred_element_type=jnp.float32
            )

    @pl.loop(0, groups - 1)
    def _(group):
        @pl.when(group + SLOTS - 1 < groups)
        def _():
            for part in range(GROUP):
                part_copy(group + SLOTS - 1, part).start()

        for part in range(GROUP):
            part_copy(group, part).wait()
        add(group, 0, deep)

    for part in range(GROUP):
        part_copy(groups - 1, part).wait()
        add(groups - 1, part, PART)
    split_rows(total, slice(0, width), sent, kept)


def stream_phase(ids, hidden, rank_down, weight):
    rows, depth = hidden.shape
    rank = rank_down.shape[0]
    width = weight.shape[1]
    return pl.pallas_call(
        stream_kernel,
        out_shape=(
            jax.ShapeDtypeStruct((rows, rank), jnp.float32),
            jax.ShapeDtypeStruct((rows // 2, width), jnp.bfloat16),
            jax.ShapeDtypeStruct((rows // 2, width), jnp.float32),
        ),
        in_specs=[HBM] * 4,
        out_specs=(VMEM,) * 3,
        scratch_shapes=[
            pltpu.VMEM(ids.shape, ids.dtype),
            pltpu.VMEM(hidden.shape, hidden.dtype),
            pltpu.VMEM(rank_down.shape, rank_down.dtype),
            pltpu.VMEM((rows, width), jnp.float32),
            pltpu.VMEM((SLOTS * GROUP * PART, width), weight.dtype),
            pltpu.SemaphoreType.DMA((3,)),
            pltpu.SemaphoreType.DMA((SLOTS * GROUP,)),
        ],
        compiler_params=pltpu.CompilerParams(vmem_limit_bytes=53 << 20),
        cost_estimate=pl.CostEstimate(
            flops=2 * rows * depth * (width + rank),
            bytes_accessed=2 * depth * (width + rank + rows),
            transcendentals=0,
        ),
        name="low_rank_and_base",
    )(ids, hidden, rank_down, weight)


def split_rows(total, at, sent, kept):
    block = total.shape[0] // 4
    bit = lax.rem(lax.axis_index("tp"), 2)
    for half in range(2):
        rows = pl.ds(half * block, block)
        there = pl.ds(pl.multiple_of((2 * half + 1 - bit) * block, block), block)
        here = pl.ds(pl.multiple_of((2 * half + bit) * block, block), block)
        sent[rows, at] = total[there, :].astype(sent.dtype)
        kept[rows, at] = total[here, :]


def join_kernel(ids, low, up_here, up_there, kept, got, residual, sent, total, joined):
    block = residual.shape[0]
    tp = lax.axis_index("tp")
    high, bit = lax.div(tp, 2), lax.rem(tp, 2)
    adapter = column_of(ids[...])
    here = jnp.where(adapter == tp.astype(jnp.float32), low[...], 0.0)
    there = jnp.where(adapter == (tp + 1 - 2 * bit).astype(jnp.float32), low[...], 0.0)
    halves = []
    for half in range(2):
        even = slice(2 * half * block, (2 * half + 1) * block)
        odd = slice((2 * half + 1) * block, (2 * half + 2) * block)
        halves.append([jnp.where(bit == 0, x[even], x[odd]) for x in (here, there)])
    coefficient = [
        jnp.concatenate([halves[0][i], halves[1][i]], axis=0).astype(jnp.bfloat16)
        for i in range(2)
    ]
    width = residual.shape[1]
    for start in range(0, width, TILE):
        at = slice(start, start + TILE)
        joined[:, at] = (
            kept[:, at]
            + got[:, at].astype(jnp.float32)
            + jnp.dot(coefficient[0], up_here[:, at], preferred_element_type=jnp.float32)
            + jnp.dot(coefficient[1], up_there[:, at], preferred_element_type=jnp.float32)
        )
    near = pl.ds(pl.multiple_of(high * block, block), block)
    far = pl.ds(pl.multiple_of((1 - high) * block, block), block)
    sent[...] = joined[far, :].astype(sent.dtype)
    total[...] = joined[near, :] + residual[...].astype(jnp.float32)


def join_phase(ids, low, up_here, up_there, kept, got, residual):
    return pl.pallas_call(
        join_kernel,
        out_shape=(
            jax.ShapeDtypeStruct(residual.shape, jnp.bfloat16),
            jax.ShapeDtypeStruct(residual.shape, jnp.float32),
        ),
        in_specs=[VMEM] * 7,
        out_specs=(VMEM,) * 2,
        scratch_shapes=[pltpu.VMEM(kept.shape, kept.dtype)],
        compiler_params=pltpu.CompilerParams(vmem_limit_bytes=8 << 20),
        name="join",
    )(ids, low, up_here, up_there, kept, got, residual)


def finish_kernel(total, got, mixed):
    mixed[...] = (total[...] + got[...].astype(jnp.float32)).astype(mixed.dtype)


def finish_phase(total, got):
    return pl.pallas_call(
        finish_kernel,
        out_shape=jax.ShapeDtypeStruct(total.shape, got.dtype),
        in_specs=[VMEM] * 2,
        out_specs=VMEM,
        compiler_params=pltpu.CompilerParams(vmem_limit_bytes=8 << 20),
        name="finish",
    )(total, got)


def swap(value, axis, bit=1):
    return lax.ppermute(value, axis, [(i, i ^ bit) for i in range(lax.axis_size(axis))])


def four_by_four(hidden, adapter_ids, weight, rank_down, rank_up, residual):
    ids = adapter_ids[None]
    up = rank_up[0]
    up_there = swap(up, "tp", 1)
    low, sent, kept = stream_phase(ids, hidden, jnp.swapaxes(rank_down, 1, 2)[0], weight)
    got = swap(sent, "tp", 1)
    low = low + swap(low, "sub")
    low = low + swap(low, "page")
    low = low + swap(low, "tp", 1)
    low = low + swap(low, "tp", 2)
    sent, total = join_phase(ids, low, up, up_there, kept, got, residual)
    return finish_phase(total, swap(sent, "tp", 2))


def any_size(hidden_units, adapter_ids, down_projection_weight, rank_down, rank_up, residual):
    owned_count = rank_down.shape[0]
    first_owned = lax.axis_index(PS) * owned_count
    chosen = (
        (adapter_ids - first_owned)[:, None] == jnp.arange(owned_count, dtype=jnp.int32)[None, :]
    ).astype(jnp.float32)
    projected = jnp.einsum(
        "rf,afk->rak", hidden_units, rank_down, preferred_element_type=jnp.float32
    )
    partial_low = jnp.einsum("rak,ra->rk", projected, chosen)
    low_rank = lax.psum(partial_low, ("tp",) + PS).astype(jnp.bfloat16)
    held_count, rank_width, columns = rank_up.shape
    first_held = lax.axis_index("tp") * held_count
    picked = (
        (adapter_ids - first_held)[:, None] == jnp.arange(held_count, dtype=jnp.int32)[None, :]
    ).astype(jnp.bfloat16)
    coefficient = (picked[:, :, None] * low_rank[:, None, :]).reshape(
        -1, held_count * rank_width
    )
    term = jnp.dot(
        hidden_units, down_projection_weight, preferred_element_type=jnp.float32
    ) + jnp.dot(
        coefficient,
        rank_up.reshape(held_count * rank_width, columns),
        preferred_element_type=jnp.float32,
    )
    summed = lax.psum_scatter(
        term.astype(jnp.bfloat16), "tp", scatter_dimension=0, tiled=True
    ).astype(jnp.float32)
    return (residual.astype(jnp.float32) + summed).astype(jnp.bfloat16)


def on_device(hidden_units, adapter_ids, down_projection_weight, rank_down, rank_up, residual):
    sizes = [lax.axis_size(axis) for axis in ("tp",) + PS]
    fits = (
        sizes[0] == 4
        and sizes[1] == 2
        and sizes[2] == 2
        and rank_down.shape[0] == 1
        and rank_up.shape[0] == 1
        and residual.shape == (16, 6 * TILE)
        and hidden_units.shape[1] % (GROUP * PART) == 0
        and hidden_units.shape[1] >= SLOTS * GROUP * PART
    )
    form = four_by_four if fits else any_size
    return form(hidden_units, adapter_ids, down_projection_weight, rank_down, rank_up, residual)


def solution(mesh):
    placed = (
        P("parts", "tp"),
        P("parts"),
        P("tp", ("page", "sub")),
        P(("parts", "page", "sub"), "tp", None),
        P(("parts", "tp"), None, ("page", "sub")),
        P(("parts", "tp"), ("page", "sub")),
    )
    return jax.shard_map(
        on_device,
        mesh=mesh,
        in_specs=placed,
        out_specs=P(("parts", "tp"), ("page", "sub")),
        check_vma=False,
    )
```

time: 121 us -> 42.1 us (0.35)
  blocking collectives: 62.9 us -> 0 us
  matrix products: 23.3 us -> 0 us
  Pallas kernels: 0 us -> 18.5 us
  between operations: 13.4 us -> 0.07 us
  starting transfers between devices: 0.01 us -> 13 us
  waiting for transfers between devices: 18 us -> 9.7 us
  other arithmetic: 2.31 us -> 0.02 us
    psum x1 -> x0, blocking collectives: 62.9 us -> none  [on_device(): low_rank = lax.psum(partial_low, ('tp', 'page', 'sub')).astype(jnp.bfloat16)]
    dot_general x3 -> x0, matrix products: 23.3 us -> none  [the longest x1 20.5 us: on_device(): jnp.dot(hidden_units, down_projection_weight, preferred_element_type=jnp....]
    pallas_call x0 -> x3, Pallas kernels: none -> 18.5 us  [the longest x1 17.5 us: stream_phase(): pl.pallas_call(stream_kernel, out_shape=(jax.ShapeDtypeStruct((rows, rank...]
    reduce_scatter x1 -> x0, waiting for transfers between devices: 18 us -> none  [on_device(): lax.psum_scatter((base_projection_term + jnp.dot(low_rank_coefficient, fl...]
    ppermute x0 -> x7, starting transfers between devices: none -> 13 us  [swap(): lax.ppermute(value, axis, [(i, i ^ bit) for i in range(lax.axis_size(axis...]
    ppermute x0 -> x7, waiting for transfers between devices: none -> 9.7 us  [swap(): lax.ppermute(value, axis, [(i, i ^ bit) for i in range(lax.axis_size(axis...]
    convert_element_type x2 -> x0, other arithmetic: 2.31 us -> none  [the longest x1 1.56 us: on_device(): return (residual.astype(jnp.float32) + summed).astype(jnp.bfloat16)]
  transfers between devices with their start and end apart: 1 -> 7, of which waited for: 1 -> 5; matrix products, arithmetic and copies ran while one was open for 0% -> 0% of each run, Pallas kernels for 0% -> 42%
where the time goes in v6:
time: 42.1 us; the launch traced here: 41.9 us
  Pallas kernels  18.5 us (44%)
  starting transfers between devices  13 us (31%)
  waiting for transfers between devices  9.7 us (23%)
  local copies, waits for them, and re-layouts  0.66 us (2%)
    pallas_call x1, Pallas kernels, stream_phase(): pl.pallas_call(stream_kernel, out_shape=(jax.ShapeDtypeStruct((rows, rank...  17.5 us
    ppermute x7, starting transfers between devices, swap(): lax.ppermute(value, axis, [(i, i ^ bit) for i in range(lax.axis_size(axis...  13 us
    ppermute x7, waiting for transfers between devices, swap(): lax.ppermute(value, axis, [(i, i ^ bit) for i in range(lax.axis_size(axis...  9.7 us
  transfers between devices with their start and end apart: 7, of which 5 were waited for; matrix products, arithmetic and copies ran while one was open for 0% of the time, Pallas kernels for 42%

profile of v6, /device:TPU:0, one launch (start us, length us, event | category | flops | bytes accessed | tf_op | source)
XLA Modules:
  0.0 41.9 jit_solution(7642260277996645793)
XLA Ops:
  0.0 3.0 %collective-permute-start.4 = (bf16[64,3072]{1,0:T(8,128)(2,1)}, bf16[64,3072]{1,0:T(8,128)(2,1)S(1)}, u32[]{:S(2)}, u32[]{:S(2)}) collective-permute-start(bf16[64,3072]{1,0:T(8,128)(2,1)} %bitcast.5), channel_id=1, source_target_pairs={{0,4},{4,0},{8,12},{12,8},{1,5},{5,1},{9,13},{13,9},{2,6},{6,2},{1... | collective-permute-start | bytes 1179656 | tf_op jit(solution)/shard_map/ppermute | solution.py:201
  3.0 0.0 copy-start.2
  3.0 0.7 %copy-done.2 = s32[64]{0:T(128)S(1)} copy-done((s32[64]{0:T(128)S(1)}, s32[64]{0:T(128)}, u32[]{:S(2)}) %copy-start.2) | copy-done | bytes 280
  3.7 0.0 copy-start
  3.7 0.0 copy-start.1
  3.7 17.5 %low_rank_and_base.1 = (f32[64,64]{1,0:T(8,128)S(1)}, bf16[32,3072]{1,0:T(8,128)(2,1)S(1)}, f32[32,3072]{1,0:T(8,128)S(1)}) custom-call(s32[1,64]{1,0:T(1,128)S(1)} %bitcast.7, bf16[64,8448]{1,0:T(8,128)(2,1)} %hidden.1, bf16[64,8448]{1,0:T(8,128)(2,1)} %bitcast.9, bf16[8448,3072]{1,0:T(8,128)(2,1)} %weight.1), custom_call_target="tpu_custom_call" | custom-call | flops 3391094784 | bytes 54067200 | tf_op jit(solution)/shard_map/low_rank_and_base/pallas_call | solution.py:100
  21.2 0.1 collective-permute-start.5
  21.3 0.1 collective-permute-start
  21.3 1.2 %collective-permute-done = f32[64,64]{1,0:T(8,128)S(1)} collective-permute-done((f32[64,64]{1,0:T(8,128)S(1)}, f32[64,64]{1,0:T(8,128)S(1)}, u32[]{:S(2)}, u32[]{:S(2)}) %collective-permute-start) | collective-permute-done | bytes 16416 | tf_op jit(solution)/shard_map/ppermute | solution.py:201
  22.5 1.9 %collective-permute-start.1 = (f32[64,64]{1,0:T(8,128)S(1)}, f32[64,64]{1,0:T(8,128)S(1)}, u32[]{:S(2)}, u32[]{:S(2)}) collective-permute-start(f32[64,64]{1,0:T(8,128)S(1)} %add.12), channel_id=1, source_target_pairs={{0,2},{2,0},{1,3},{3,1},{4,6},{6,4},{5,7},{7,5},{8,10},{10,8},{9,1... | collective-permute-start | bytes 49160 | tf_op jit(solution)/shard_map/ppermute | solution.py:201
  24.4 2.0 %collective-permute-done.1 = f32[64,64]{1,0:T(8,128)S(1)} collective-permute-done((f32[64,64]{1,0:T(8,128)S(1)}, f32[64,64]{1,0:T(8,128)S(1)}, u32[]{:S(2)}, u32[]{:S(2)}) %collective-permute-start.1) | collective-permute-done | bytes 16416 | tf_op jit(solution)/shard_map/ppermute | solution.py:201
  26.5 1.9 %collective-permute-start.2 = (f32[64,64]{1,0:T(8,128)S(1)}, f32[64,64]{1,0:T(8,128)S(1)}, u32[]{:S(2)}, u32[]{:S(2)}) collective-permute-start(f32[64,64]{1,0:T(8,128)S(1)} %add.13), channel_id=1, source_target_pairs={{0,4},{4,0},{8,12},{12,8},{1,5},{5,1},{9,13},{13,9},{2,6},{6,2},{1... | collective-permute-start | bytes 49160 | tf_op jit(solution)/shard_map/ppermute | solution.py:201
  28.4 2.0 %collective-permute-done.2 = f32[64,64]{1,0:T(8,128)S(1)} collective-permute-done((f32[64,64]{1,0:T(8,128)S(1)}, f32[64,64]{1,0:T(8,128)S(1)}, u32[]{:S(2)}, u32[]{:S(2)}) %collective-permute-start.2) | collective-permute-done | bytes 16416 | tf_op jit(solution)/shard_map/ppermute | solution.py:201
  30.4 3.0 %collective-permute-start.3 = (f32[64,64]{1,0:T(8,128)S(1)}, f32[64,64]{1,0:T(8,128)S(1)}, u32[]{:S(2)}, u32[]{:S(2)}) collective-permute-start(f32[64,64]{1,0:T(8,128)S(1)} %add.14), channel_id=1, source_target_pairs={{0,8},{4,12},{8,0},{12,4},{1,9},{5,13},{9,1},{13,5},{2,10},{6,14},... | collective-permute-start | bytes 49160 | tf_op jit(solution)/shard_map/ppermute | solution.py:201
  33.4 1.9 %collective-permute-done.3 = f32[64,64]{1,0:T(8,128)S(1)} collective-permute-done((f32[64,64]{1,0:T(8,128)S(1)}, f32[64,64]{1,0:T(8,128)S(1)}, u32[]{:S(2)}, u32[]{:S(2)}) %collective-permute-start.3) | collective-permute-done | bytes 16416 | tf_op jit(solution)/shard_map/ppermute | solution.py:201
  35.3 0.0 collective-permute-done.5.got
  35.3 0.0 collective-permute-done.4.up_there
  35.3 0.0 copy-done
  35.3 0.0 copy-done.1
  35.3 0.4 join.1
  35.7 3.0 %collective-permute-start.6 = (bf16[16,3072]{1,0:T(8,128)(2,1)S(1)}, bf16[16,3072]{1,0:T(8,128)(2,1)S(1)}, u32[]{:S(2)}, u32[]{:S(2)}) collective-permute-start(bf16[16,3072]{1,0:T(8,128)(2,1)S(1)} %get-tuple-element.14), channel_id=1, source_target_pairs={{0,8},{4,12},{8,0},{12,4},{1,9},{5,13},{9,1},{13,5},{2,10},{6,14},... | collective-permute-start | bytes 294920 | tf_op jit(solution)/shard_map/ppermute | solution.py:201
  38.7 2.6 %collective-permute-done.6.got = bf16[16,3072]{1,0:T(8,128)(2,1)S(1)} collective-permute-done((bf16[16,3072]{1,0:T(8,128)(2,1)S(1)}, bf16[16,3072]{1,0:T(8,128)(2,1)S(1)}, u32[]{:S(2)}, u32[]{:S(2)}) %collective-permute-start.6) | collective-permute-done | bytes 98336 | tf_op jit(solution)/shard_map/ppermute | solution.py:201
  41.3 0.7 %finish.1 = bf16[16,3072]{1,0:T(8,128)(2,1)} custom-call(f32[16,3072]{1,0:T(8,128)S(1)} %get-tuple-element.13.total, bf16[16,3072]{1,0:T(8,128)(2,1)S(1)} %collective-permute-done.6.got), custom_call_target="tpu_custom_call" | custom-call | tf_op jit(solution)/shard_map/finish/pallas_call | solution.py:190
  (4 shorter events, 0.0 us)
Async XLA Ops:
  0.0 35.3 %collective-permute-start.4 = (bf16[64,3072]{1,0:T(8,128)(2,1)}, bf16[64,3072]{1,0:T(8,128)(2,1)S(1)}, u32[]{:S(2)}, u32[]{:S(2)}) collective-permute-start(bf16[64,3072]{1,0:T(8,128)(2,1)} %bitcast.5), channel_id=1, source_target_pairs={{0,4},{4,0},{8,12},{12,8},{1,5},{5,1},{9,13},{13,9},{2,6},{6,2},{1... | collective-permute-start | bytes 1179656 | tf_op jit(solution)/shard_map/ppermute | solution.py:201
  3.0 0.7 %copy-start.2 = (s32[64]{0:T(128)S(1)}, s32[64]{0:T(128)}, u32[]{:S(2)}) copy-start(s32[64]{0:T(128)} %param.7) | copy-start | bytes 772
  3.7 31.6 %copy-start = (bf16[1,64,3072]{2,1,0:T(8,128)(2,1)S(1)}, bf16[1,64,3072]{2,1,0:T(8,128)(2,1)}, u32[]{:S(2)}) copy-start(bf16[1,64,3072]{2,1,0:T(8,128)(2,1)} %param.10) | copy-start | bytes 1179652
  3.7 31.6 %copy-start.1 = (bf16[16,3072]{1,0:T(8,128)(2,1)S(1)}, bf16[16,3072]{1,0:T(8,128)(2,1)}, u32[]{:S(2)}) copy-start(bf16[16,3072]{1,0:T(8,128)(2,1)} %residual.1) | copy-start | bytes 294916
  21.2 14.1 %collective-permute-start.5 = (bf16[32,3072]{1,0:T(8,128)(2,1)S(1)}, bf16[32,3072]{1,0:T(8,128)(2,1)S(1)}, u32[]{:S(2)}, u32[]{:S(2)}) collective-permute-start(bf16[32,3072]{1,0:T(8,128)(2,1)S(1)} %get-tuple-element.12), channel_id=1, source_target_pairs={{0,4},{4,0},{8,12},{12,8},{1,5},{5,1},{9,13},{13,9},{2,6},{6,2},{1... | collective-permute-start | bytes 589832 | tf_op jit(solution)/shard_map/ppermute | solution.py:201
  21.3 1.3 %collective-permute-start = (f32[64,64]{1,0:T(8,128)S(1)}, f32[64,64]{1,0:T(8,128)S(1)}, u32[]{:S(2)}, u32[]{:S(2)}) collective-permute-start(f32[64,64]{1,0:T(8,128)S(1)} %get-tuple-element.10), channel_id=1, source_target_pairs={{0,1},{1,0},{2,3},{3,2},{4,5},{5,4},{6,7},{7,6},{8,9},{9,8},{10,11... | collective-permute-start | bytes 49160 | tf_op jit(solution)/shard_map/ppermute | solution.py:201
  22.5 3.9 %collective-permute-start.1 = (f32[64,64]{1,0:T(8,128)S(1)}, f32[64,64]{1,0:T(8,128)S(1)}, u32[]{:S(2)}, u32[]{:S(2)}) collective-permute-start(f32[64,64]{1,0:T(8,128)S(1)} %add.12), channel_id=1, source_target_pairs={{0,2},{2,0},{1,3},{3,1},{4,6},{6,4},{5,7},{7,5},{8,10},{10,8},{9,1... | collective-permute-start | bytes 49160 | tf_op jit(solution)/shard_map/ppermute | solution.py:201
  26.5 3.9 %collective-permute-start.2 = (f32[64,64]{1,0:T(8,128)S(1)}, f32[64,64]{1,0:T(8,128)S(1)}, u32[]{:S(2)}, u32[]{:S(2)}) collective-permute-start(f32[64,64]{1,0:T(8,128)S(1)} %add.13), channel_id=1, source_target_pairs={{0,4},{4,0},{8,12},{12,8},{1,5},{5,1},{9,13},{13,9},{2,6},{6,2},{1... | collective-permute-start | bytes 49160 | tf_op jit(solution)/shard_map/ppermute | solution.py:201
  30.4 4.9 %collective-permute-start.3 = (f32[64,64]{1,0:T(8,128)S(1)}, f32[64,64]{1,0:T(8,128)S(1)}, u32[]{:S(2)}, u32[]{:S(2)}) collective-permute-start(f32[64,64]{1,0:T(8,128)S(1)} %add.14), channel_id=1, source_target_pairs={{0,8},{4,12},{8,0},{12,4},{1,9},{5,13},{9,1},{13,5},{2,10},{6,14},... | collective-permute-start | bytes 49160 | tf_op jit(solution)/shard_map/ppermute | solution.py:201
  35.7 5.6 %collective-permute-start.6 = (bf16[16,3072]{1,0:T(8,128)(2,1)S(1)}, bf16[16,3072]{1,0:T(8,128)(2,1)S(1)}, u32[]{:S(2)}, u32[]{:S(2)}) collective-permute-start(bf16[16,3072]{1,0:T(8,128)(2,1)S(1)} %get-tuple-element.14), channel_id=1, source_target_pairs={{0,8},{4,12},{8,0},{12,4},{1,9},{5,13},{9,1},{13,5},{2,10},{6,14},... | collective-permute-start | bytes 294920 | tf_op jit(solution)/shard_map/ppermute | solution.py:201

commit v7 on v6

--- a/solution.py
+++ b/solution.py
@@ -27,7 +27,7 @@
 
 
 def stream_kernel(
-    ids, hidden, rank_down, weight, low, sent, kept, ids_here, hidden_here, down_here, total, held, got, arrived
+    hidden, rank_down, weight, packed, sent, kept, hidden_here, down_here, total, held, got, arrived
 ):
     groups = weight.shape[0] // (PART * GROUP)
     width = weight.shape[1]
@@ -44,7 +44,6 @@
     first = [
         pltpu.make_async_copy(hidden, hidden_here, got.at[0]),
         pltpu.make_async_copy(rank_down, down_here, got.at[1]),
-        pltpu.make_async_copy(ids, ids_here, got.at[2]),
     ]
     for copy in first:
         copy.start()
@@ -57,15 +56,20 @@
     total[...] = jnp.zeros_like(total)
     for copy in first:
         copy.wait()
-    owned = lax.axis_index("page") * lax.axis_size("sub") + lax.axis_index("sub")
-    mine = column_of(ids_here[...]) == owned.astype(jnp.float32)
-    product = lax.dot_general(
+    low = lax.dot_general(
         hidden_here[...],
         down_here[...],
         (((1,), (1,)), ((), ())),
         preferred_element_type=jnp.float32,
     )
-    low[...] = jnp.where(mine, product, 0.0)
+    block = low.shape[0] // 4
+    for bit in range(2):
+        wanted = jnp.concatenate(
+            [low[(half + bit) * block : (half + bit + 1) * block] for half in (0, 2)], axis=1
+        )
+        for to in range(packed.shape[0]):
+            if (to // 4) % 2 == bit:
+                packed[to] = wanted
 
     def add(group, part, depth):
         at = pl.ds(pl.multiple_of(group * deep + part * PART, PART), depth)
@@ -93,26 +97,25 @@
     split_rows(total, slice(0, width), sent, kept)
 
 
-def stream_phase(ids, hidden, rank_down, weight):
+def stream_phase(hidden, rank_down, weight):
     rows, depth = hidden.shape
     rank = rank_down.shape[0]
     width = weight.shape[1]
     return pl.pallas_call(
         stream_kernel,
         out_shape=(
-            jax.ShapeDtypeStruct((rows, rank), jnp.float32),
+            jax.ShapeDtypeStruct((16, rows // 4, 2 * rank), jnp.float32),
             jax.ShapeDtypeStruct((rows // 2, width), jnp.bfloat16),
             jax.ShapeDtypeStruct((rows // 2, width), jnp.float32),
         ),
-        in_specs=[HBM] * 4,
+        in_specs=[HBM] * 3,
         out_specs=(VMEM,) * 3,
         scratch_shapes=[
-            pltpu.VMEM(ids.shape, ids.dtype),
             pltpu.VMEM(hidden.shape, hidden.dtype),
             pltpu.VMEM(rank_down.shape, rank_down.dtype),
             pltpu.VMEM((rows, width), jnp.float32),
             pltpu.VMEM((SLOTS * GROUP * PART, width), weight.dtype),
-            pltpu.SemaphoreType.DMA((3,)),
+            pltpu.SemaphoreType.DMA((2,)),
             pltpu.SemaphoreType.DMA((SLOTS * GROUP,)),
         ],
         compiler_params=pltpu.CompilerParams(vmem_limit_bytes=53 << 20),
@@ -122,7 +125,7 @@
             transcendentals=0,
         ),
         name="low_rank_and_base",
-    )(ids, hidden, rank_down, weight)
+    )(hidden, rank_down, weight)
 
 
 def split_rows(total, at, sent, kept):
@@ -136,22 +139,24 @@
         kept[rows, at] = total[here, :]
 
 
-def join_kernel(ids, low, up_here, up_there, kept, got, residual, sent, total, joined):
+def join_kernel(ids, packed, up_here, up_there, kept, got, residual, sent, total, joined):
     block = residual.shape[0]
+    rank = up_here.shape[0]
     tp = lax.axis_index("tp")
     high, bit = lax.div(tp, 2), lax.rem(tp, 2)
-    adapter = column_of(ids[...])
-    here = jnp.where(adapter == tp.astype(jnp.float32), low[...], 0.0)
-    there = jnp.where(adapter == (tp + 1 - 2 * bit).astype(jnp.float32), low[...], 0.0)
-    halves = []
-    for half in range(2):
-        even = slice(2 * half * block, (2 * half + 1) * block)
-        odd = slice((2 * half + 1) * block, (2 * half + 2) * block)
-        halves.append([jnp.where(bit == 0, x[even], x[odd]) for x in (here, there)])
-    coefficient = [
-        jnp.concatenate([halves[0][i], halves[1][i]], axis=0).astype(jnp.bfloat16)
-        for i in range(2)
-    ]
+    every = column_of(ids[...])
+    parts = [every[index * block : (index + 1) * block] for index in range(4)]
+    adapter = jnp.concatenate(
+        [jnp.where(bit == 0, parts[half], parts[half + 1]) for half in (0, 2)], axis=0
+    )
+    coefficient = []
+    for index in (tp, tp + 1 - 2 * bit):
+        low = packed[index]
+        for source in range(1, 4):
+            low = low + packed[4 * source + index]
+        low = jnp.concatenate([low[:, :rank], low[:, rank:]], axis=0)
+        low = jnp.where(adapter == index.astype(jnp.float32), low, 0.0)
+        coefficient.append(low.astype(jnp.bfloat16))
     width = residual.shape[1]
     for start in range(0, width, TILE):
         at = slice(start, start + TILE)
@@ -167,7 +172,7 @@
     total[...] = joined[near, :] + residual[...].astype(jnp.float32)
 
 
-def join_phase(ids, low, up_here, up_there, kept, got, residual):
+def join_phase(ids, packed, up_here, up_there, kept, got, residual):
     return pl.pallas_call(
         join_kernel,
         out_shape=(
@@ -179,7 +184,7 @@
         scratch_shapes=[pltpu.VMEM(kept.shape, kept.dtype)],
         compiler_params=pltpu.CompilerParams(vmem_limit_bytes=8 << 20),
         name="join",
-    )(ids, low, up_here, up_there, kept, got, residual)
+    )(ids, packed, up_here, up_there, kept, got, residual)
 
 
 def finish_kernel(total, got, mixed):
@@ -197,22 +202,18 @@
     )(total, got)
 
 
-def swap(value, axis, bit=1):
-    return lax.ppermute(value, axis, [(i, i ^ bit) for i in range(lax.axis_size(axis))])
+def swap(value, bit):
+    return lax.ppermute(value, "tp", [(i, i ^ bit) for i in range(lax.axis_size("tp"))])
 
 
 def four_by_four(hidden, adapter_ids, weight, rank_down, rank_up, residual):
-    ids = adapter_ids[None]
     up = rank_up[0]
-    up_there = swap(up, "tp", 1)
-    low, sent, kept = stream_phase(ids, hidden, jnp.swapaxes(rank_down, 1, 2)[0], weight)
-    got = swap(sent, "tp", 1)
-    low = low + swap(low, "sub")
-    low = low + swap(low, "page")
-    low = low + swap(low, "tp", 1)
-    low = low + swap(low, "tp", 2)
-    sent, total = join_phase(ids, low, up, up_there, kept, got, residual)
-    return finish_phase(total, swap(sent, "tp", 2))
+    up_there = swap(up, 1)
+    packed, sent, kept = stream_phase(hidden, jnp.swapaxes(rank_down, 1, 2)[0], weight)
+    got = swap(sent, 1)
+    packed = lax.all_to_all(packed, ("tp",) + PS, split_axis=0, concat_axis=0, tiled=True)
+    sent, total = join_phase(adapter_ids[None], packed, up, up_there, kept, got, residual)
+    return finish_phase(total, swap(sent, 2))
 
 
 def any_size(hidden_units, adapter_ids, down_projection_weight, rank_down, rank_up, residual):

time: 42.1 us -> 43.9 us (1.043)
  waiting for transfers between devices: 9.7 us -> 12.5 us
  starting transfers between devices: 13 us -> 12.3 us
  local copies, waits for them, and re-layouts: 0.66 us -> 0.01 us
    ppermute x7 -> x3, starting transfers between devices: 13 us -> 7.38 us  [swap(): lax.ppermute(value, 'tp', [(i, i ^ bit) for i in range(lax.axis_size('tp'...]
    all_to_all x0 -> x1, starting transfers between devices: none -> 4.91 us  [four_by_four(): lax.all_to_all(packed, ('tp',) + PS, split_axis=0, concat_axis=0, tiled=T...]
    ppermute x7 -> x3, waiting for transfers between devices: 9.7 us -> 12.5 us  [swap(): lax.ppermute(value, 'tp', [(i, i ^ bit) for i in range(lax.axis_size('tp'...]
    unnamed x6, local copies, waits for them, and re-layouts: 0.66 us -> 0.01 us
  transfers between devices with their start and end apart: 7 -> 4, of which waited for: 5 -> 2; matrix products, arithmetic and copies ran while one was open for 0% -> 0% of each run, Pallas kernels for 42% -> 41%
where the time goes in v7:
time: 43.9 us; the launch traced here: 43.7 us
  Pallas kernels  18.8 us (43%)
  waiting for transfers between devices  12.5 us (28%)
  starting transfers between devices  12.3 us (28%)
    pallas_call x1, Pallas kernels, stream_phase(): pl.pallas_call(stream_kernel, out_shape=(jax.ShapeDtypeStruct((16, rows /...  17.7 us
    ppermute x3, waiting for transfers between devices, swap(): lax.ppermute(value, 'tp', [(i, i ^ bit) for i in range(lax.axis_size('tp'...  12.5 us
    ppermute x3, starting transfers between devices, swap(): lax.ppermute(value, 'tp', [(i, i ^ bit) for i in range(lax.axis_size('tp'...  7.38 us
    all_to_all x1, starting transfers between devices, four_by_four(): lax.all_to_all(packed, ('tp',) + PS, split_axis=0, concat_axis=0, tiled=T...  4.91 us
  transfers between devices with their start and end apart: 4, of which 2 were waited for; matrix products, arithmetic and copies ran while one was open for 0% of the time, Pallas kernels for 41%

profile of v7, /device:TPU:0, one launch (start us, length us, event | category | flops | bytes accessed | tf_op | source)
XLA Modules:
  0.0 43.7 jit_solution(12683757052003764906)
XLA Ops:
  0.0 3.0 %collective-permute-start = (bf16[64,3072]{1,0:T(8,128)(2,1)}, bf16[64,3072]{1,0:T(8,128)(2,1)S(1)}, u32[]{:S(2)}, u32[]{:S(2)}) collective-permute-start(bf16[64,3072]{1,0:T(8,128)(2,1)} %bitcast.5), channel_id=1, source_target_pairs={{0,4},{4,0},{8,12},{12,8},{1,5},{5,1},{9,13},{13,9},{2,6},{6,2},{1... | collective-permute-start | bytes 1179656 | tf_op jit(solution)/shard_map/ppermute | solution.py:206
  3.0 0.0 copy-start
  3.0 0.0 copy-start.1
  3.0 0.0 copy-start.2
  3.0 17.7 %low_rank_and_base.1 = (f32[16,16,128]{2,1,0:T(8,128)}, bf16[32,3072]{1,0:T(8,128)(2,1)S(1)}, f32[32,3072]{1,0:T(8,128)S(1)}) custom-call(bf16[64,8448]{1,0:T(8,128)(2,1)} %hidden.1, bf16[64,8448]{1,0:T(8,128)(2,1)} %bitcast.8, bf16[8448,3072]{1,0:T(8,128)(2,1)} %weight.1), custom_call_target="tpu_custom_call" | custom-call | flops 3391094784 | bytes 54067200 | tf_op jit(solution)/shard_map/low_rank_and_base/pallas_call | solution.py:104
  20.7 4.9 %all-to-all-start = ((f32[16,16,128]{2,1,0:T(8,128)}), f32[16,16,128]{2,1,0:T(8,128)S(1)}, u32[]{:S(2)}, u32[]{:S(2)}) async-start(f32[16,16,128]{2,1,0:T(8,128)} %get-tuple-element.10), calls=%async_computation | async-start | bytes 262144 | tf_op jit(solution)/shard_map/all_to_all | solution.py:214
  25.7 1.9 %collective-permute-start.1 = (bf16[32,3072]{1,0:T(8,128)(2,1)S(1)}, bf16[32,3072]{1,0:T(8,128)(2,1)S(1)}, u32[]{:S(2)}, u32[]{:S(2)}) collective-permute-start(bf16[32,3072]{1,0:T(8,128)(2,1)S(1)} %get-tuple-element.12), channel_id=1, source_target_pairs={{0,4},{4,0},{8,12},{12,8},{1,5},{5,1},{9,13},{13,9},{2,6},{6,2},{1... | collective-permute-start | bytes 589832 | tf_op jit(solution)/shard_map/ppermute | solution.py:206
  27.6 7.5 %collective-permute-done.1.got = bf16[32,3072]{1,0:T(8,128)(2,1)S(1)} collective-permute-done((bf16[32,3072]{1,0:T(8,128)(2,1)S(1)}, bf16[32,3072]{1,0:T(8,128)(2,1)S(1)}, u32[]{:S(2)}, u32[]{:S(2)}) %collective-permute-start.1) | collective-permute-done | bytes 196640 | tf_op jit(solution)/shard_map/ppermute | solution.py:206
  35.1 0.0 all-to-all-done.packed
  35.1 0.0 collective-permute-done.up_there
  35.1 0.0 copy-done
  35.1 0.0 copy-done.1
  35.1 0.0 copy-done.2
  35.1 0.4 %join.1 = (bf16[16,3072]{1,0:T(8,128)(2,1)S(1)}, f32[16,3072]{1,0:T(8,128)S(1)}) custom-call(s32[1,64]{1,0:T(1,128)S(1)} %bitcast.7, f32[16,16,128]{2,1,0:T(8,128)S(1)} %all-to-all-done.packed, bf16[64,3072]{1,0:T(8,128)(2,1)S(1)} %bitcast.6, bf16[64,3072]{1,0:T(8,128)(2,1)S(1)} %collective-permute-done.up_there, f32[32,3072]{1,0:T(8,128)S(1)} %get-tuple-element.11.kept, ...), custom_call_target="tpu_custom_call" | custom-call | tf_op jit(solution)/shard_map/join/pallas_call | solution.py:176
  35.6 2.4 %collective-permute-start.2 = (bf16[16,3072]{1,0:T(8,128)(2,1)S(1)}, bf16[16,3072]{1,0:T(8,128)(2,1)S(1)}, u32[]{:S(2)}, u32[]{:S(2)}) collective-permute-start(bf16[16,3072]{1,0:T(8,128)(2,1)S(1)} %get-tuple-element.14), channel_id=1, source_target_pairs={{0,8},{4,12},{8,0},{12,4},{1,9},{5,13},{9,1},{13,5},{2,10},{6,14},... | collective-permute-start | bytes 294920 | tf_op jit(solution)/shard_map/ppermute | solution.py:206
  38.0 5.0 %collective-permute-done.2.got = bf16[16,3072]{1,0:T(8,128)(2,1)S(1)} collective-permute-done((bf16[16,3072]{1,0:T(8,128)(2,1)S(1)}, bf16[16,3072]{1,0:T(8,128)(2,1)S(1)}, u32[]{:S(2)}, u32[]{:S(2)}) %collective-permute-start.2) | collective-permute-done | bytes 98336 | tf_op jit(solution)/shard_map/ppermute | solution.py:206
  43.0 0.7 %finish.1 = bf16[16,3072]{1,0:T(8,128)(2,1)} custom-call(f32[16,3072]{1,0:T(8,128)S(1)} %get-tuple-element.13.total, bf16[16,3072]{1,0:T(8,128)(2,1)S(1)} %collective-permute-done.2.got), custom_call_target="tpu_custom_call" | custom-call | tf_op jit(solution)/shard_map/finish/pallas_call | solution.py:195
Async XLA Ops:
  0.0 35.1 %collective-permute-start = (bf16[64,3072]{1,0:T(8,128)(2,1)}, bf16[64,3072]{1,0:T(8,128)(2,1)S(1)}, u32[]{:S(2)}, u32[]{:S(2)}) collective-permute-start(bf16[64,3072]{1,0:T(8,128)(2,1)} %bitcast.5), channel_id=1, source_target_pairs={{0,4},{4,0},{8,12},{12,8},{1,5},{5,1},{9,13},{13,9},{2,6},{6,2},{1... | collective-permute-start | bytes 1179656 | tf_op jit(solution)/shard_map/ppermute | solution.py:206
  3.0 32.1 %copy-start = (bf16[1,64,3072]{2,1,0:T(8,128)(2,1)S(1)}, bf16[1,64,3072]{2,1,0:T(8,128)(2,1)}, u32[]{:S(2)}) copy-start(bf16[1,64,3072]{2,1,0:T(8,128)(2,1)} %param.10) | copy-start | bytes 1179652
  3.0 32.1 %copy-start.1 = (bf16[16,3072]{1,0:T(8,128)(2,1)S(1)}, bf16[16,3072]{1,0:T(8,128)(2,1)}, u32[]{:S(2)}) copy-start(bf16[16,3072]{1,0:T(8,128)(2,1)} %residual.1) | copy-start | bytes 294916
  3.0 32.1 %copy-start.2 = (s32[64]{0:T(128)S(1)}, s32[64]{0:T(128)}, u32[]{:S(2)}) copy-start(s32[64]{0:T(128)} %param.7) | copy-start | bytes 772
  20.7 14.4 %all-to-all-start = ((f32[16,16,128]{2,1,0:T(8,128)}), f32[16,16,128]{2,1,0:T(8,128)S(1)}, u32[]{:S(2)}, u32[]{:S(2)}) async-start(f32[16,16,128]{2,1,0:T(8,128)} %get-tuple-element.10), calls=%async_computation | async-start | bytes 262144 | tf_op jit(solution)/shard_map/all_to_all | solution.py:214
  25.7 9.4 %collective-permute-start.1 = (bf16[32,3072]{1,0:T(8,128)(2,1)S(1)}, bf16[32,3072]{1,0:T(8,128)(2,1)S(1)}, u32[]{:S(2)}, u32[]{:S(2)}) collective-permute-start(bf16[32,3072]{1,0:T(8,128)(2,1)S(1)} %get-tuple-element.12), channel_id=1, source_target_pairs={{0,4},{4,0},{8,12},{12,8},{1,5},{5,1},{9,13},{13,9},{2,6},{6,2},{1... | collective-permute-start | bytes 589832 | tf_op jit(solution)/shard_map/ppermute | solution.py:206
  35.6 7.4 %collective-permute-start.2 = (bf16[16,3072]{1,0:T(8,128)(2,1)S(1)}, bf16[16,3072]{1,0:T(8,128)(2,1)S(1)}, u32[]{:S(2)}, u32[]{:S(2)}) collective-permute-start(bf16[16,3072]{1,0:T(8,128)(2,1)S(1)} %get-tuple-element.14), channel_id=1, source_target_pairs={{0,8},{4,12},{8,0},{12,4},{1,9},{5,13},{9,1},{13,5},{2,10},{6,14},... | collective-permute-start | bytes 294920 | tf_op jit(solution)/shard_map/ppermute | solution.py:206

commit v8 on v7

--- a/solution.py
+++ b/solution.py
@@ -139,7 +139,23 @@
         kept[rows, at] = total[here, :]
 
 
-def join_kernel(ids, packed, up_here, up_there, kept, got, residual, sent, total, joined):
+def pair_kernel(kept, got, pair):
+    pair[...] = kept[...] + got[...].astype(jnp.float32)
+
+
+def pair_phase(kept, got):
+    return pl.pallas_call(
+        pair_kernel,
+        out_shape=jax.ShapeDtypeStruct(kept.shape, kept.dtype),
+        in_specs=[VMEM] * 2,
+        out_specs=VMEM,
+        compiler_params=pltpu.CompilerParams(vmem_limit_bytes=8 << 20),
+        cost_estimate=pl.CostEstimate(flops=1 << 34, bytes_accessed=1 << 28, transcendentals=0),
+        name="pair_sum",
+    )(kept, got)
+
+
+def join_kernel(ids, packed, up_here, up_there, pair, residual, sent, total, joined):
     block = residual.shape[0]
     rank = up_here.shape[0]
     tp = lax.axis_index("tp")
@@ -161,8 +177,7 @@
     for start in range(0, width, TILE):
         at = slice(start, start + TILE)
         joined[:, at] = (
-            kept[:, at]
-            + got[:, at].astype(jnp.float32)
+            pair[:, at]
             + jnp.dot(coefficient[0], up_here[:, at], preferred_element_type=jnp.float32)
             + jnp.dot(coefficient[1], up_there[:, at], preferred_element_type=jnp.float32)
         )
@@ -172,19 +187,19 @@
     total[...] = joined[near, :] + residual[...].astype(jnp.float32)
 
 
-def join_phase(ids, packed, up_here, up_there, kept, got, residual):
+def join_phase(ids, packed, up_here, up_there, pair, residual):
     return pl.pallas_call(
         join_kernel,
         out_shape=(
             jax.ShapeDtypeStruct(residual.shape, jnp.bfloat16),
             jax.ShapeDtypeStruct(residual.shape, jnp.float32),
         ),
-        in_specs=[VMEM] * 7,
+        in_specs=[VMEM] * 6,
         out_specs=(VMEM,) * 2,
-        scratch_shapes=[pltpu.VMEM(kept.shape, kept.dtype)],
+        scratch_shapes=[pltpu.VMEM(pair.shape, pair.dtype)],
         compiler_params=pltpu.CompilerParams(vmem_limit_bytes=8 << 20),
         name="join",
-    )(ids, packed, up_here, up_there, kept, got, residual)
+    )(ids, packed, up_here, up_there, pair, residual)
 
 
 def finish_kernel(total, got, mixed):
@@ -210,9 +225,9 @@
     up = rank_up[0]
     up_there = swap(up, 1)
     packed, sent, kept = stream_phase(hidden, jnp.swapaxes(rank_down, 1, 2)[0], weight)
-    got = swap(sent, 1)
+    pair = pair_phase(kept, swap(sent, 1))
     packed = lax.all_to_all(packed, ("tp",) + PS, split_axis=0, concat_axis=0, tiled=True)
-    sent, total = join_phase(adapter_ids[None], packed, up, up_there, kept, got, residual)
+    sent, total = join_phase(adapter_ids[None], packed, up, up_there, pair, residual)
     return finish_phase(total, swap(sent, 2))
 
 

time: 43.9 us -> 48.1 us (1.096)
  waiting for transfers between devices: 12.5 us -> 16.6 us
    all_to_all x1, waiting for transfers between devices: 0.01 us -> 6.37 us  [four_by_four(): lax.all_to_all(packed, ('tp',) + PS, split_axis=0, concat_axis=0, tiled=T...]
    ppermute x3, waiting for transfers between devices: 12.5 us -> 10.2 us  [swap(): lax.ppermute(value, 'tp', [(i, i ^ bit) for i in range(lax.axis_size('tp'...]
  transfers between devices with their start and end apart: 4 -> 4, of which waited for: 2 -> 3; matrix products, arithmetic and copies ran while one was open for 0% -> 0% of each run, Pallas kernels for 41% -> 0%
where the time goes in v8:
time: 48.1 us; the launch traced here: 47.9 us
  Pallas kernels  18.8 us (39%)
  waiting for transfers between devices  16.6 us (35%)
  starting transfers between devices  12.4 us (26%)
    pallas_call x1, Pallas kernels, stream_phase(): pl.pallas_call(stream_kernel, out_shape=(jax.ShapeDtypeStruct((16, rows /...  17.7 us
    ppermute x3, waiting for transfers between devices, swap(): lax.ppermute(value, 'tp', [(i, i ^ bit) for i in range(lax.axis_size('tp'...  10.2 us
    ppermute x3, starting transfers between devices, swap(): lax.ppermute(value, 'tp', [(i, i ^ bit) for i in range(lax.axis_size('tp'...  7.51 us
    all_to_all x1, waiting for transfers between devices, four_by_four(): lax.all_to_all(packed, ('tp',) + PS, split_axis=0, concat_axis=0, tiled=T...  6.37 us
    all_to_all x1, starting transfers between devices, four_by_four(): lax.all_to_all(packed, ('tp',) + PS, split_axis=0, concat_axis=0, tiled=T...  4.9 us
  transfers between devices with their start and end apart: 4, of which 3 were waited for; matrix products, arithmetic and copies ran while one was open for 0% of the time, Pallas kernels for 0%

profile of v8, /device:TPU:0, one launch (start us, length us, event | category | flops | bytes accessed | tf_op | source)
XLA Modules:
  0.0 47.9 jit_solution(3853682825729690821)
XLA Ops:
  0.0 0.0 copy-start
  0.0 17.7 %low_rank_and_base.1 = (f32[16,16,128]{2,1,0:T(8,128)}, bf16[32,3072]{1,0:T(8,128)(2,1)S(1)}, f32[32,3072]{1,0:T(8,128)S(1)}) custom-call(bf16[64,8448]{1,0:T(8,128)(2,1)} %hidden.1, bf16[64,8448]{1,0:T(8,128)(2,1)} %bitcast.8, bf16[8448,3072]{1,0:T(8,128)(2,1)} %weight.1), custom_call_target="tpu_custom_call" | custom-call | flops 3391094784 | bytes 54067200 | tf_op jit(solution)/shard_map/low_rank_and_base/pallas_call | solution.py:104
  17.7 3.1 %collective-permute-start.1 = (bf16[32,3072]{1,0:T(8,128)(2,1)S(1)}, bf16[32,3072]{1,0:T(8,128)(2,1)S(1)}, u32[]{:S(2)}, u32[]{:S(2)}) collective-permute-start(bf16[32,3072]{1,0:T(8,128)(2,1)S(1)} %get-tuple-element.12), channel_id=1, source_target_pairs={{0,4},{4,0},{8,12},{12,8},{1,5},{5,1},{9,13},{13,9},{2,6},{6,2},{1... | collective-permute-start | bytes 589832 | tf_op jit(solution)/shard_map/ppermute | solution.py:221
  20.8 4.9 %all-to-all-start = ((f32[16,16,128]{2,1,0:T(8,128)}), f32[16,16,128]{2,1,0:T(8,128)S(1)}, u32[]{:S(2)}, u32[]{:S(2)}) async-start(f32[16,16,128]{2,1,0:T(8,128)} %get-tuple-element.10), calls=%async_computation | async-start | bytes 262144 | tf_op jit(solution)/shard_map/all_to_all | solution.py:229
  25.7 0.0 copy-done
  25.7 2.0 %collective-permute-start = (bf16[64,3072]{1,0:T(8,128)(2,1)S(1)}, bf16[64,3072]{1,0:T(8,128)(2,1)S(1)}, u32[]{:S(2)}, u32[]{:S(2)}) collective-permute-start(bf16[64,3072]{1,0:T(8,128)(2,1)S(1)} %bitcast.5), channel_id=1, source_target_pairs={{0,4},{4,0},{8,12},{12,8},{1,5},{5,1},{9,13},{13,9},{2,6},{6,2},{1... | collective-permute-start | bytes 1179656 | tf_op jit(solution)/shard_map/ppermute | solution.py:221
  27.7 0.0 collective-permute-done.1.got
  27.7 0.0 copy-start.1
  27.7 0.0 copy-start.2
  27.8 6.4 %all-to-all-done.packed = f32[16,16,128]{2,1,0:T(8,128)S(1)} async-done(((f32[16,16,128]{2,1,0:T(8,128)}), f32[16,16,128]{2,1,0:T(8,128)S(1)}, u32[]{:S(2)}, u32[]{:S(2)}) %all-to-all-start) | async-done | bytes 131104 | tf_op jit(solution)/shard_map/all_to_all | solution.py:229
  34.1 5.2 %collective-permute-done.up_there = bf16[64,3072]{1,0:T(8,128)(2,1)S(1)} collective-permute-done((bf16[64,3072]{1,0:T(8,128)(2,1)S(1)}, bf16[64,3072]{1,0:T(8,128)(2,1)S(1)}, u32[]{:S(2)}, u32[]{:S(2)}) %collective-permute-start) | collective-permute-done | bytes 393248 | tf_op jit(solution)/shard_map/ppermute | solution.py:221
  39.4 0.0 copy-done.1
  39.4 0.0 copy-done.2
  39.4 0.4 join.1
  39.8 2.4 %collective-permute-start.2 = (bf16[16,3072]{1,0:T(8,128)(2,1)S(1)}, bf16[16,3072]{1,0:T(8,128)(2,1)S(1)}, u32[]{:S(2)}, u32[]{:S(2)}) collective-permute-start(bf16[16,3072]{1,0:T(8,128)(2,1)S(1)} %get-tuple-element.14), channel_id=1, source_target_pairs={{0,8},{4,12},{8,0},{12,4},{1,9},{5,13},{9,1},{13,5},{2,10},{6,14},... | collective-permute-start | bytes 294920 | tf_op jit(solution)/shard_map/ppermute | solution.py:221
  42.3 5.0 %collective-permute-done.2.got = bf16[16,3072]{1,0:T(8,128)(2,1)S(1)} collective-permute-done((bf16[16,3072]{1,0:T(8,128)(2,1)S(1)}, bf16[16,3072]{1,0:T(8,128)(2,1)S(1)}, u32[]{:S(2)}, u32[]{:S(2)}) %collective-permute-start.2) | collective-permute-done | bytes 98336 | tf_op jit(solution)/shard_map/ppermute | solution.py:221
  47.2 0.7 %finish.1 = bf16[16,3072]{1,0:T(8,128)(2,1)} custom-call(f32[16,3072]{1,0:T(8,128)S(1)} %get-tuple-element.13.total, bf16[16,3072]{1,0:T(8,128)(2,1)S(1)} %collective-permute-done.2.got), custom_call_target="tpu_custom_call" | custom-call | tf_op jit(solution)/shard_map/finish/pallas_call | solution.py:210
  (1 shorter events, 0.0 us)
Async XLA Ops:
  0.0 25.7 %copy-start = (bf16[1,64,3072]{2,1,0:T(8,128)(2,1)S(1)}, bf16[1,64,3072]{2,1,0:T(8,128)(2,1)}, u32[]{:S(2)}) copy-start(bf16[1,64,3072]{2,1,0:T(8,128)(2,1)} %param.10) | copy-start | bytes 1179652
  17.7 10.0 %collective-permute-start.1 = (bf16[32,3072]{1,0:T(8,128)(2,1)S(1)}, bf16[32,3072]{1,0:T(8,128)(2,1)S(1)}, u32[]{:S(2)}, u32[]{:S(2)}) collective-permute-start(bf16[32,3072]{1,0:T(8,128)(2,1)S(1)} %get-tuple-element.12), channel_id=1, source_target_pairs={{0,4},{4,0},{8,12},{12,8},{1,5},{5,1},{9,13},{13,9},{2,6},{6,2},{1... | collective-permute-start | bytes 589832 | tf_op jit(solution)/shard_map/ppermute | solution.py:221
  20.8 13.3 %all-to-all-start = ((f32[16,16,128]{2,1,0:T(8,128)}), f32[16,16,128]{2,1,0:T(8,128)S(1)}, u32[]{:S(2)}, u32[]{:S(2)}) async-start(f32[16,16,128]{2,1,0:T(8,128)} %get-tuple-element.10), calls=%async_computation | async-start | bytes 262144 | tf_op jit(solution)/shard_map/all_to_all | solution.py:229
  25.7 13.7 %collective-permute-start = (bf16[64,3072]{1,0:T(8,128)(2,1)S(1)}, bf16[64,3072]{1,0:T(8,128)(2,1)S(1)}, u32[]{:S(2)}, u32[]{:S(2)}) collective-permute-start(bf16[64,3072]{1,0:T(8,128)(2,1)S(1)} %bitcast.5), channel_id=1, source_target_pairs={{0,4},{4,0},{8,12},{12,8},{1,5},{5,1},{9,13},{13,9},{2,6},{6,2},{1... | collective-permute-start | bytes 1179656 | tf_op jit(solution)/shard_map/ppermute | solution.py:221
  27.7 11.7 %copy-start.1 = (bf16[16,3072]{1,0:T(8,128)(2,1)S(1)}, bf16[16,3072]{1,0:T(8,128)(2,1)}, u32[]{:S(2)}) copy-start(bf16[16,3072]{1,0:T(8,128)(2,1)} %residual.1) | copy-start | bytes 294916
  27.7 11.7 %copy-start.2 = (s32[64]{0:T(128)S(1)}, s32[64]{0:T(128)}, u32[]{:S(2)}) copy-start(s32[64]{0:T(128)} %param.7) | copy-start | bytes 772
  39.8 7.4 %collective-permute-start.2 = (bf16[16,3072]{1,0:T(8,128)(2,1)S(1)}, bf16[16,3072]{1,0:T(8,128)(2,1)S(1)}, u32[]{:S(2)}, u32[]{:S(2)}) collective-permute-start(bf16[16,3072]{1,0:T(8,128)(2,1)S(1)} %get-tuple-element.14), channel_id=1, source_target_pairs={{0,8},{4,12},{8,0},{12,4},{1,9},{5,13},{9,1},{13,5},{2,10},{6,14},... | collective-permute-start | bytes 294920 | tf_op jit(solution)/shard_map/ppermute | solution.py:221

commit v9 on v8

--- a/solution.py
+++ b/solution.py
@@ -225,6 +225,7 @@
     up = rank_up[0]
     up_there = swap(up, 1)
     packed, sent, kept = stream_phase(hidden, jnp.swapaxes(rank_down, 1, 2)[0], weight)
+    sent, up_there = lax.optimization_barrier((sent, up_there))
     pair = pair_phase(kept, swap(sent, 1))
     packed = lax.all_to_all(packed, ("tp",) + PS, split_axis=0, concat_axis=0, tiled=True)
     sent, total = join_phase(adapter_ids[None], packed, up, up_there, pair, residual)

time: 48.1 us -> 43.6 us (0.906)
  starting transfers between devices: 12.4 us -> 9.93 us
  waiting for transfers between devices: 16.6 us -> 14.5 us
    ppermute x3, starting transfers between devices: 7.51 us -> 3.58 us  [swap(): lax.ppermute(value, 'tp', [(i, i ^ bit) for i in range(lax.axis_size('tp'...]
    ppermute x3, waiting for transfers between devices: 10.2 us -> 6.63 us  [swap(): lax.ppermute(value, 'tp', [(i, i ^ bit) for i in range(lax.axis_size('tp'...]
    all_to_all x1, waiting for transfers between devices: 6.37 us -> 7.84 us  [four_by_four(): lax.all_to_all(packed, ('tp',) + PS, split_axis=0, concat_axis=0, tiled=T...]
    all_to_all x1, starting transfers between devices: 4.9 us -> 6.35 us  [four_by_four(): lax.all_to_all(packed, ('tp',) + PS, split_axis=0, concat_axis=0, tiled=T...]
  transfers between devices with their start and end apart: 4 -> 4, of which waited for: 3 -> 2; matrix products, arithmetic and copies ran while one was open for 0% -> 0% of each run, Pallas kernels for 0% -> 41%
where the time goes in v9:
time: 43.6 us; the launch traced here: 43.4 us
  Pallas kernels  18.8 us (43%)
  waiting for transfers between devices  14.5 us (33%)
  starting transfers between devices  9.93 us (23%)
    pallas_call x1, Pallas kernels, stream_phase(): pl.pallas_call(stream_kernel, out_shape=(jax.ShapeDtypeStruct((16, rows /...  17.7 us
    all_to_all x1, waiting for transfers between devices, four_by_four(): lax.all_to_all(packed, ('tp',) + PS, split_axis=0, concat_axis=0, tiled=T...  7.84 us
    ppermute x3, waiting for transfers between devices, swap(): lax.ppermute(value, 'tp', [(i, i ^ bit) for i in range(lax.axis_size('tp'...  6.63 us
    all_to_all x1, starting transfers between devices, four_by_four(): lax.all_to_all(packed, ('tp',) + PS, split_axis=0, concat_axis=0, tiled=T...  6.35 us
    ppermute x3, starting transfers between devices, swap(): lax.ppermute(value, 'tp', [(i, i ^ bit) for i in range(lax.axis_size('tp'...  3.58 us
  transfers between devices with their start and end apart: 4, of which 2 were waited for; matrix products, arithmetic and copies ran while one was open for 0% of the time, Pallas kernels for 41%

profile of v9, /device:TPU:0, one launch (start us, length us, event | category | flops | bytes accessed | tf_op | source)
XLA Modules:
  0.0 43.4 jit_solution(8778677724202901640)
XLA Ops:
  0.0 3.0 %collective-permute-start = (bf16[64,3072]{1,0:T(8,128)(2,1)}, bf16[64,3072]{1,0:T(8,128)(2,1)S(1)}, u32[]{:S(2)}, u32[]{:S(2)}) collective-permute-start(bf16[64,3072]{1,0:T(8,128)(2,1)} %bitcast.5), channel_id=1, source_target_pairs={{0,4},{4,0},{8,12},{12,8},{1,5},{5,1},{9,13},{13,9},{2,6},{6,2},{1... | collective-permute-start | bytes 1179656 | tf_op jit(solution)/shard_map/ppermute | solution.py:221
  3.0 17.7 %low_rank_and_base.1 = (f32[16,16,128]{2,1,0:T(8,128)}, bf16[32,3072]{1,0:T(8,128)(2,1)S(1)}, f32[32,3072]{1,0:T(8,128)S(1)}) custom-call(bf16[64,8448]{1,0:T(8,128)(2,1)} %hidden.1, bf16[64,8448]{1,0:T(8,128)(2,1)} %bitcast.8, bf16[8448,3072]{1,0:T(8,128)(2,1)} %weight.1), custom_call_target="tpu_custom_call" | custom-call | flops 3391094784 | bytes 54067200 | tf_op jit(solution)/shard_map/low_rank_and_base/pallas_call | solution.py:104
  20.7 0.0 collective-permute-done.up_there
  20.8 0.1 collective-permute-start.1
  20.8 6.3 %all-to-all-start = ((f32[16,16,128]{2,1,0:T(8,128)}), f32[16,16,128]{2,1,0:T(8,128)S(1)}, u32[]{:S(2)}, u32[]{:S(2)}) async-start(f32[16,16,128]{2,1,0:T(8,128)} %get-tuple-element.12), calls=%async_computation | async-start | bytes 262144 | tf_op jit(solution)/shard_map/all_to_all | solution.py:230
  27.2 0.0 collective-permute-done.1.got
  27.2 0.0 copy-start
  27.2 0.0 copy-start.1
  27.2 0.0 copy-start.2
  27.3 7.8 %all-to-all-done.packed = f32[16,16,128]{2,1,0:T(8,128)S(1)} async-done(((f32[16,16,128]{2,1,0:T(8,128)}), f32[16,16,128]{2,1,0:T(8,128)S(1)}, u32[]{:S(2)}, u32[]{:S(2)}) %all-to-all-start) | async-done | bytes 131104 | tf_op jit(solution)/shard_map/all_to_all | solution.py:230
  35.1 0.0 copy-done
  35.1 0.0 copy-done.1
  35.1 0.0 copy-done.2
  35.1 0.4 %join.1 = (bf16[16,3072]{1,0:T(8,128)(2,1)S(1)}, f32[16,3072]{1,0:T(8,128)S(1)}) custom-call(s32[1,64]{1,0:T(1,128)S(1)} %bitcast.7, f32[16,16,128]{2,1,0:T(8,128)S(1)} %all-to-all-done.packed, bf16[64,3072]{1,0:T(8,128)(2,1)S(1)} %bitcast.6, bf16[64,3072]{1,0:T(8,128)(2,1)S(1)} %collective-permute-done.up_there, f32[32,3072]{1,0:T(8,128)S(1)} %pair_sum.1.pair, ...), custom_call_target="tpu_custom_call" | custom-call | tf_op jit(solution)/shard_map/join/pallas_call | solution.py:191
  35.6 0.5 %collective-permute-start.2 = (bf16[16,3072]{1,0:T(8,128)(2,1)S(1)}, bf16[16,3072]{1,0:T(8,128)(2,1)S(1)}, u32[]{:S(2)}, u32[]{:S(2)}) collective-permute-start(bf16[16,3072]{1,0:T(8,128)(2,1)S(1)} %get-tuple-element.18), channel_id=1, source_target_pairs={{0,8},{4,12},{8,0},{12,4},{1,9},{5,13},{9,1},{13,5},{2,10},{6,14},... | collective-permute-start | bytes 294920 | tf_op jit(solution)/shard_map/ppermute | solution.py:221
  36.1 6.6 %collective-permute-done.2.got = bf16[16,3072]{1,0:T(8,128)(2,1)S(1)} collective-permute-done((bf16[16,3072]{1,0:T(8,128)(2,1)S(1)}, bf16[16,3072]{1,0:T(8,128)(2,1)S(1)}, u32[]{:S(2)}, u32[]{:S(2)}) %collective-permute-start.2) | collective-permute-done | bytes 98336 | tf_op jit(solution)/shard_map/ppermute | solution.py:221
  42.7 0.7 %finish.1 = bf16[16,3072]{1,0:T(8,128)(2,1)} custom-call(f32[16,3072]{1,0:T(8,128)S(1)} %get-tuple-element.17.total, bf16[16,3072]{1,0:T(8,128)(2,1)S(1)} %collective-permute-done.2.got), custom_call_target="tpu_custom_call" | custom-call | tf_op jit(solution)/shard_map/finish/pallas_call | solution.py:210
  (1 shorter events, 0.0 us)
Async XLA Ops:
  0.0 20.7 %collective-permute-start = (bf16[64,3072]{1,0:T(8,128)(2,1)}, bf16[64,3072]{1,0:T(8,128)(2,1)S(1)}, u32[]{:S(2)}, u32[]{:S(2)}) collective-permute-start(bf16[64,3072]{1,0:T(8,128)(2,1)} %bitcast.5), channel_id=1, source_target_pairs={{0,4},{4,0},{8,12},{12,8},{1,5},{5,1},{9,13},{13,9},{2,6},{6,2},{1... | collective-permute-start | bytes 1179656 | tf_op jit(solution)/shard_map/ppermute | solution.py:221
  20.8 6.4 %collective-permute-start.1 = (bf16[32,3072]{1,0:T(8,128)(2,1)S(1)}, bf16[32,3072]{1,0:T(8,128)(2,1)S(1)}, u32[]{:S(2)}, u32[]{:S(2)}) collective-permute-start(bf16[32,3072]{1,0:T(8,128)(2,1)S(1)} %get-tuple-element.16), channel_id=1, source_target_pairs={{0,4},{4,0},{8,12},{12,8},{1,5},{5,1},{9,13},{13,9},{2,6},{6,2},{1... | collective-permute-start | bytes 589832 | tf_op jit(solution)/shard_map/ppermute | solution.py:221
  20.8 14.3 %all-to-all-start = ((f32[16,16,128]{2,1,0:T(8,128)}), f32[16,16,128]{2,1,0:T(8,128)S(1)}, u32[]{:S(2)}, u32[]{:S(2)}) async-start(f32[16,16,128]{2,1,0:T(8,128)} %get-tuple-element.12), calls=%async_computation | async-start | bytes 262144 | tf_op jit(solution)/shard_map/all_to_all | solution.py:230
  27.2 7.9 %copy-start = (bf16[1,64,3072]{2,1,0:T(8,128)(2,1)S(1)}, bf16[1,64,3072]{2,1,0:T(8,128)(2,1)}, u32[]{:S(2)}) copy-start(bf16[1,64,3072]{2,1,0:T(8,128)(2,1)} %param.10) | copy-start | bytes 1179652
  27.2 7.9 %copy-start.1 = (bf16[16,3072]{1,0:T(8,128)(2,1)S(1)}, bf16[16,3072]{1,0:T(8,128)(2,1)}, u32[]{:S(2)}) copy-start(bf16[16,3072]{1,0:T(8,128)(2,1)} %residual.1) | copy-start | bytes 294916
  27.2 7.9 %copy-start.2 = (s32[64]{0:T(128)S(1)}, s32[64]{0:T(128)}, u32[]{:S(2)}) copy-start(s32[64]{0:T(128)} %param.7) | copy-start | bytes 772
  35.6 7.1 %collective-permute-start.2 = (bf16[16,3072]{1,0:T(8,128)(2,1)S(1)}, bf16[16,3072]{1,0:T(8,128)(2,1)S(1)}, u32[]{:S(2)}, u32[]{:S(2)}) collective-permute-start(bf16[16,3072]{1,0:T(8,128)(2,1)S(1)} %get-tuple-element.18), channel_id=1, source_target_pairs={{0,8},{4,12},{8,0},{12,4},{1,9},{5,13},{9,1},{13,5},{2,10},{6,14},... | collective-permute-start | bytes 294920 | tf_op jit(solution)/shard_map/ppermute | solution.py:221

commit v10 on v7

--- a/solution.py
+++ b/solution.py
@@ -62,14 +62,8 @@
         (((1,), (1,)), ((), ())),
         preferred_element_type=jnp.float32,
     )
-    block = low.shape[0] // 4
-    for bit in range(2):
-        wanted = jnp.concatenate(
-            [low[(half + bit) * block : (half + bit + 1) * block] for half in (0, 2)], axis=1
-        )
-        for to in range(packed.shape[0]):
-            if (to // 4) % 2 == bit:
-                packed[to] = wanted
+    half = low.shape[0] // 2
+    packed[...] = jnp.concatenate([low[:half], low[half:]], axis=1)
 
     def add(group, part, depth):
         at = pl.ds(pl.multiple_of(group * deep + part * PART, PART), depth)
@@ -104,7 +98,7 @@
     return pl.pallas_call(
         stream_kernel,
         out_shape=(
-            jax.ShapeDtypeStruct((16, rows // 4, 2 * rank), jnp.float32),
+            jax.ShapeDtypeStruct((rows // 2, 2 * rank), jnp.float32),
             jax.ShapeDtypeStruct((rows // 2, width), jnp.bfloat16),
             jax.ShapeDtypeStruct((rows // 2, width), jnp.float32),
         ),
@@ -139,9 +133,44 @@
         kept[rows, at] = total[here, :]
 
 
-def join_kernel(ids, packed, up_here, up_there, kept, got, residual, sent, total, joined):
+def unpacked(packed):
+    rank = packed.shape[1] // 2
+    return jnp.concatenate([packed[:, :rank], packed[:, rank:]], axis=0)
+
+
+def merge_kernel(ids, own, other, same, flipped):
+    page, sub = lax.axis_index("page"), lax.axis_index("sub")
+    adapter = column_of(ids[...])
+    mine = (2 * page + sub).astype(jnp.float32)
+    theirs = (2 * page + 1 - sub).astype(jnp.float32)
+    low = jnp.where(
+        adapter == mine,
+        unpacked(own[...]),
+        jnp.where(adapter == theirs, unpacked(other[...]), 0.0),
+    )
+    block = low.shape[0] // 4
+    rows = [low[index * block : (index + 1) * block] for index in range(4)]
+    even = jnp.concatenate([rows[0], rows[2]], axis=1)
+    odd = jnp.concatenate([rows[1], rows[3]], axis=1)
+    bit = lax.rem(lax.axis_index("tp"), 2)
+    same[...] = jnp.where(bit == 0, even, odd)
+    flipped[...] = jnp.where(bit == 0, odd, even)
+
+
+def merge_phase(ids, own, other):
+    shape = jax.ShapeDtypeStruct((own.shape[0] // 2, own.shape[1]), own.dtype)
+    return pl.pallas_call(
+        merge_kernel,
+        out_shape=(shape, shape),
+        in_specs=[VMEM] * 3,
+        out_specs=(VMEM,) * 2,
+        compiler_params=pltpu.CompilerParams(vmem_limit_bytes=4 << 20),
+        name="merge_low_rank",
+    )(ids, own, other)
+
+
+def join_kernel(ids, near, far, up_here, up_there, kept, got, residual, sent, total, joined):
     block = residual.shape[0]
-    rank = up_here.shape[0]
     tp = lax.axis_index("tp")
     high, bit = lax.div(tp, 2), lax.rem(tp, 2)
     every = column_of(ids[...])
@@ -149,14 +178,11 @@
     adapter = jnp.concatenate(
         [jnp.where(bit == 0, parts[half], parts[half + 1]) for half in (0, 2)], axis=0
     )
-    coefficient = []
-    for index in (tp, tp + 1 - 2 * bit):
-        low = packed[index]
-        for source in range(1, 4):
-            low = low + packed[4 * source + index]
-        low = jnp.concatenate([low[:, :rank], low[:, rank:]], axis=0)
-        low = jnp.where(adapter == index.astype(jnp.float32), low, 0.0)
-        coefficient.append(low.astype(jnp.bfloat16))
+    low = unpacked(near[...] + far[...])
+    coefficient = [
+        jnp.where(adapter == index.astype(jnp.float32), low, 0.0).astype(jnp.bfloat16)
+        for index in (tp, tp + 1 - 2 * bit)
+    ]
     width = residual.shape[1]
     for start in range(0, width, TILE):
         at = slice(start, start + TILE)
@@ -166,25 +192,25 @@
             + jnp.dot(coefficient[0], up_here[:, at], preferred_element_type=jnp.float32)
             + jnp.dot(coefficient[1], up_there[:, at], preferred_element_type=jnp.float32)
         )
-    near = pl.ds(pl.multiple_of(high * block, block), block)
-    far = pl.ds(pl.multiple_of((1 - high) * block, block), block)
-    sent[...] = joined[far, :].astype(sent.dtype)
-    total[...] = joined[near, :] + residual[...].astype(jnp.float32)
-
-
-def join_phase(ids, packed, up_here, up_there, kept, got, residual):
+    here = pl.ds(pl.multiple_of(high * block, block), block)
+    there = pl.ds(pl.multiple_of((1 - high) * block, block), block)
+    sent[...] = joined[there, :].astype(sent.dtype)
+    total[...] = joined[here, :] + residual[...].astype(jnp.float32)
+
+
+def join_phase(ids, near, far, up_here, up_there, kept, got, residual):
     return pl.pallas_call(
         join_kernel,
         out_shape=(
             jax.ShapeDtypeStruct(residual.shape, jnp.bfloat16),
             jax.ShapeDtypeStruct(residual.shape, jnp.float32),
         ),
-        in_specs=[VMEM] * 7,
+        in_specs=[VMEM] * 8,
         out_specs=(VMEM,) * 2,
         scratch_shapes=[pltpu.VMEM(kept.shape, kept.dtype)],
         compiler_params=pltpu.CompilerParams(vmem_limit_bytes=8 << 20),
         name="join",
-    )(ids, packed, up_here, up_there, kept, got, residual)
+    )(ids, near, far, up_here, up_there, kept, got, residual)
 
 
 def finish_kernel(total, got, mixed):
@@ -202,18 +228,31 @@
     )(total, got)
 
 
-def swap(value, bit):
-    return lax.ppermute(value, "tp", [(i, i ^ bit) for i in range(lax.axis_size("tp"))])
+def swap(value, axis, bit=1):
+    return lax.ppermute(value, axis, [(i, i ^ bit) for i in range(lax.axis_size(axis))])
+
+
+def to_holders(value, flip):
+    pairs = []
+    for tp in range(4):
+        for page in range(2):
+            for sub in range(2):
+                to = (2 * page + (tp % 2 ^ flip), tp // 2 ^ sub, sub)
+                pairs.append((4 * tp + 2 * page + sub, 4 * to[0] + 2 * to[1] + to[2]))
+    return lax.ppermute(value, ("tp",) + PS, pairs)
 
 
 def four_by_four(hidden, adapter_ids, weight, rank_down, rank_up, residual):
+    ids = adapter_ids[None]
     up = rank_up[0]
-    up_there = swap(up, 1)
+    up_there = swap(up, "tp", 1)
     packed, sent, kept = stream_phase(hidden, jnp.swapaxes(rank_down, 1, 2)[0], weight)
-    got = swap(sent, 1)
-    packed = lax.all_to_all(packed, ("tp",) + PS, split_axis=0, concat_axis=0, tiled=True)
-    sent, total = join_phase(adapter_ids[None], packed, up, up_there, kept, got, residual)
-    return finish_phase(total, swap(sent, 2))
+    sent, up_there = lax.optimization_barrier((sent, up_there))
+    got = swap(sent, "tp", 1)
+    same, flipped = merge_phase(ids, packed, swap(packed, "sub"))
+    low = to_holders(same, 0) + to_holders(flipped, 1)
+    sent, total = join_phase(ids, low, swap(low, "sub"), up, up_there, kept, got, residual)
+    return finish_phase(total, swap(sent, "tp", 2))
 
 
 def any_size(hidden_units, adapter_ids, down_projection_weight, rank_down, rank_up, residual):

time: 43.9 us -> 41.6 us (0.948)
  the two profiles are of different devices: /device:TPU:0 before, /device:TPU:3 now
where the time goes in v10:
time: 41.6 us; the launch traced here: 41.5 us
  Pallas kernels  18.7 us (45%)
  starting transfers between devices  11.9 us (29%)
  waiting for transfers between devices  10.8 us (26%)
    pallas_call x1, Pallas kernels, stream_phase(): pl.pallas_call(stream_kernel, out_shape=(jax.ShapeDtypeStruct((rows // 2,...  17.5 us
    ppermute x5, waiting for transfers between devices, swap(): lax.ppermute(value, axis, [(i, i ^ bit) for i in range(lax.axis_size(axis...  8.61 us
    ppermute x5, starting transfers between devices, swap(): lax.ppermute(value, axis, [(i, i ^ bit) for i in range(lax.axis_size(axis...  6.39 us
    ppermute x2, starting transfers between devices, to_holders(): return lax.ppermute(value, ('tp',) + PS, pairs)  5.53 us
    ppermute x2, waiting for transfers between devices, to_holders(): return lax.ppermute(value, ('tp',) + PS, pairs)  2.14 us
  transfers between devices with their start and end apart: 7, of which 4 were waited for; matrix products, arithmetic and copies ran while one was open for 0% of the time, Pallas kernels for 43%

profile of v10, /device:TPU:3, one launch (start us, length us, event | category | flops | bytes accessed | tf_op | source)
XLA Modules:
  0.0 41.5 jit_solution(9642865584893953783)
XLA Ops:
  0.0 1.3 %collective-permute-start.4 = (bf16[64,3072]{1,0:T(8,128)(2,1)}, bf16[64,3072]{1,0:T(8,128)(2,1)S(1)}, u32[]{:S(2)}, u32[]{:S(2)}) collective-permute-start(bf16[64,3072]{1,0:T(8,128)(2,1)} %bitcast.5), channel_id=1, source_target_pairs={{0,4},{4,0},{8,12},{12,8},{1,5},{5,1},{9,13},{13,9},{2,6},{6,2},{1... | collective-permute-start | bytes 1179656 | tf_op jit(solution)/shard_map/ppermute | solution.py:232
  1.3 0.0 copy-start.2
  1.3 0.0 copy-start
  1.3 0.0 copy-start.1
  1.3 17.5 %low_rank_and_base.1 = (f32[32,128]{1,0:T(8,128)S(1)}, bf16[32,3072]{1,0:T(8,128)(2,1)S(1)}, f32[32,3072]{1,0:T(8,128)S(1)}) custom-call(bf16[64,8448]{1,0:T(8,128)(2,1)} %hidden.1, bf16[64,8448]{1,0:T(8,128)(2,1)} %bitcast.9, bf16[8448,3072]{1,0:T(8,128)(2,1)} %weight.1), custom_call_target="tpu_custom_call" | custom-call | flops 3391094784 | bytes 54067200 | tf_op jit(solution)/shard_map/low_rank_and_base/pallas_call | solution.py:98
  18.8 0.0 collective-permute-done.4.up_there
  18.8 0.2 collective-permute-start.5
  19.0 1.2 %collective-permute-start = (f32[32,128]{1,0:T(8,128)S(1)}, f32[32,128]{1,0:T(8,128)S(1)}, u32[]{:S(2)}, u32[]{:S(2)}) collective-permute-start(f32[32,128]{1,0:T(8,128)S(1)} %get-tuple-element.14.own), channel_id=1, source_target_pairs={{0,1},{1,0},{2,3},{3,2},{4,5},{5,4},{6,7},{7,6},{8,9},{9,8},{10,11... | collective-permute-start | bytes 49160 | tf_op jit(solution)/shard_map/ppermute | solution.py:232
  20.3 0.8 %collective-permute-done.other = f32[32,128]{1,0:T(8,128)S(1)} collective-permute-done((f32[32,128]{1,0:T(8,128)S(1)}, f32[32,128]{1,0:T(8,128)S(1)}, u32[]{:S(2)}, u32[]{:S(2)}) %collective-permute-start) | collective-permute-done | bytes 16416 | tf_op jit(solution)/shard_map/ppermute | solution.py:232
  21.1 0.0 copy-done.2
  21.1 0.2 merge_low_rank.1
  21.3 4.2 %collective-permute-start.1 = (f32[16,128]{1,0:T(8,128)S(1)}, f32[16,128]{1,0:T(8,128)S(1)}, u32[]{:S(2)}, u32[]{:S(2)}) collective-permute-start(f32[16,128]{1,0:T(8,128)S(1)} %get-tuple-element.15), channel_id=1, source_target_pairs={{0,0},{1,3},{2,8},{3,11},{4,4},{5,7},{6,12},{7,15},{8,2},{9,1},{10... | collective-permute-start | bytes 24584 | tf_op jit(solution)/shard_map/ppermute | solution.py:242
  25.5 1.3 %collective-permute-start.2 = (f32[16,128]{1,0:T(8,128)S(1)}, f32[16,128]{1,0:T(8,128)S(1)}, u32[]{:S(2)}, u32[]{:S(2)}) collective-permute-start(f32[16,128]{1,0:T(8,128)S(1)} %get-tuple-element.16), channel_id=1, source_target_pairs={{0,4},{1,7},{2,12},{3,15},{4,0},{5,3},{6,8},{7,11},{8,6},{9,5},{10... | collective-permute-start | bytes 24584 | tf_op jit(solution)/shard_map/ppermute | solution.py:242
  26.8 0.0 collective-permute-done.1
  26.8 2.1 %collective-permute-done.2 = f32[16,128]{1,0:T(8,128)S(1)} collective-permute-done((f32[16,128]{1,0:T(8,128)S(1)}, f32[16,128]{1,0:T(8,128)S(1)}, u32[]{:S(2)}, u32[]{:S(2)}) %collective-permute-start.2) | collective-permute-done | bytes 8224 | tf_op jit(solution)/shard_map/ppermute | solution.py:242
  29.0 3.5 %collective-permute-start.3 = (f32[16,128]{1,0:T(8,128)S(1)}, f32[16,128]{1,0:T(8,128)S(1)}, u32[]{:S(2)}, u32[]{:S(2)}) collective-permute-start(f32[16,128]{1,0:T(8,128)S(1)} %add.3.near), channel_id=1, source_target_pairs={{0,1},{1,0},{2,3},{3,2},{4,5},{5,4},{6,7},{7,6},{8,9},{9,8},{10,11... | collective-permute-start | bytes 24584 | tf_op jit(solution)/shard_map/ppermute | solution.py:232
  32.5 0.8 %collective-permute-done.3.far = f32[16,128]{1,0:T(8,128)S(1)} collective-permute-done((f32[16,128]{1,0:T(8,128)S(1)}, f32[16,128]{1,0:T(8,128)S(1)}, u32[]{:S(2)}, u32[]{:S(2)}) %collective-permute-start.3) | collective-permute-done | bytes 8224 | tf_op jit(solution)/shard_map/ppermute | solution.py:232
  33.3 0.0 collective-permute-done.5.got
  33.3 0.0 copy-done
  33.3 0.0 copy-done.1
  33.3 0.4 %join.1 = (bf16[16,3072]{1,0:T(8,128)(2,1)S(1)}, f32[16,3072]{1,0:T(8,128)S(1)}) custom-call(s32[1,64]{1,0:T(1,128)S(1)} %bitcast.8, f32[16,128]{1,0:T(8,128)S(1)} %add.3.near, f32[16,128]{1,0:T(8,128)S(1)} %collective-permute-done.3.far, bf16[64,3072]{1,0:T(8,128)(2,1)S(1)} %bitcast.6, bf16[64,3072]{1,0:T(8,128)(2,1)S(1)} %collective-permute-done.4.up_there, ...), custom_call_target="tpu_custom_call" | custom-call | tf_op jit(solution)/shard_map/join/pallas_call | solution.py:202
  33.8 0.1 collective-permute-start.6
  33.9 6.9 %collective-permute-done.6.got = bf16[16,3072]{1,0:T(8,128)(2,1)S(1)} collective-permute-done((bf16[16,3072]{1,0:T(8,128)(2,1)S(1)}, bf16[16,3072]{1,0:T(8,128)(2,1)S(1)}, u32[]{:S(2)}, u32[]{:S(2)}) %collective-permute-start.6) | collective-permute-done | bytes 98336 | tf_op jit(solution)/shard_map/ppermute | solution.py:232
  40.8 0.7 %finish.1 = bf16[16,3072]{1,0:T(8,128)(2,1)} custom-call(f32[16,3072]{1,0:T(8,128)S(1)} %get-tuple-element.21.total, bf16[16,3072]{1,0:T(8,128)(2,1)S(1)} %collective-permute-done.6.got), custom_call_target="tpu_custom_call" | custom-call | tf_op jit(solution)/shard_map/finish/pallas_call | solution.py:221
  (1 shorter events, 0.0 us)
Async XLA Ops:
  0.0 18.8 %collective-permute-start.4 = (bf16[64,3072]{1,0:T(8,128)(2,1)}, bf16[64,3072]{1,0:T(8,128)(2,1)S(1)}, u32[]{:S(2)}, u32[]{:S(2)}) collective-permute-start(bf16[64,3072]{1,0:T(8,128)(2,1)} %bitcast.5), channel_id=1, source_target_pairs={{0,4},{4,0},{8,12},{12,8},{1,5},{5,1},{9,13},{13,9},{2,6},{6,2},{1... | collective-permute-start | bytes 1179656 | tf_op jit(solution)/shard_map/ppermute | solution.py:232
  1.3 19.8 %copy-start.2 = (s32[64]{0:T(128)S(1)}, s32[64]{0:T(128)}, u32[]{:S(2)}) copy-start(s32[64]{0:T(128)} %param.7) | copy-start | bytes 772
  1.3 32.0 %copy-start = (bf16[1,64,3072]{2,1,0:T(8,128)(2,1)S(1)}, bf16[1,64,3072]{2,1,0:T(8,128)(2,1)}, u32[]{:S(2)}) copy-start(bf16[1,64,3072]{2,1,0:T(8,128)(2,1)} %param.10) | copy-start | bytes 1179652
  1.3 32.0 %copy-start.1 = (bf16[16,3072]{1,0:T(8,128)(2,1)S(1)}, bf16[16,3072]{1,0:T(8,128)(2,1)}, u32[]{:S(2)}) copy-start(bf16[16,3072]{1,0:T(8,128)(2,1)} %residual.1) | copy-start | bytes 294916
  18.8 14.5 %collective-permute-start.5 = (bf16[32,3072]{1,0:T(8,128)(2,1)S(1)}, bf16[32,3072]{1,0:T(8,128)(2,1)S(1)}, u32[]{:S(2)}, u32[]{:S(2)}) collective-permute-start(bf16[32,3072]{1,0:T(8,128)(2,1)S(1)} %get-tuple-element.20), channel_id=1, source_target_pairs={{0,4},{4,0},{8,12},{12,8},{1,5},{5,1},{9,13},{13,9},{2,6},{6,2},{1... | collective-permute-start | bytes 589832 | tf_op jit(solution)/shard_map/ppermute | solution.py:232
  19.0 2.1 %collective-permute-start = (f32[32,128]{1,0:T(8,128)S(1)}, f32[32,128]{1,0:T(8,128)S(1)}, u32[]{:S(2)}, u32[]{:S(2)}) collective-permute-start(f32[32,128]{1,0:T(8,128)S(1)} %get-tuple-element.14.own), channel_id=1, source_target_pairs={{0,1},{1,0},{2,3},{3,2},{4,5},{5,4},{6,7},{7,6},{8,9},{9,8},{10,11... | collective-permute-start | bytes 49160 | tf_op jit(solution)/shard_map/ppermute | solution.py:232
  21.3 5.5 %collective-permute-start.1 = (f32[16,128]{1,0:T(8,128)S(1)}, f32[16,128]{1,0:T(8,128)S(1)}, u32[]{:S(2)}, u32[]{:S(2)}) collective-permute-start(f32[16,128]{1,0:T(8,128)S(1)} %get-tuple-element.15), channel_id=1, source_target_pairs={{0,0},{1,3},{2,8},{3,11},{4,4},{5,7},{6,12},{7,15},{8,2},{9,1},{10... | collective-permute-start | bytes 24584 | tf_op jit(solution)/shard_map/ppermute | solution.py:242
  25.5 3.5 %collective-permute-start.2 = (f32[16,128]{1,0:T(8,128)S(1)}, f32[16,128]{1,0:T(8,128)S(1)}, u32[]{:S(2)}, u32[]{:S(2)}) collective-permute-start(f32[16,128]{1,0:T(8,128)S(1)} %get-tuple-element.16), channel_id=1, source_target_pairs={{0,4},{1,7},{2,12},{3,15},{4,0},{5,3},{6,8},{7,11},{8,6},{9,5},{10... | collective-permute-start | bytes 24584 | tf_op jit(solution)/shard_map/ppermute | solution.py:242
  29.0 4.4 %collective-permute-start.3 = (f32[16,128]{1,0:T(8,128)S(1)}, f32[16,128]{1,0:T(8,128)S(1)}, u32[]{:S(2)}, u32[]{:S(2)}) collective-permute-start(f32[16,128]{1,0:T(8,128)S(1)} %add.3.near), channel_id=1, source_target_pairs={{0,1},{1,0},{2,3},{3,2},{4,5},{5,4},{6,7},{7,6},{8,9},{9,8},{10,11... | collective-permute-start | bytes 24584 | tf_op jit(solution)/shard_map/ppermute | solution.py:232
  33.8 7.0 %collective-permute-start.6 = (bf16[16,3072]{1,0:T(8,128)(2,1)S(1)}, bf16[16,3072]{1,0:T(8,128)(2,1)S(1)}, u32[]{:S(2)}, u32[]{:S(2)}) collective-permute-start(bf16[16,3072]{1,0:T(8,128)(2,1)S(1)} %get-tuple-element.22), channel_id=1, source_target_pairs={{0,8},{4,12},{8,0},{12,4},{1,9},{5,13},{9,1},{13,5},{2,10},{6,14},... | collective-permute-start | bytes 294920 | tf_op jit(solution)/shard_map/ppermute | solution.py:232

commit v11 on v10

--- a/solution.py
+++ b/solution.py
@@ -9,7 +9,8 @@
 
 PART = 256
 GROUP = 3
-SLOTS = 6
+SLOTS = 5
+HELD = 3
 TILE = 512
 PS = ("page", "sub")
 VMEM = pl.BlockSpec(memory_space=pltpu.VMEM)
@@ -26,9 +27,51 @@
     )
 
 
-def stream_kernel(
-    hidden, rank_down, weight, packed, sent, kept, hidden_here, down_here, total, held, got, arrived
-):
+def low_kernel(hidden, rank_down, packed, hidden_here, down_here, got):
+    copies = [
+        pltpu.make_async_copy(hidden, hidden_here, got.at[0]),
+        pltpu.make_async_copy(rank_down, down_here, got.at[1]),
+    ]
+    for copy in copies:
+        copy.start()
+    for copy in copies:
+        copy.wait()
+    low = lax.dot_general(
+        hidden_here[...],
+        down_here[...],
+        (((1,), (1,)), ((), ())),
+        preferred_element_type=jnp.float32,
+    )
+    half = low.shape[0] // 2
+    packed[...] = jnp.concatenate([low[:half], low[half:]], axis=1)
+
+
+def low_phase(hidden, rank_down):
+    rows, depth = hidden.shape
+    rank = rank_down.shape[0]
+    return pl.pallas_call(
+        low_kernel,
+        out_shape=(
+            jax.ShapeDtypeStruct((rows // 2, 2 * rank), jnp.float32),
+            jax.ShapeDtypeStruct(hidden.shape, hidden.dtype),
+        ),
+        in_specs=[HBM] * 2,
+        out_specs=(VMEM,) * 2,
+        scratch_shapes=[
+            pltpu.VMEM(rank_down.shape, rank_down.dtype),
+            pltpu.SemaphoreType.DMA((2,)),
+        ],
+        compiler_params=pltpu.CompilerParams(vmem_limit_bytes=52 << 20),
+        cost_estimate=pl.CostEstimate(
+            flops=2 * rows * depth * rank,
+            bytes_accessed=2 * depth * (rank + rows),
+            transcendentals=0,
+        ),
+        name="low_rank",
+    )(hidden, rank_down)
+
+
+def stream_kernel(hidden, slab, weight, sent, kept, total, held, arrived):
     groups = weight.shape[0] // (PART * GROUP)
     width = weight.shape[1]
     deep = PART * GROUP
@@ -41,40 +84,33 @@
             weight.at[rows], held.at[there], arrived.at[slot * GROUP + part]
         )
 
-    first = [
-        pltpu.make_async_copy(hidden, hidden_here, got.at[0]),
-        pltpu.make_async_copy(rank_down, down_here, got.at[1]),
-    ]
-    for copy in first:
-        copy.start()
-
-    @pl.loop(0, SLOTS - 1)
+    @pl.loop(HELD, HELD + SLOTS - 1)
     def _(group):
         for part in range(GROUP):
             part_copy(group, part).start()
 
     total[...] = jnp.zeros_like(total)
-    for copy in first:
-        copy.wait()
-    low = lax.dot_general(
-        hidden_here[...],
-        down_here[...],
-        (((1,), (1,)), ((), ())),
-        preferred_element_type=jnp.float32,
-    )
-    half = low.shape[0] // 2
-    packed[...] = jnp.concatenate([low[:half], low[half:]], axis=1)
-
-    def add(group, part, depth):
-        at = pl.ds(pl.multiple_of(group * deep + part * PART, PART), depth)
-        slot = pl.ds(pl.multiple_of(lax.rem(group, SLOTS) * deep + part * PART, PART), depth)
+
+    def add(rows, at, depth):
         for start in range(0, width, TILE):
             columns = slice(start, start + TILE)
             total[:, columns] += jnp.dot(
-                hidden_here[:, at], held[slot, columns], preferred_element_type=jnp.float32
+                hidden[:, pl.ds(at, depth)],
+                rows[:, columns],
+                preferred_element_type=jnp.float32,
             )
 
-    @pl.loop(0, groups - 1)
+    @pl.loop(0, HELD)
+    def _(group):
+        at = pl.multiple_of(group * deep, deep)
+        add(slab.at[pl.ds(at, deep)], at, deep)
+
+    def add_part(group, part, depth):
+        at = pl.multiple_of(group * deep + part * PART, PART)
+        slot = pl.multiple_of(lax.rem(group, SLOTS) * deep + part * PART, PART)
+        add(held.at[pl.ds(slot, depth)], at, depth)
+
+    @pl.loop(HELD, groups - 1)
     def _(group):
         @pl.when(group + SLOTS - 1 < groups)
         def _():
@@ -83,43 +119,36 @@
 
         for part in range(GROUP):
             part_copy(group, part).wait()
-        add(group, 0, deep)
+        add_part(group, 0, deep)
 
     for part in range(GROUP):
         part_copy(groups - 1, part).wait()
-        add(groups - 1, part, PART)
+        add_part(groups - 1, part, PART)
     split_rows(total, slice(0, width), sent, kept)
 
 
-def stream_phase(hidden, rank_down, weight):
+def stream_phase(hidden, weight):
     rows, depth = hidden.shape
-    rank = rank_down.shape[0]
     width = weight.shape[1]
     return pl.pallas_call(
         stream_kernel,
         out_shape=(
-            jax.ShapeDtypeStruct((rows // 2, 2 * rank), jnp.float32),
             jax.ShapeDtypeStruct((rows // 2, width), jnp.bfloat16),
             jax.ShapeDtypeStruct((rows // 2, width), jnp.float32),
         ),
-        in_specs=[HBM] * 3,
-        out_specs=(VMEM,) * 3,
+        in_specs=[VMEM, VMEM, HBM],
+        out_specs=(VMEM,) * 2,
         scratch_shapes=[
-            pltpu.VMEM(hidden.shape, hidden.dtype),
-            pltpu.VMEM(rank_down.shape, rank_down.dtype),
             pltpu.VMEM((rows, width), jnp.float32),
             pltpu.VMEM((SLOTS * GROUP * PART, width), weight.dtype),
-            pltpu.SemaphoreType.DMA((2,)),
             pltpu.SemaphoreType.DMA((SLOTS * GROUP,)),
         ],
-        compiler_params=pltpu.CompilerParams(vmem_limit_bytes=53 << 20),
+        compiler_params=pltpu.CompilerParams(vmem_limit_bytes=28 << 20),
         cost_estimate=pl.CostEstimate(
-            flops=2 * rows * depth * (width + rank),
-            bytes_accessed=2 * depth * (width + rank + rows),
-            transcendentals=0,
-        ),
-        name="low_rank_and_base",
-    )(hidden, rank_down, weight)
+            flops=2 * rows * depth * width, bytes_accessed=2 * depth * width, transcendentals=0
+        ),
+        name="base",
+    )(hidden, weight[: HELD * GROUP * PART], weight)
 
 
 def split_rows(total, at, sent, kept):
@@ -245,12 +274,14 @@
 def four_by_four(hidden, adapter_ids, weight, rank_down, rank_up, residual):
     ids = adapter_ids[None]
     up = rank_up[0]
+    packed, hidden = low_phase(hidden, jnp.swapaxes(rank_down, 1, 2)[0])
     up_there = swap(up, "tp", 1)
-    packed, sent, kept = stream_phase(hidden, jnp.swapaxes(rank_down, 1, 2)[0], weight)
-    sent, up_there = lax.optimization_barrier((sent, up_there))
+    same, flipped = merge_phase(ids, packed, swap(packed, "sub"))
+    low, flipped = to_holders(same, 0), to_holders(flipped, 1)
+    sent, kept = stream_phase(hidden, weight)
+    sent, up_there, low, flipped = lax.optimization_barrier((sent, up_there, low, flipped))
     got = swap(sent, "tp", 1)
-    same, flipped = merge_phase(ids, packed, swap(packed, "sub"))
-    low = to_holders(same, 0) + to_holders(flipped, 1)
+    low = low + flipped
     sent, total = join_phase(ids, low, swap(low, "sub"), up, up_there, kept, got, residual)
     return finish_phase(total, swap(sent, "tp", 2))
 

time: 41.6 us -> 45.1 us (1.084)
  the two profiles are of different devices: /device:TPU:3 before, /device:TPU:0 now
where the time goes in v11:
time: 45.1 us; the launch traced here: 45 us
  Pallas kernels  16.2 us (36%)
  starting transfers between devices  15.8 us (35%)
  local copies, waits for them, and re-layouts  7.36 us (16%)
  waiting for transfers between devices  5.43 us (12%)
    ppermute x5, starting transfers between devices, swap(): lax.ppermute(value, axis, [(i, i ^ bit) for i in range(lax.axis_size(axis...  15.1 us
    pallas_call x1, Pallas kernels, stream_phase(): pl.pallas_call(stream_kernel, out_shape=(jax.ShapeDtypeStruct((rows // 2,...  12.9 us
    slice x1, local copies, waits for them, and re-layouts, stream_phase(): weight[:HELD * GROUP * PART]  7.34 us
    ppermute x5, waiting for transfers between devices, swap(): lax.ppermute(value, axis, [(i, i ^ bit) for i in range(lax.axis_size(axis...  5.42 us
    pallas_call x1, Pallas kernels, low_phase(): pl.pallas_call(low_kernel, out_shape=(jax.ShapeDtypeStruct((rows // 2, 2...  2.09 us
  transfers between devices with their start and end apart: 7, of which 2 were waited for; matrix products, arithmetic and copies ran while one was open for 16% of the time, Pallas kernels for 34%

profile of v11, /device:TPU:0, one launch (start us, length us, event | category | flops | bytes accessed | tf_op | source)
XLA Modules:
  0.0 45.0 jit_solution(8547000816559455600)
XLA Ops:
  0.0 3.0 %collective-permute-start = (bf16[64,3072]{1,0:T(8,128)(2,1)}, bf16[64,3072]{1,0:T(8,128)(2,1)S(1)}, u32[]{:S(2)}, u32[]{:S(2)}) collective-permute-start(bf16[64,3072]{1,0:T(8,128)(2,1)} %bitcast.5), channel_id=1, source_target_pairs={{0,4},{4,0},{8,12},{12,8},{1,5},{5,1},{9,13},{13,9},{2,6},{6,2},{1... | collective-permute-start | bytes 1179656 | tf_op jit(solution)/shard_map/ppermute | solution.py:261
  3.0 2.1 %low_rank.1 = (f32[32,128]{1,0:T(8,128)S(1)}, bf16[64,8448]{1,0:T(8,128)(2,1)S(1)}) custom-call(bf16[64,8448]{1,0:T(8,128)(2,1)} %hidden.1, bf16[64,8448]{1,0:T(8,128)(2,1)} %bitcast.9), custom_call_target="tpu_custom_call" | custom-call | flops 69206016 | bytes 2162688 | tf_op jit(solution)/shard_map/low_rank/pallas_call | solution.py:52
  5.1 0.0 copy-start.2
  5.1 0.1 collective-permute-start.1
  5.2 7.3 %slice.3.slab = bf16[2304,3072]{1,0:T(8,128)(2,1)S(1)} slice(bf16[8448,3072]{1,0:T(8,128)(2,1)} %weight.1), slice={[0:2304], [0:3072]} | slice | bytes 28311552 | tf_op jit(solution)/shard_map/slice | solution.py:151
  12.6 0.0 collective-permute-done.1.other
  12.6 0.0 copy-done.2
  12.6 0.2 merge_low_rank.1
  12.7 0.7 %collective-permute-start.2 = (f32[16,128]{1,0:T(8,128)S(1)}, f32[16,128]{1,0:T(8,128)S(1)}, u32[]{:S(2)}, u32[]{:S(2)}) collective-permute-start(f32[16,128]{1,0:T(8,128)S(1)} %get-tuple-element.20), channel_id=1, source_target_pairs={{0,0},{1,3},{2,8},{3,11},{4,4},{5,7},{6,12},{7,15},{8,2},{9,1},{10... | collective-permute-start | bytes 24584 | tf_op jit(solution)/shard_map/ppermute | solution.py:271
  13.4 0.1 collective-permute-start.3
  13.5 0.0 copy-start
  13.5 0.0 copy-start.1
  13.5 12.9 %base.1 = (bf16[32,3072]{1,0:T(8,128)(2,1)S(1)}, f32[32,3072]{1,0:T(8,128)S(1)}) custom-call(bf16[64,8448]{1,0:T(8,128)(2,1)S(1)} %get-tuple-element.17.hidden, bf16[2304,3072]{1,0:T(8,128)(2,1)S(1)} %slice.3.slab, bf16[8448,3072]{1,0:T(8,128)(2,1)} %weight.1), custom_call_target="tpu_custom_call" | custom-call | flops 3321888768 | bytes 51904512 | tf_op jit(solution)/shard_map/base/pallas_call | solution.py:133
  26.4 0.0 collective-permute-done.2
  26.4 0.0 collective-permute-done.3
  26.4 0.0 collective-permute-done.up_there
  26.4 2.1 %collective-permute-start.5 = (bf16[32,3072]{1,0:T(8,128)(2,1)S(1)}, bf16[32,3072]{1,0:T(8,128)(2,1)S(1)}, u32[]{:S(2)}, u32[]{:S(2)}) collective-permute-start(bf16[32,3072]{1,0:T(8,128)(2,1)S(1)} %get-tuple-element.26), channel_id=1, source_target_pairs={{0,4},{4,0},{8,12},{12,8},{1,5},{5,1},{9,13},{13,9},{2,6},{6,2},{1... | collective-permute-start | bytes 589832 | tf_op jit(solution)/shard_map/ppermute | solution.py:261
  28.5 4.4 %collective-permute-start.4 = (f32[16,128]{1,0:T(8,128)S(1)}, f32[16,128]{1,0:T(8,128)S(1)}, u32[]{:S(2)}, u32[]{:S(2)}) collective-permute-start(f32[16,128]{1,0:T(8,128)S(1)} %add.3.near), channel_id=1, source_target_pairs={{0,1},{1,0},{2,3},{3,2},{4,5},{5,4},{6,7},{7,6},{8,9},{9,8},{10,11... | collective-permute-start | bytes 24584 | tf_op jit(solution)/shard_map/ppermute | solution.py:261
  32.9 0.8 %collective-permute-done.4.far = f32[16,128]{1,0:T(8,128)S(1)} collective-permute-done((f32[16,128]{1,0:T(8,128)S(1)}, f32[16,128]{1,0:T(8,128)S(1)}, u32[]{:S(2)}, u32[]{:S(2)}) %collective-permute-start.4) | collective-permute-done | bytes 8224 | tf_op jit(solution)/shard_map/ppermute | solution.py:261
  33.7 0.0 collective-permute-done.5.got
  33.7 0.0 copy-done
  33.7 0.0 copy-done.1
  33.7 0.4 join.1
  34.1 5.6 %collective-permute-start.6 = (bf16[16,3072]{1,0:T(8,128)(2,1)S(1)}, bf16[16,3072]{1,0:T(8,128)(2,1)S(1)}, u32[]{:S(2)}, u32[]{:S(2)}) collective-permute-start(bf16[16,3072]{1,0:T(8,128)(2,1)S(1)} %get-tuple-element.28), channel_id=1, source_target_pairs={{0,8},{4,12},{8,0},{12,4},{1,9},{5,13},{9,1},{13,5},{2,10},{6,14},... | collective-permute-start | bytes 294920 | tf_op jit(solution)/shard_map/ppermute | solution.py:261
  39.7 4.6 %collective-permute-done.6.got = bf16[16,3072]{1,0:T(8,128)(2,1)S(1)} collective-permute-done((bf16[16,3072]{1,0:T(8,128)(2,1)S(1)}, bf16[16,3072]{1,0:T(8,128)(2,1)S(1)}, u32[]{:S(2)}, u32[]{:S(2)}) %collective-permute-start.6) | collective-permute-done | bytes 98336 | tf_op jit(solution)/shard_map/ppermute | solution.py:261
  44.3 0.7 %finish.1 = bf16[16,3072]{1,0:T(8,128)(2,1)} custom-call(f32[16,3072]{1,0:T(8,128)S(1)} %get-tuple-element.27.total, bf16[16,3072]{1,0:T(8,128)(2,1)S(1)} %collective-permute-done.6.got), custom_call_target="tpu_custom_call" | custom-call | tf_op jit(solution)/shard_map/finish/pallas_call | solution.py:250
  (1 shorter events, 0.0 us)
Async XLA Ops:
  0.0 26.4 %collective-permute-start = (bf16[64,3072]{1,0:T(8,128)(2,1)}, bf16[64,3072]{1,0:T(8,128)(2,1)S(1)}, u32[]{:S(2)}, u32[]{:S(2)}) collective-permute-start(bf16[64,3072]{1,0:T(8,128)(2,1)} %bitcast.5), channel_id=1, source_target_pairs={{0,4},{4,0},{8,12},{12,8},{1,5},{5,1},{9,13},{13,9},{2,6},{6,2},{1... | collective-permute-start | bytes 1179656 | tf_op jit(solution)/shard_map/ppermute | solution.py:261
  5.1 7.5 %copy-start.2 = (s32[64]{0:T(128)S(1)}, s32[64]{0:T(128)}, u32[]{:S(2)}) copy-start(s32[64]{0:T(128)} %param.7) | copy-start | bytes 772
  5.1 7.4 %collective-permute-start.1 = (f32[32,128]{1,0:T(8,128)S(1)}, f32[32,128]{1,0:T(8,128)S(1)}, u32[]{:S(2)}, u32[]{:S(2)}) collective-permute-start(f32[32,128]{1,0:T(8,128)S(1)} %get-tuple-element.19.own), channel_id=1, source_target_pairs={{0,1},{1,0},{2,3},{3,2},{4,5},{5,4},{6,7},{7,6},{8,9},{9,8},{10,11... | collective-permute-start | bytes 49160 | tf_op jit(solution)/shard_map/ppermute | solution.py:261
  12.7 13.6 %collective-permute-start.2 = (f32[16,128]{1,0:T(8,128)S(1)}, f32[16,128]{1,0:T(8,128)S(1)}, u32[]{:S(2)}, u32[]{:S(2)}) collective-permute-start(f32[16,128]{1,0:T(8,128)S(1)} %get-tuple-element.20), channel_id=1, source_target_pairs={{0,0},{1,3},{2,8},{3,11},{4,4},{5,7},{6,12},{7,15},{8,2},{9,1},{10... | collective-permute-start | bytes 24584 | tf_op jit(solution)/shard_map/ppermute | solution.py:271
  13.4 13.0 %collective-permute-start.3 = (f32[16,128]{1,0:T(8,128)S(1)}, f32[16,128]{1,0:T(8,128)S(1)}, u32[]{:S(2)}, u32[]{:S(2)}) collective-permute-start(f32[16,128]{1,0:T(8,128)S(1)} %get-tuple-element.21), channel_id=1, source_target_pairs={{0,4},{1,7},{2,12},{3,15},{4,0},{5,3},{6,8},{7,11},{8,6},{9,5},{10... | collective-permute-start | bytes 24584 | tf_op jit(solution)/shard_map/ppermute | solution.py:271
  13.5 20.2 %copy-start = (bf16[1,64,3072]{2,1,0:T(8,128)(2,1)S(1)}, bf16[1,64,3072]{2,1,0:T(8,128)(2,1)}, u32[]{:S(2)}) copy-start(bf16[1,64,3072]{2,1,0:T(8,128)(2,1)} %param.10) | copy-start | bytes 1179652
  13.5 20.2 %copy-start.1 = (bf16[16,3072]{1,0:T(8,128)(2,1)S(1)}, bf16[16,3072]{1,0:T(8,128)(2,1)}, u32[]{:S(2)}) copy-start(bf16[16,3072]{1,0:T(8,128)(2,1)} %residual.1) | copy-start | bytes 294916
  26.4 7.3 %collective-permute-start.5 = (bf16[32,3072]{1,0:T(8,128)(2,1)S(1)}, bf16[32,3072]{1,0:T(8,128)(2,1)S(1)}, u32[]{:S(2)}, u32[]{:S(2)}) collective-permute-start(bf16[32,3072]{1,0:T(8,128)(2,1)S(1)} %get-tuple-element.26), channel_id=1, source_target_pairs={{0,4},{4,0},{8,12},{12,8},{1,5},{5,1},{9,13},{13,9},{2,6},{6,2},{1... | collective-permute-start | bytes 589832 | tf_op jit(solution)/shard_map/ppermute | solution.py:261
  28.5 5.2 %collective-permute-start.4 = (f32[16,128]{1,0:T(8,128)S(1)}, f32[16,128]{1,0:T(8,128)S(1)}, u32[]{:S(2)}, u32[]{:S(2)}) collective-permute-start(f32[16,128]{1,0:T(8,128)S(1)} %add.3.near), channel_id=1, source_target_pairs={{0,1},{1,0},{2,3},{3,2},{4,5},{5,4},{6,7},{7,6},{8,9},{9,8},{10,11... | collective-permute-start | bytes 24584 | tf_op jit(solution)/shard_map/ppermute | solution.py:261
  34.1 10.1 %collective-permute-start.6 = (bf16[16,3072]{1,0:T(8,128)(2,1)S(1)}, bf16[16,3072]{1,0:T(8,128)(2,1)S(1)}, u32[]{:S(2)}, u32[]{:S(2)}) collective-permute-start(bf16[16,3072]{1,0:T(8,128)(2,1)S(1)} %get-tuple-element.28), channel_id=1, source_target_pairs={{0,8},{4,12},{8,0},{12,4},{1,9},{5,13},{9,1},{13,5},{2,10},{6,14},... | collective-permute-start | bytes 294920 | tf_op jit(solution)/shard_map/ppermute | solution.py:261

commit v12 on v3

--- a/solution.py
+++ b/solution.py
@@ -7,7 +7,7 @@
 from jax.experimental.pallas import tpu as pltpu
 from jax.sharding import PartitionSpec as P
 
-WIDTHS = (1024, 1280, 768)
+WIDTHS = (2304, 768)
 DEPTH = 768
 PS = ("page", "sub")
 VMEM = pl.BlockSpec(memory_space=pltpu.VMEM)
@@ -37,91 +37,46 @@
     return copy
 
 
-def first_kernel(
-    start,
-    width,
-    hidden,
-    rank_down,
-    weight,
-    low,
-    base,
-    hidden_here,
-    down_here,
-    held,
-    got,
-    arrived,
-):
-    steps = weight.shape[0] // DEPTH
-    copy = weight_copies(weight, held, arrived, start, width)
-
-    def hidden_copy(k):
-        return pltpu.make_async_copy(
-            hidden.at[:, deep(k)], hidden_here.at[:, deep(k)], got.at[0, k]
-        )
-
-    def down_copy(k):
-        return pltpu.make_async_copy(
-            rank_down.at[:, deep(k)], down_here.at[:, deep(k)], got.at[1, k]
-        )
-
-    @pl.loop(0, steps)
-    def _(k):
-        hidden_copy(k).start()
-        down_copy(k).start()
-
-    @pl.loop(0, steps)
-    def _(k):
-        copy(k).start()
-
-    low[...] = jnp.zeros_like(low)
-    base[...] = jnp.zeros_like(base)
-
-    @pl.loop(0, steps)
-    def _(k):
-        hidden_copy(k).wait()
-        down_copy(k).wait()
-        low[...] += lax.dot_general(
-            hidden_here[:, deep(k)],
-            down_here[:, deep(k)],
-            (((1,), (1,)), ((), ())),
-            preferred_element_type=jnp.float32,
-        )
-
-    @pl.loop(0, steps)
-    def _(k):
-        copy(k).wait()
-        base[...] += jnp.dot(
-            hidden_here[:, deep(k)], held[deep(k)], preferred_element_type=jnp.float32
-        )
-
-
-def first_phase(hidden, rank_down, weight, start, width):
+def low_kernel(hidden, rank_down, low, hidden_here, down_here, got):
+    copies = [
+        pltpu.make_async_copy(hidden, hidden_here, got.at[0]),
+        pltpu.make_async_copy(rank_down, down_here, got.at[1]),
+    ]
+    for copy in copies:
+        copy.start()
+    for copy in copies:
+        copy.wait()
+    low[...] = lax.dot_general(
+        hidden_here[...],
+        down_here[...],
+        (((1,), (1,)), ((), ())),
+        preferred_element_type=jnp.float32,
+    )
+
+
+def low_phase(hidden, rank_down):
     rows, depth = hidden.shape
     rank = rank_down.shape[0]
-    steps = depth // DEPTH
-    return pl.pallas_call(
-        functools.partial(first_kernel, start, width),
+    return pl.pallas_call(
+        low_kernel,
         out_shape=(
             jax.ShapeDtypeStruct((rows, rank), jnp.float32),
-            jax.ShapeDtypeStruct((rows, width), jnp.float32),
             jax.ShapeDtypeStruct(hidden.shape, hidden.dtype),
         ),
-        in_specs=[HBM] * 3,
-        out_specs=(VMEM, VMEM, VMEM),
+        in_specs=[HBM] * 2,
+        out_specs=(VMEM,) * 2,
         scratch_shapes=[
             pltpu.VMEM(rank_down.shape, rank_down.dtype),
-            pltpu.VMEM((depth, width), weight.dtype),
-            pltpu.SemaphoreType.DMA((2, steps)),
-            pltpu.SemaphoreType.DMA((steps,)),
+            pltpu.SemaphoreType.DMA((2,)),
         ],
         compiler_params=pltpu.CompilerParams(vmem_limit_bytes=52 << 20),
         cost_estimate=pl.CostEstimate(
-            flops=2 * rows * depth * (width + rank),
-            bytes_accessed=2 * depth * (width + rank + rows),
+            flops=2 * rows * depth * rank,
+            bytes_accessed=2 * depth * (rank + rows),
             transcendentals=0,
         ),
-        name="low_rank_and_base",
-    )(hidden, rank_down, weight)
+        name="low_rank",
+    )(hidden, rank_down)
 
 
 def stream_dot(hidden, weight, total, held, arrived, start):
@@ -155,7 +110,7 @@
             pltpu.VMEM((depth, width), weight.dtype),
             pltpu.SemaphoreType.DMA((depth // DEPTH,)),
         ],
-        compiler_params=pltpu.CompilerParams(vmem_limit_bytes=32 << 20),
+        compiler_params=pltpu.CompilerParams(vmem_limit_bytes=42 << 20),
         cost_estimate=pl.CostEstimate(
             flops=2 * rows * depth * width, bytes_accessed=2 * depth * width, transcendentals=0
         ),
@@ -178,21 +133,17 @@
     return jnp.dot(low.astype(jnp.bfloat16), up, preferred_element_type=jnp.float32)
 
 
-def correct_kernel(ids, low_a, low_b, low_c, low_d, up, base_one, base_two, low, sent, kept, total):
+def correct_kernel(ids, low_a, low_b, low_c, low_d, up, base, low, sent, kept, total):
     held = column_of(ids[...]) == lax.axis_index("tp").astype(jnp.float32)
     low[...] = jnp.where(held, (low_a[...] + low_b[...]) + (low_c[...] + low_d[...]), 0.0)
-    start = 0
-    for base in (base_one, base_two):
-        width = base.shape[1]
-        at = slice(start, start + width)
-        total[:, at] = base[...] + adapter_term(low[...], up[:, at])
-        start += width
-    split_rows(total, slice(0, start), sent, kept)
-
-
-def correct_phase(ids, lows, up, base_one, base_two):
+    width = base.shape[1]
+    total[...] = base[...] + adapter_term(low[...], up[:, :width])
+    split_rows(total, slice(0, width), sent, kept)
+
+
+def correct_phase(ids, lows, up, base):
     rows, rank = lows[0].shape
-    width = base_one.shape[1] + base_two.shape[1]
+    width = base.shape[1]
     return pl.pallas_call(
         correct_kernel,
         out_shape=(
@@ -200,12 +151,12 @@
             jax.ShapeDtypeStruct((rows // 2, width), jnp.bfloat16),
             jax.ShapeDtypeStruct((rows // 2, width), jnp.float32),
         ),
-        in_specs=[VMEM] * 8,
+        in_specs=[VMEM] * 7,
         out_specs=(VMEM,) * 3,
         scratch_shapes=[pltpu.VMEM((rows, width), jnp.float32)],
         compiler_params=pltpu.CompilerParams(vmem_limit_bytes=8 << 20),
         name="adapter_term",
-    )(ids, *lows, up, base_one, base_two)
+    )(ids, *lows, up, base)
 
 
 def last_kernel(start, hidden, weight, low, up, sent, kept, total, held, arrived):
@@ -287,20 +238,18 @@
     return lax.ppermute(value, "tp", [(i, i ^ bit) for i in range(lax.axis_size("tp"))])
 
 
-def four_by_four(hidden_units, adapter_ids, weight, rank_down, rank_up, residual):
+def four_by_four(hidden, adapter_ids, weight, rank_down, rank_up, residual):
     up = rank_up[0]
-    one, two, three = WIDTHS
-    low, base_one, hidden = first_phase(
-        hidden_units, jnp.swapaxes(rank_down, 1, 2)[0], weight, 0, one
-    )
+    one, two = WIDTHS
+    low, hidden = low_phase(hidden, jnp.swapaxes(rank_down, 1, 2)[0])
     lows = []
     for j in range(4):
         pairs = [(t * 4 + a, a * 4 + (t + j) % 4) for t in range(4) for a in range(4)]
         lows.append(lax.ppermute(low, ("tp",) + PS, pairs))
-    base_two = base_phase(hidden, weight, one, two)
-    low, sent, kept = correct_phase(adapter_ids[None], lows, up, base_one, base_two)
+    base = base_phase(hidden, weight, 0, one)
+    low, sent, kept = correct_phase(adapter_ids[None], lows, up, base)
     got = swap(sent, 1)
-    sent_last, kept_last = last_phase(hidden, weight, low, up, one + two, three)
+    sent_last, kept_last = last_phase(hidden, weight, low, up, one, two)
     got_last = swap(sent_last, 1)
     sent, total = pair_phase(kept, got)
     got = swap(sent, 2)

time: 41.5 us -> 41.1 us (level)
    pallas_call x1, Pallas kernels: 7.5 us -> 2 us  [low_phase(): pl.pallas_call(low_kernel, out_shape=(jax.ShapeDtypeStruct((rows, rank),...]
    pallas_call x1, Pallas kernels: 7.92 us -> 13 us  [base_phase(): pl.pallas_call(functools.partial(base_kernel, start), out_shape=jax.Shape...]
  transfers between devices with their start and end apart: 8 -> 8, of which waited for: 2 -> 2; matrix products, arithmetic and copies ran while one was open for 0% -> 0% of each run, Pallas kernels for 32% -> 45%
where the time goes in v12:
time: 41.1 us; the launch traced here: 40.9 us
  Pallas kernels  21.6 us (53%)
  starting transfers between devices  16.1 us (39%)
  waiting for transfers between devices  3.09 us (8%)
    pallas_call x1, Pallas kernels, base_phase(): pl.pallas_call(functools.partial(base_kernel, start), out_shape=jax.Shape...  13 us
    ppermute x4, starting transfers between devices, swap(): lax.ppermute(value, 'tp', [(i, i ^ bit) for i in range(lax.axis_size('tp'...  9.78 us
    ppermute x4, starting transfers between devices, four_by_four(): lows.append(lax.ppermute(low, ('tp',) + PS, pairs))  6.34 us
    pallas_call x1, Pallas kernels, last_phase(): pl.pallas_call(functools.partial(last_kernel, start), out_shape=(jax.Shap...  5.42 us
    ppermute x4, waiting for transfers between devices, swap(): lax.ppermute(value, 'tp', [(i, i ^ bit) for i in range(lax.axis_size('tp'...  3.08 us
    pallas_call x1, Pallas kernels, low_phase(): pl.pallas_call(low_kernel, out_shape=(jax.ShapeDtypeStruct((rows, rank),...  2 us
  transfers between devices with their start and end apart: 8, of which 2 were waited for; matrix products, arithmetic and copies ran while one was open for 0% of the time, Pallas kernels for 45%

profile of v12, /device:TPU:0, one launch (start us, length us, event | category | flops | bytes accessed | tf_op | source)
XLA Modules:
  0.0 40.9 jit_solution(427621701086526319)
XLA Ops:
  0.0 2.0 %low_rank.1 = (f32[64,64]{1,0:T(8,128)S(1)}, bf16[64,8448]{1,0:T(8,128)(2,1)S(1)}) custom-call(bf16[64,8448]{1,0:T(8,128)(2,1)} %hidden.1, bf16[64,8448]{1,0:T(8,128)(2,1)} %bitcast.8), custom_call_target="tpu_custom_call" | custom-call | flops 69206016 | bytes 2162688 | tf_op jit(solution)/shard_map/low_rank/pallas_call | solution.py:60
  2.0 2.4 %collective-permute-start.3 = (f32[64,64]{1,0:T(8,128)S(1)}, f32[64,64]{1,0:T(8,128)S(1)}, u32[]{:S(2)}, u32[]{:S(2)}) collective-permute-start(f32[64,64]{1,0:T(8,128)S(1)} %get-tuple-element.16), channel_id=1, source_target_pairs={{0,3},{1,7},{2,11},{3,15},{4,0},{5,4},{6,8},{7,12},{8,1},{9,5},{10... | collective-permute-start | bytes 49160 | tf_op jit(solution)/shard_map/ppermute | solution.py:248
  4.5 2.6 %collective-permute-start.2 = (f32[64,64]{1,0:T(8,128)S(1)}, f32[64,64]{1,0:T(8,128)S(1)}, u32[]{:S(2)}, u32[]{:S(2)}) collective-permute-start(f32[64,64]{1,0:T(8,128)S(1)} %get-tuple-element.16), channel_id=1, source_target_pairs={{0,2},{1,6},{2,10},{3,14},{4,3},{5,7},{6,11},{7,15},{8,0},{9,4},{1... | collective-permute-start | bytes 49160 | tf_op jit(solution)/shard_map/ppermute | solution.py:248
  7.0 0.7 %collective-permute-start.1 = (f32[64,64]{1,0:T(8,128)S(1)}, f32[64,64]{1,0:T(8,128)S(1)}, u32[]{:S(2)}, u32[]{:S(2)}) collective-permute-start(f32[64,64]{1,0:T(8,128)S(1)} %get-tuple-element.16), channel_id=1, source_target_pairs={{0,1},{1,5},{2,9},{3,13},{4,2},{5,6},{6,10},{7,14},{8,3},{9,7},{10... | collective-permute-start | bytes 49160 | tf_op jit(solution)/shard_map/ppermute | solution.py:248
  7.7 0.7 %collective-permute-start = (f32[64,64]{1,0:T(8,128)S(1)}, f32[64,64]{1,0:T(8,128)S(1)}, u32[]{:S(2)}, u32[]{:S(2)}) collective-permute-start(f32[64,64]{1,0:T(8,128)S(1)} %get-tuple-element.16), channel_id=1, source_target_pairs={{0,0},{1,4},{2,8},{3,12},{4,1},{5,5},{6,9},{7,13},{8,2},{9,6},{10,... | collective-permute-start | bytes 49160 | tf_op jit(solution)/shard_map/ppermute | solution.py:248
  8.4 0.0 copy-start
  8.4 0.0 copy-start.2
  8.4 13.0 %base.1 = f32[64,2304]{1,0:T(8,128)S(1)} custom-call(bf16[64,8448]{1,0:T(8,128)(2,1)S(1)} %get-tuple-element.17.hidden, bf16[8448,3072]{1,0:T(8,128)(2,1)} %weight.3), custom_call_target="tpu_custom_call" | custom-call | flops 2491416576 | bytes 38928384 | tf_op jit(solution)/shard_map/base/pallas_call | solution.py:104
  21.4 0.0 collective-permute-done.3.low_d
  21.4 0.0 collective-permute-done.2.low_c
  21.5 0.0 collective-permute-done.1.low_b
  21.5 0.0 collective-permute-done.low_a
  21.5 0.0 copy-done
  21.5 0.0 copy-done.2
  21.5 0.4 adapter_term.1
  21.9 4.0 %collective-permute-start.4 = (bf16[32,2304]{1,0:T(8,128)(2,1)S(1)}, bf16[32,2304]{1,0:T(8,128)(2,1)S(1)}, u32[]{:S(2)}, u32[]{:S(2)}) collective-permute-start(bf16[32,2304]{1,0:T(8,128)(2,1)S(1)} %get-tuple-element.19), channel_id=1, source_target_pairs={{0,4},{4,0},{8,12},{12,8},{1,5},{5,1},{9,13},{13,9},{2,6},{6,2},{1... | collective-permute-start | bytes 442376 | tf_op jit(solution)/shard_map/ppermute | solution.py:238
  25.8 0.0 copy-start.1
  25.8 5.4 %last_base.1 = (bf16[32,768]{1,0:T(8,128)(2,1)S(1)}, f32[32,768]{1,0:T(8,128)S(1)}) custom-call(bf16[64,8448]{1,0:T(8,128)(2,1)S(1)} %get-tuple-element.17.hidden, bf16[8448,3072]{1,0:T(8,128)(2,1)} %weight.3, f32[64,64]{1,0:T(8,128)S(1)} %get-tuple-element.22.low, bf16[64,3072]{1,0:T(8,128)(2,1)S(1)} %bitcast.6), custom_call_target="tpu_custom_call" | custom-call | flops 830472192 | bytes 12976128 | tf_op jit(solution)/shard_map/last_base/pallas_call | solution.py:171
  31.3 0.1 collective-permute-start.6
  31.4 0.0 collective-permute-done.4.got
  31.4 2.9 %collective-permute-start.5 = (bf16[16,2304]{1,0:T(8,128)(2,1)S(1)}, bf16[16,2304]{1,0:T(8,128)(2,1)S(1)}, u32[]{:S(2)}, u32[]{:S(2)}) collective-permute-start(bf16[16,2304]{1,0:T(8,128)(2,1)S(1)} %get-tuple-element.21), channel_id=1, source_target_pairs={{0,8},{4,12},{8,0},{12,4},{1,9},{5,13},{9,1},{13,5},{2,10},{6,14},... | collective-permute-start | bytes 221192 | tf_op jit(solution)/shard_map/ppermute | solution.py:238
  34.3 1.1 %collective-permute-done.6.got = bf16[32,768]{1,0:T(8,128)(2,1)S(1)} collective-permute-done((bf16[32,768]{1,0:T(8,128)(2,1)S(1)}, bf16[32,768]{1,0:T(8,128)(2,1)S(1)}, u32[]{:S(2)}, u32[]{:S(2)}) %collective-permute-start.6) | collective-permute-done | bytes 49184 | tf_op jit(solution)/shard_map/ppermute | solution.py:238
  35.4 2.9 %collective-permute-start.7 = (bf16[16,768]{1,0:T(8,128)(2,1)S(1)}, bf16[16,768]{1,0:T(8,128)(2,1)S(1)}, u32[]{:S(2)}, u32[]{:S(2)}) collective-permute-start(bf16[16,768]{1,0:T(8,128)(2,1)S(1)} %get-tuple-element.26), channel_id=1, source_target_pairs={{0,8},{4,12},{8,0},{12,4},{1,9},{5,13},{9,1},{13,5},{2,10},{6,14},... | collective-permute-start | bytes 73736 | tf_op jit(solution)/shard_map/ppermute | solution.py:238
  38.3 1.9 %collective-permute-done.7.got_two = bf16[16,768]{1,0:T(8,128)(2,1)S(1)} collective-permute-done((bf16[16,768]{1,0:T(8,128)(2,1)S(1)}, bf16[16,768]{1,0:T(8,128)(2,1)S(1)}, u32[]{:S(2)}, u32[]{:S(2)}) %collective-permute-start.7) | collective-permute-done | bytes 24608 | tf_op jit(solution)/shard_map/ppermute | solution.py:238
  40.2 0.0 collective-permute-done.5.got_one
  40.2 0.0 copy-done.1
  40.2 0.7 %finish.1 = bf16[16,3072]{1,0:T(8,128)(2,1)} custom-call(bf16[16,3072]{1,0:T(8,128)(2,1)S(1)} %copy-done.1, f32[16,2304]{1,0:T(8,128)S(1)} %get-tuple-element.20.total_one, bf16[16,2304]{1,0:T(8,128)(2,1)S(1)} %collective-permute-done.5.got_one, f32[16,768]{1,0:T(8,128)S(1)} %get-tuple-element.25.total_two, bf16[16,768]{1,0:T(8,128)(2,1)S(1)} %collective-permute-done.7.got_two), custom_call_target="tpu_custom_call" | custom-call | tf_op jit(solution)/shard_map/finish/pallas_call | solution.py:227
  (2 shorter events, 0.0 us)
Async XLA Ops:
  2.0 19.4 %collective-permute-start.3 = (f32[64,64]{1,0:T(8,128)S(1)}, f32[64,64]{1,0:T(8,128)S(1)}, u32[]{:S(2)}, u32[]{:S(2)}) collective-permute-start(f32[64,64]{1,0:T(8,128)S(1)} %get-tuple-element.16), channel_id=1, source_target_pairs={{0,3},{1,7},{2,11},{3,15},{4,0},{5,4},{6,8},{7,12},{8,1},{9,5},{10... | collective-permute-start | bytes 49160 | tf_op jit(solution)/shard_map/ppermute | solution.py:248
  4.5 17.0 %collective-permute-start.2 = (f32[64,64]{1,0:T(8,128)S(1)}, f32[64,64]{1,0:T(8,128)S(1)}, u32[]{:S(2)}, u32[]{:S(2)}) collective-permute-start(f32[64,64]{1,0:T(8,128)S(1)} %get-tuple-element.16), channel_id=1, source_target_pairs={{0,2},{1,6},{2,10},{3,14},{4,3},{5,7},{6,11},{7,15},{8,0},{9,4},{1... | collective-permute-start | bytes 49160 | tf_op jit(solution)/shard_map/ppermute | solution.py:248
  7.0 14.4 %collective-permute-start.1 = (f32[64,64]{1,0:T(8,128)S(1)}, f32[64,64]{1,0:T(8,128)S(1)}, u32[]{:S(2)}, u32[]{:S(2)}) collective-permute-start(f32[64,64]{1,0:T(8,128)S(1)} %get-tuple-element.16), channel_id=1, source_target_pairs={{0,1},{1,5},{2,9},{3,13},{4,2},{5,6},{6,10},{7,14},{8,3},{9,7},{10... | collective-permute-start | bytes 49160 | tf_op jit(solution)/shard_map/ppermute | solution.py:248
  7.7 13.8 %collective-permute-start = (f32[64,64]{1,0:T(8,128)S(1)}, f32[64,64]{1,0:T(8,128)S(1)}, u32[]{:S(2)}, u32[]{:S(2)}) collective-permute-start(f32[64,64]{1,0:T(8,128)S(1)} %get-tuple-element.16), channel_id=1, source_target_pairs={{0,0},{1,4},{2,8},{3,12},{4,1},{5,5},{6,9},{7,13},{8,2},{9,6},{10,... | collective-permute-start | bytes 49160 | tf_op jit(solution)/shard_map/ppermute | solution.py:248
  8.4 13.1 %copy-start = (bf16[1,64,3072]{2,1,0:T(8,128)(2,1)S(1)}, bf16[1,64,3072]{2,1,0:T(8,128)(2,1)}, u32[]{:S(2)}) copy-start(bf16[1,64,3072]{2,1,0:T(8,128)(2,1)} %param.10) | copy-start | bytes 1179652
  8.4 13.1 %copy-start.2 = (s32[64]{0:T(128)S(1)}, s32[64]{0:T(128)}, u32[]{:S(2)}) copy-start(s32[64]{0:T(128)} %param.7) | copy-start | bytes 772
  21.9 9.5 %collective-permute-start.4 = (bf16[32,2304]{1,0:T(8,128)(2,1)S(1)}, bf16[32,2304]{1,0:T(8,128)(2,1)S(1)}, u32[]{:S(2)}, u32[]{:S(2)}) collective-permute-start(bf16[32,2304]{1,0:T(8,128)(2,1)S(1)} %get-tuple-element.19), channel_id=1, source_target_pairs={{0,4},{4,0},{8,12},{12,8},{1,5},{5,1},{9,13},{13,9},{2,6},{6,2},{1... | collective-permute-start | bytes 442376 | tf_op jit(solution)/shard_map/ppermute | solution.py:238
  25.8 14.4 %copy-start.1 = (bf16[16,3072]{1,0:T(8,128)(2,1)S(1)}, bf16[16,3072]{1,0:T(8,128)(2,1)}, u32[]{:S(2)}) copy-start(bf16[16,3072]{1,0:T(8,128)(2,1)} %residual.1) | copy-start | bytes 294916
  31.3 4.2 %collective-permute-start.6 = (bf16[32,768]{1,0:T(8,128)(2,1)S(1)}, bf16[32,768]{1,0:T(8,128)(2,1)S(1)}, u32[]{:S(2)}, u32[]{:S(2)}) collective-permute-start(bf16[32,768]{1,0:T(8,128)(2,1)S(1)} %get-tuple-element.24), channel_id=1, source_target_pairs={{0,4},{4,0},{8,12},{12,8},{1,5},{5,1},{9,13},{13,9},{2,6},{6,2},{1... | collective-permute-start | bytes 147464 | tf_op jit(solution)/shard_map/ppermute | solution.py:238
  31.4 8.8 %collective-permute-start.5 = (bf16[16,2304]{1,0:T(8,128)(2,1)S(1)}, bf16[16,2304]{1,0:T(8,128)(2,1)S(1)}, u32[]{:S(2)}, u32[]{:S(2)}) collective-permute-start(bf16[16,2304]{1,0:T(8,128)(2,1)S(1)} %get-tuple-element.21), channel_id=1, source_target_pairs={{0,8},{4,12},{8,0},{12,4},{1,9},{5,13},{9,1},{13,5},{2,10},{6,14},... | collective-permute-start | bytes 221192 | tf_op jit(solution)/shard_map/ppermute | solution.py:238
  35.4 4.8 %collective-permute-start.7 = (bf16[16,768]{1,0:T(8,128)(2,1)S(1)}, bf16[16,768]{1,0:T(8,128)(2,1)S(1)}, u32[]{:S(2)}, u32[]{:S(2)}) collective-permute-start(bf16[16,768]{1,0:T(8,128)(2,1)S(1)} %get-tuple-element.26), channel_id=1, source_target_pairs={{0,8},{4,12},{8,0},{12,4},{1,9},{5,13},{9,1},{13,5},{2,10},{6,14},... | collective-permute-start | bytes 73736 | tf_op jit(solution)/shard_map/ppermute | solution.py:238

commit v13 on v12

--- a/solution.py
+++ b/solution.py
@@ -37,7 +37,7 @@
     return copy
 
 
-def low_kernel(hidden, rank_down, low, hidden_here, down_here, got):
+def low_kernel(hidden, rank_down, packed, hidden_here, down_here, got):
     copies = [
         pltpu.make_async_copy(hidden, hidden_here, got.at[0]),
         pltpu.make_async_copy(rank_down, down_here, got.at[1]),
@@ -46,12 +46,16 @@
         copy.start()
     for copy in copies:
         copy.wait()
-    low[...] = lax.dot_general(
+    low = lax.dot_general(
         hidden_here[...],
         down_here[...],
         (((1,), (1,)), ((), ())),
         preferred_element_type=jnp.float32,
     )
+    half = low.shape[0] // 2
+    block = jnp.concatenate([low[:half], low[half:]], axis=1)
+    for to in range(packed.shape[0]):
+        packed[to] = block
 
 
 def low_phase(hidden, rank_down):
@@ -60,7 +64,7 @@
     return pl.pallas_call(
         low_kernel,
         out_shape=(
-            jax.ShapeDtypeStruct((rows, rank), jnp.float32),
+            jax.ShapeDtypeStruct((16, rows // 2, 2 * rank), jnp.float32),
             jax.ShapeDtypeStruct(hidden.shape, hidden.dtype),
         ),
         in_specs=[HBM] * 2,
@@ -133,16 +137,23 @@
     return jnp.dot(low.astype(jnp.bfloat16), up, preferred_element_type=jnp.float32)
 
 
-def correct_kernel(ids, low_a, low_b, low_c, low_d, up, base, low, sent, kept, total):
-    held = column_of(ids[...]) == lax.axis_index("tp").astype(jnp.float32)
-    low[...] = jnp.where(held, (low_a[...] + low_b[...]) + (low_c[...] + low_d[...]), 0.0)
+def correct_kernel(ids, packed, up, base, low, sent, kept, total):
+    tp = lax.axis_index("tp")
+    summed = packed[tp]
+    for source in range(1, 4):
+        summed = summed + packed[4 * source + tp]
+    rank = low.shape[1]
+    summed = jnp.concatenate([summed[:, :rank], summed[:, rank:]], axis=0)
+    held = column_of(ids[...]) == tp.astype(jnp.float32)
+    low[...] = jnp.where(held, summed, 0.0)
     width = base.shape[1]
     total[...] = base[...] + adapter_term(low[...], up[:, :width])
     split_rows(total, slice(0, width), sent, kept)
 
 
-def correct_phase(ids, lows, up, base):
-    rows, rank = lows[0].shape
+def correct_phase(ids, packed, up, base):
+    rows = base.shape[0]
+    rank = up.shape[0]
     width = base.shape[1]
     return pl.pallas_call(
         correct_kernel,
@@ -151,12 +162,12 @@
             jax.ShapeDtypeStruct((rows // 2, width), jnp.bfloat16),
             jax.ShapeDtypeStruct((rows // 2, width), jnp.float32),
         ),
-        in_specs=[VMEM] * 7,
+        in_specs=[VMEM] * 4,
         out_specs=(VMEM,) * 3,
         scratch_shapes=[pltpu.VMEM((rows, width), jnp.float32)],
         compiler_params=pltpu.CompilerParams(vmem_limit_bytes=8 << 20),
         name="adapter_term",
-    )(ids, *lows, up, base)
+    )(ids, packed, up, base)
 
 
 def last_kernel(start, hidden, weight, low, up, sent, kept, total, held, arrived):
@@ -241,13 +252,10 @@
 def four_by_four(hidden, adapter_ids, weight, rank_down, rank_up, residual):
     up = rank_up[0]
     one, two = WIDTHS
-    low, hidden = low_phase(hidden, jnp.swapaxes(rank_down, 1, 2)[0])
-    lows = []
-    for j in range(4):
-        pairs = [(t * 4 + a, a * 4 + (t + j) % 4) for t in range(4) for a in range(4)]
-        lows.append(lax.ppermute(low, ("tp",) + PS, pairs))
+    packed, hidden = low_phase(hidden, jnp.swapaxes(rank_down, 1, 2)[0])
+    packed = lax.all_to_all(packed, ("tp",) + PS, split_axis=0, concat_axis=0, tiled=True)
     base = base_phase(hidden, weight, 0, one)
-    low, sent, kept = correct_phase(adapter_ids[None], lows, up, base)
+    low, sent, kept = correct_phase(adapter_ids[None], packed, up, base)
     got = swap(sent, 1)
     sent_last, kept_last = last_phase(hidden, weight, low, up, one, two)
     got_last = swap(sent_last, 1)

time: 41.1 us -> 42.1 us (1.024)
  waiting for transfers between devices: 3.09 us -> 5.25 us
  starting transfers between devices: 16.1 us -> 14 us
  Pallas kernels: 21.6 us -> 22.4 us
    all_to_all x0 -> x1, starting transfers between devices: none -> 7.37 us  [four_by_four(): lax.all_to_all(packed, ('tp',) + PS, split_axis=0, concat_axis=0, tiled=T...]
    ppermute x4 -> x0, starting transfers between devices: 6.34 us -> none  [four_by_four(): lows.append(lax.ppermute(low, ('tp',) + PS, pairs))]
    ppermute x4, starting transfers between devices: 9.78 us -> 6.67 us  [swap(): lax.ppermute(value, 'tp', [(i, i ^ bit) for i in range(lax.axis_size('tp'...]
    ppermute x4, waiting for transfers between devices: 3.08 us -> 5.24 us  [swap(): lax.ppermute(value, 'tp', [(i, i ^ bit) for i in range(lax.axis_size('tp'...]
    pallas_call x1, Pallas kernels: 2 us -> 2.78 us  [low_phase(): pl.pallas_call(low_kernel, out_shape=(jax.ShapeDtypeStruct((16, rows // 2...]
  transfers between devices with their start and end apart: 8 -> 5, of which waited for: 2 -> 2; matrix products, arithmetic and copies ran while one was open for 0% -> 0% of each run, Pallas kernels for 45% -> 44%
where the time goes in v13:
time: 42.1 us; the launch traced here: 41.8 us
  Pallas kernels  22.4 us (53%)
  starting transfers between devices  14 us (33%)
  waiting for transfers between devices  5.25 us (12%)
    pallas_call x1, Pallas kernels, base_phase(): pl.pallas_call(functools.partial(base_kernel, start), out_shape=jax.Shape...  13 us
    all_to_all x1, starting transfers between devices, four_by_four(): lax.all_to_all(packed, ('tp',) + PS, split_axis=0, concat_axis=0, tiled=T...  7.37 us
    ppermute x4, starting transfers between devices, swap(): lax.ppermute(value, 'tp', [(i, i ^ bit) for i in range(lax.axis_size('tp'...  6.67 us
    pallas_call x1, Pallas kernels, last_phase(): pl.pallas_call(functools.partial(last_kernel, start), out_shape=(jax.Shap...  5.43 us
    ppermute x4, waiting for transfers between devices, swap(): lax.ppermute(value, 'tp', [(i, i ^ bit) for i in range(lax.axis_size('tp'...  5.24 us
    pallas_call x1, Pallas kernels, low_phase(): pl.pallas_call(low_kernel, out_shape=(jax.ShapeDtypeStruct((16, rows // 2...  2.78 us
  transfers between devices with their start and end apart: 5, of which 2 were waited for; matrix products, arithmetic and copies ran while one was open for 0% of the time, Pallas kernels for 44%

profile of v13, /device:TPU:0, one launch (start us, length us, event | category | flops | bytes accessed | tf_op | source)
XLA Modules:
  0.0 41.8 jit_solution(16028905316252950671)
XLA Ops:
  0.0 2.8 %low_rank.1 = (f32[16,32,128]{2,1,0:T(8,128)}, bf16[64,8448]{1,0:T(8,128)(2,1)S(1)}) custom-call(bf16[64,8448]{1,0:T(8,128)(2,1)} %hidden.1, bf16[64,8448]{1,0:T(8,128)(2,1)} %bitcast.8), custom_call_target="tpu_custom_call" | custom-call | flops 69206016 | bytes 2162688 | tf_op jit(solution)/shard_map/low_rank/pallas_call | solution.py:64
  2.8 7.4 %all-to-all-start = ((f32[16,32,128]{2,1,0:T(8,128)}), f32[16,32,128]{2,1,0:T(8,128)S(1)}, u32[]{:S(2)}, u32[]{:S(2)}) async-start(f32[16,32,128]{2,1,0:T(8,128)} %get-tuple-element.16), calls=%async_computation | async-start | bytes 524288 | tf_op jit(solution)/shard_map/all_to_all | solution.py:256
  10.2 0.0 copy-start
  10.2 0.0 copy-start.2
  10.2 13.0 %base.1 = f32[64,2304]{1,0:T(8,128)S(1)} custom-call(bf16[64,8448]{1,0:T(8,128)(2,1)S(1)} %get-tuple-element.17.hidden, bf16[8448,3072]{1,0:T(8,128)(2,1)} %weight.3), custom_call_target="tpu_custom_call" | custom-call | flops 2491416576 | bytes 38928384 | tf_op jit(solution)/shard_map/base/pallas_call | solution.py:108
  23.2 0.0 all-to-all-done.packed
  23.3 0.0 copy-done
  23.3 0.0 copy-done.2
  23.3 0.4 adapter_term.1
  23.7 2.0 %collective-permute-start = (bf16[32,2304]{1,0:T(8,128)(2,1)S(1)}, bf16[32,2304]{1,0:T(8,128)(2,1)S(1)}, u32[]{:S(2)}, u32[]{:S(2)}) collective-permute-start(bf16[32,2304]{1,0:T(8,128)(2,1)S(1)} %get-tuple-element.19), channel_id=1, source_target_pairs={{0,4},{4,0},{8,12},{12,8},{1,5},{5,1},{9,13},{13,9},{2,6},{6,2},{1... | collective-permute-start | bytes 442376 | tf_op jit(solution)/shard_map/ppermute | solution.py:249
  25.7 0.0 copy-start.1
  25.7 5.4 %last_base.1 = (bf16[32,768]{1,0:T(8,128)(2,1)S(1)}, f32[32,768]{1,0:T(8,128)S(1)}) custom-call(bf16[64,8448]{1,0:T(8,128)(2,1)S(1)} %get-tuple-element.17.hidden, bf16[8448,3072]{1,0:T(8,128)(2,1)} %weight.3, f32[64,64]{1,0:T(8,128)S(1)} %get-tuple-element.22.low, bf16[64,3072]{1,0:T(8,128)(2,1)S(1)} %bitcast.6), custom_call_target="tpu_custom_call" | custom-call | flops 830472192 | bytes 12976128 | tf_op jit(solution)/shard_map/last_base/pallas_call | solution.py:182
  31.1 0.2 collective-permute-start.2
  31.3 0.0 collective-permute-done.got
  31.3 2.9 %collective-permute-start.1 = (bf16[16,2304]{1,0:T(8,128)(2,1)S(1)}, bf16[16,2304]{1,0:T(8,128)(2,1)S(1)}, u32[]{:S(2)}, u32[]{:S(2)}) collective-permute-start(bf16[16,2304]{1,0:T(8,128)(2,1)S(1)} %get-tuple-element.21), channel_id=1, source_target_pairs={{0,8},{4,12},{8,0},{12,4},{1,9},{5,13},{9,1},{13,5},{2,10},{6,14},... | collective-permute-start | bytes 221192 | tf_op jit(solution)/shard_map/ppermute | solution.py:249
  34.2 2.1 %collective-permute-done.2.got = bf16[32,768]{1,0:T(8,128)(2,1)S(1)} collective-permute-done((bf16[32,768]{1,0:T(8,128)(2,1)S(1)}, bf16[32,768]{1,0:T(8,128)(2,1)S(1)}, u32[]{:S(2)}, u32[]{:S(2)}) %collective-permute-start.2) | collective-permute-done | bytes 49184 | tf_op jit(solution)/shard_map/ppermute | solution.py:249
  36.3 1.6 %collective-permute-start.3 = (bf16[16,768]{1,0:T(8,128)(2,1)S(1)}, bf16[16,768]{1,0:T(8,128)(2,1)S(1)}, u32[]{:S(2)}, u32[]{:S(2)}) collective-permute-start(bf16[16,768]{1,0:T(8,128)(2,1)S(1)} %get-tuple-element.26), channel_id=1, source_target_pairs={{0,8},{4,12},{8,0},{12,4},{1,9},{5,13},{9,1},{13,5},{2,10},{6,14},... | collective-permute-start | bytes 73736 | tf_op jit(solution)/shard_map/ppermute | solution.py:249
  37.9 3.2 %collective-permute-done.3.got_two = bf16[16,768]{1,0:T(8,128)(2,1)S(1)} collective-permute-done((bf16[16,768]{1,0:T(8,128)(2,1)S(1)}, bf16[16,768]{1,0:T(8,128)(2,1)S(1)}, u32[]{:S(2)}, u32[]{:S(2)}) %collective-permute-start.3) | collective-permute-done | bytes 24608 | tf_op jit(solution)/shard_map/ppermute | solution.py:249
  41.1 0.0 collective-permute-done.1.got_one
  41.1 0.0 copy-done.1
  41.1 0.7 %finish.1 = bf16[16,3072]{1,0:T(8,128)(2,1)} custom-call(bf16[16,3072]{1,0:T(8,128)(2,1)S(1)} %copy-done.1, f32[16,2304]{1,0:T(8,128)S(1)} %get-tuple-element.20.total_one, bf16[16,2304]{1,0:T(8,128)(2,1)S(1)} %collective-permute-done.1.got_one, f32[16,768]{1,0:T(8,128)S(1)} %get-tuple-element.25.total_two, bf16[16,768]{1,0:T(8,128)(2,1)S(1)} %collective-permute-done.3.got_two), custom_call_target="tpu_custom_call" | custom-call | tf_op jit(solution)/shard_map/finish/pallas_call | solution.py:238
  (2 shorter events, 0.0 us)
Async XLA Ops:
  2.8 20.5 %all-to-all-start = ((f32[16,32,128]{2,1,0:T(8,128)}), f32[16,32,128]{2,1,0:T(8,128)S(1)}, u32[]{:S(2)}, u32[]{:S(2)}) async-start(f32[16,32,128]{2,1,0:T(8,128)} %get-tuple-element.16), calls=%async_computation | async-start | bytes 524288 | tf_op jit(solution)/shard_map/all_to_all | solution.py:256
  10.2 13.1 %copy-start = (bf16[1,64,3072]{2,1,0:T(8,128)(2,1)S(1)}, bf16[1,64,3072]{2,1,0:T(8,128)(2,1)}, u32[]{:S(2)}) copy-start(bf16[1,64,3072]{2,1,0:T(8,128)(2,1)} %param.10) | copy-start | bytes 1179652
  10.2 13.1 %copy-start.2 = (s32[64]{0:T(128)S(1)}, s32[64]{0:T(128)}, u32[]{:S(2)}) copy-start(s32[64]{0:T(128)} %param.7) | copy-start | bytes 772
  23.7 7.6 %collective-permute-start = (bf16[32,2304]{1,0:T(8,128)(2,1)S(1)}, bf16[32,2304]{1,0:T(8,128)(2,1)S(1)}, u32[]{:S(2)}, u32[]{:S(2)}) collective-permute-start(bf16[32,2304]{1,0:T(8,128)(2,1)S(1)} %get-tuple-element.19), channel_id=1, source_target_pairs={{0,4},{4,0},{8,12},{12,8},{1,5},{5,1},{9,13},{13,9},{2,6},{6,2},{1... | collective-permute-start | bytes 442376 | tf_op jit(solution)/shard_map/ppermute | solution.py:249
  25.7 15.4 %copy-start.1 = (bf16[16,3072]{1,0:T(8,128)(2,1)S(1)}, bf16[16,3072]{1,0:T(8,128)(2,1)}, u32[]{:S(2)}) copy-start(bf16[16,3072]{1,0:T(8,128)(2,1)} %residual.1) | copy-start | bytes 294916
  31.1 5.2 %collective-permute-start.2 = (bf16[32,768]{1,0:T(8,128)(2,1)S(1)}, bf16[32,768]{1,0:T(8,128)(2,1)S(1)}, u32[]{:S(2)}, u32[]{:S(2)}) collective-permute-start(bf16[32,768]{1,0:T(8,128)(2,1)S(1)} %get-tuple-element.24), channel_id=1, source_target_pairs={{0,4},{4,0},{8,12},{12,8},{1,5},{5,1},{9,13},{13,9},{2,6},{6,2},{1... | collective-permute-start | bytes 147464 | tf_op jit(solution)/shard_map/ppermute | solution.py:249
  31.3 9.8 %collective-permute-start.1 = (bf16[16,2304]{1,0:T(8,128)(2,1)S(1)}, bf16[16,2304]{1,0:T(8,128)(2,1)S(1)}, u32[]{:S(2)}, u32[]{:S(2)}) collective-permute-start(bf16[16,2304]{1,0:T(8,128)(2,1)S(1)} %get-tuple-element.21), channel_id=1, source_target_pairs={{0,8},{4,12},{8,0},{12,4},{1,9},{5,13},{9,1},{13,5},{2,10},{6,14},... | collective-permute-start | bytes 221192 | tf_op jit(solution)/shard_map/ppermute | solution.py:249
  36.3 4.8 %collective-permute-start.3 = (bf16[16,768]{1,0:T(8,128)(2,1)S(1)}, bf16[16,768]{1,0:T(8,128)(2,1)S(1)}, u32[]{:S(2)}, u32[]{:S(2)}) collective-permute-start(bf16[16,768]{1,0:T(8,128)(2,1)S(1)} %get-tuple-element.26), channel_id=1, source_target_pairs={{0,8},{4,12},{8,0},{12,4},{1,9},{5,13},{9,1},{13,5},{2,10},{6,14},... | collective-permute-start | bytes 73736 | tf_op jit(solution)/shard_map/ppermute | solution.py:249

commit v14 on v12

--- a/solution.py
+++ b/solution.py
@@ -9,6 +9,12 @@
 
 WIDTHS = (2304, 768)
 DEPTH = 768
+HOLDERS = (
+    ((2, 0, 1, 3), (1, 3, 2, 0), (3, 2, 0, 1), (0, 1, 3, 2)),
+    ((3, 2, 0, 1), (0, 3, 1, 2), (1, 0, 2, 3), (2, 1, 3, 0)),
+    ((3, 2, 1, 0), (1, 0, 3, 2), (2, 1, 0, 3), (0, 3, 2, 1)),
+    ((1, 2, 3, 0), (3, 1, 0, 2), (2, 0, 1, 3), (0, 3, 2, 1)),
+)
 PS = ("page", "sub")
 VMEM = pl.BlockSpec(memory_space=pltpu.VMEM)
 HBM = pl.BlockSpec(memory_space=pltpu.HBM)
@@ -243,8 +249,8 @@
     one, two = WIDTHS
     low, hidden = low_phase(hidden, jnp.swapaxes(rank_down, 1, 2)[0])
     lows = []
-    for j in range(4):
-        pairs = [(t * 4 + a, a * 4 + (t + j) % 4) for t in range(4) for a in range(4)]
+    for k in (3, 2, 1, 0):
+        pairs = [(t * 4 + a, a * 4 + HOLDERS[a][k][t]) for t in range(4) for a in range(4)]
         lows.append(lax.ppermute(low, ("tp",) + PS, pairs))
     base = base_phase(hidden, weight, 0, one)
     low, sent, kept = correct_phase(adapter_ids[None], lows, up, base)

time: 41.1 us -> 43.5 us (1.058)
  waiting for transfers between devices: 3.09 us -> 4.61 us
  starting transfers between devices: 16.1 us -> 17 us
    ppermute x4, starting transfers between devices: 6.34 us -> 9.13 us  [four_by_four(): lows.append(lax.ppermute(low, ('tp',) + PS, pairs))]
    ppermute x4, starting transfers between devices: 9.78 us -> 7.89 us  [swap(): lax.ppermute(value, 'tp', [(i, i ^ bit) for i in range(lax.axis_size('tp'...]
    ppermute x4, waiting for transfers between devices: 3.08 us -> 4.6 us  [swap(): lax.ppermute(value, 'tp', [(i, i ^ bit) for i in range(lax.axis_size('tp'...]
  transfers between devices with their start and end apart: 8 -> 8, of which waited for: 2 -> 2; matrix products, arithmetic and copies ran while one was open for 0% -> 0% of each run, Pallas kernels for 45% -> 43%
where the time goes in v14:
time: 43.5 us; the launch traced here: 43.4 us
  Pallas kernels  21.6 us (50%)
  starting transfers between devices  17 us (39%)
  waiting for transfers between devices  4.61 us (11%)
    pallas_call x1, Pallas kernels, base_phase(): pl.pallas_call(functools.partial(base_kernel, start), out_shape=jax.Shape...  13 us
    ppermute x4, starting transfers between devices, four_by_four(): lows.append(lax.ppermute(low, ('tp',) + PS, pairs))  9.13 us
    ppermute x4, starting transfers between devices, swap(): lax.ppermute(value, 'tp', [(i, i ^ bit) for i in range(lax.axis_size('tp'...  7.89 us
    pallas_call x1, Pallas kernels, last_phase(): pl.pallas_call(functools.partial(last_kernel, start), out_shape=(jax.Shap...  5.43 us
    ppermute x4, waiting for transfers between devices, swap(): lax.ppermute(value, 'tp', [(i, i ^ bit) for i in range(lax.axis_size('tp'...  4.6 us
    pallas_call x1, Pallas kernels, low_phase(): pl.pallas_call(low_kernel, out_shape=(jax.ShapeDtypeStruct((rows, rank),...  2 us
  transfers between devices with their start and end apart: 8, of which 2 were waited for; matrix products, arithmetic and copies ran while one was open for 0% of the time, Pallas kernels for 43%

profile of v14, /device:TPU:0, one launch (start us, length us, event | category | flops | bytes accessed | tf_op | source)
XLA Modules:
  0.0 43.4 jit_solution(9903946305602219246)
XLA Ops:
  0.0 2.0 %low_rank.1 = (f32[64,64]{1,0:T(8,128)S(1)}, bf16[64,8448]{1,0:T(8,128)(2,1)S(1)}) custom-call(bf16[64,8448]{1,0:T(8,128)(2,1)} %hidden.1, bf16[64,8448]{1,0:T(8,128)(2,1)} %bitcast.8), custom_call_target="tpu_custom_call" | custom-call | flops 69206016 | bytes 2162688 | tf_op jit(solution)/shard_map/low_rank/pallas_call | solution.py:66
  2.0 3.0 %collective-permute-start.3 = (f32[64,64]{1,0:T(8,128)S(1)}, f32[64,64]{1,0:T(8,128)S(1)}, u32[]{:S(2)}, u32[]{:S(2)}) collective-permute-start(f32[64,64]{1,0:T(8,128)S(1)} %get-tuple-element.16), channel_id=1, source_target_pairs={{0,2},{1,7},{2,11},{3,13},{4,0},{5,6},{6,10},{7,14},{8,1},{9,4},{1... | collective-permute-start | bytes 49160 | tf_op jit(solution)/shard_map/ppermute | solution.py:254
  5.0 0.6 %collective-permute-start.2 = (f32[64,64]{1,0:T(8,128)S(1)}, f32[64,64]{1,0:T(8,128)S(1)}, u32[]{:S(2)}, u32[]{:S(2)}) collective-permute-start(f32[64,64]{1,0:T(8,128)S(1)} %get-tuple-element.16), channel_id=1, source_target_pairs={{0,1},{1,4},{2,9},{3,15},{4,3},{5,7},{6,8},{7,13},{8,2},{9,5},{10,... | collective-permute-start | bytes 49160 | tf_op jit(solution)/shard_map/ppermute | solution.py:254
  5.6 4.9 %collective-permute-start.1 = (f32[64,64]{1,0:T(8,128)S(1)}, f32[64,64]{1,0:T(8,128)S(1)}, u32[]{:S(2)}, u32[]{:S(2)}) collective-permute-start(f32[64,64]{1,0:T(8,128)S(1)} %get-tuple-element.16), channel_id=1, source_target_pairs={{0,3},{1,5},{2,10},{3,14},{4,2},{5,4},{6,9},{7,12},{8,0},{9,6},{10... | collective-permute-start | bytes 49160 | tf_op jit(solution)/shard_map/ppermute | solution.py:254
  10.5 0.7 %collective-permute-start = (f32[64,64]{1,0:T(8,128)S(1)}, f32[64,64]{1,0:T(8,128)S(1)}, u32[]{:S(2)}, u32[]{:S(2)}) collective-permute-start(f32[64,64]{1,0:T(8,128)S(1)} %get-tuple-element.16), channel_id=1, source_target_pairs={{0,0},{1,6},{2,8},{3,12},{4,1},{5,5},{6,11},{7,15},{8,3},{9,7},{10... | collective-permute-start | bytes 49160 | tf_op jit(solution)/shard_map/ppermute | solution.py:254
  11.2 0.0 copy-start
  11.2 0.0 copy-start.2
  11.2 13.0 %base.1 = f32[64,2304]{1,0:T(8,128)S(1)} custom-call(bf16[64,8448]{1,0:T(8,128)(2,1)S(1)} %get-tuple-element.17.hidden, bf16[8448,3072]{1,0:T(8,128)(2,1)} %weight.3), custom_call_target="tpu_custom_call" | custom-call | flops 2491416576 | bytes 38928384 | tf_op jit(solution)/shard_map/base/pallas_call | solution.py:110
  24.2 0.0 collective-permute-done.3.low_d
  24.3 0.0 collective-permute-done.2.low_c
  24.3 0.0 collective-permute-done.1.low_b
  24.3 0.0 collective-permute-done.low_a
  24.3 0.0 copy-done
  24.3 0.0 copy-done.2
  24.3 0.4 adapter_term.1
  24.7 3.1 %collective-permute-start.4 = (bf16[32,2304]{1,0:T(8,128)(2,1)S(1)}, bf16[32,2304]{1,0:T(8,128)(2,1)S(1)}, u32[]{:S(2)}, u32[]{:S(2)}) collective-permute-start(bf16[32,2304]{1,0:T(8,128)(2,1)S(1)} %get-tuple-element.19), channel_id=1, source_target_pairs={{0,4},{4,0},{8,12},{12,8},{1,5},{5,1},{9,13},{13,9},{2,6},{6,2},{1... | collective-permute-start | bytes 442376 | tf_op jit(solution)/shard_map/ppermute | solution.py:244
  27.8 0.0 copy-start.1
  27.8 5.4 %last_base.1 = (bf16[32,768]{1,0:T(8,128)(2,1)S(1)}, f32[32,768]{1,0:T(8,128)S(1)}) custom-call(bf16[64,8448]{1,0:T(8,128)(2,1)S(1)} %get-tuple-element.17.hidden, bf16[8448,3072]{1,0:T(8,128)(2,1)} %weight.3, f32[64,64]{1,0:T(8,128)S(1)} %get-tuple-element.22.low, bf16[64,3072]{1,0:T(8,128)(2,1)S(1)} %bitcast.6), custom_call_target="tpu_custom_call" | custom-call | flops 830472192 | bytes 12976128 | tf_op jit(solution)/shard_map/last_base/pallas_call | solution.py:177
  33.2 0.1 collective-permute-start.6
  33.3 0.0 collective-permute-done.4.got
  33.4 2.9 %collective-permute-start.5 = (bf16[16,2304]{1,0:T(8,128)(2,1)S(1)}, bf16[16,2304]{1,0:T(8,128)(2,1)S(1)}, u32[]{:S(2)}, u32[]{:S(2)}) collective-permute-start(bf16[16,2304]{1,0:T(8,128)(2,1)S(1)} %get-tuple-element.21), channel_id=1, source_target_pairs={{0,8},{4,12},{8,0},{12,4},{1,9},{5,13},{9,1},{13,5},{2,10},{6,14},... | collective-permute-start | bytes 221192 | tf_op jit(solution)/shard_map/ppermute | solution.py:244
  36.3 1.6 %collective-permute-done.6.got = bf16[32,768]{1,0:T(8,128)(2,1)S(1)} collective-permute-done((bf16[32,768]{1,0:T(8,128)(2,1)S(1)}, bf16[32,768]{1,0:T(8,128)(2,1)S(1)}, u32[]{:S(2)}, u32[]{:S(2)}) %collective-permute-start.6) | collective-permute-done | bytes 49184 | tf_op jit(solution)/shard_map/ppermute | solution.py:244
  37.9 1.8 %collective-permute-start.7 = (bf16[16,768]{1,0:T(8,128)(2,1)S(1)}, bf16[16,768]{1,0:T(8,128)(2,1)S(1)}, u32[]{:S(2)}, u32[]{:S(2)}) collective-permute-start(bf16[16,768]{1,0:T(8,128)(2,1)S(1)} %get-tuple-element.26), channel_id=1, source_target_pairs={{0,8},{4,12},{8,0},{12,4},{1,9},{5,13},{9,1},{13,5},{2,10},{6,14},... | collective-permute-start | bytes 73736 | tf_op jit(solution)/shard_map/ppermute | solution.py:244
  39.7 3.0 %collective-permute-done.7.got_two = bf16[16,768]{1,0:T(8,128)(2,1)S(1)} collective-permute-done((bf16[16,768]{1,0:T(8,128)(2,1)S(1)}, bf16[16,768]{1,0:T(8,128)(2,1)S(1)}, u32[]{:S(2)}, u32[]{:S(2)}) %collective-permute-start.7) | collective-permute-done | bytes 24608 | tf_op jit(solution)/shard_map/ppermute | solution.py:244
  42.7 0.0 collective-permute-done.5.got_one
  42.7 0.0 copy-done.1
  42.7 0.7 %finish.1 = bf16[16,3072]{1,0:T(8,128)(2,1)} custom-call(bf16[16,3072]{1,0:T(8,128)(2,1)S(1)} %copy-done.1, f32[16,2304]{1,0:T(8,128)S(1)} %get-tuple-element.20.total_one, bf16[16,2304]{1,0:T(8,128)(2,1)S(1)} %collective-permute-done.5.got_one, f32[16,768]{1,0:T(8,128)S(1)} %get-tuple-element.25.total_two, bf16[16,768]{1,0:T(8,128)(2,1)S(1)} %collective-permute-done.7.got_two), custom_call_target="tpu_custom_call" | custom-call | tf_op jit(solution)/shard_map/finish/pallas_call | solution.py:233
  (2 shorter events, 0.0 us)
Async XLA Ops:
  2.0 22.2 %collective-permute-start.3 = (f32[64,64]{1,0:T(8,128)S(1)}, f32[64,64]{1,0:T(8,128)S(1)}, u32[]{:S(2)}, u32[]{:S(2)}) collective-permute-start(f32[64,64]{1,0:T(8,128)S(1)} %get-tuple-element.16), channel_id=1, source_target_pairs={{0,2},{1,7},{2,11},{3,13},{4,0},{5,6},{6,10},{7,14},{8,1},{9,4},{1... | collective-permute-start | bytes 49160 | tf_op jit(solution)/shard_map/ppermute | solution.py:254
  5.0 19.2 %collective-permute-start.2 = (f32[64,64]{1,0:T(8,128)S(1)}, f32[64,64]{1,0:T(8,128)S(1)}, u32[]{:S(2)}, u32[]{:S(2)}) collective-permute-start(f32[64,64]{1,0:T(8,128)S(1)} %get-tuple-element.16), channel_id=1, source_target_pairs={{0,1},{1,4},{2,9},{3,15},{4,3},{5,7},{6,8},{7,13},{8,2},{9,5},{10,... | collective-permute-start | bytes 49160 | tf_op jit(solution)/shard_map/ppermute | solution.py:254
  5.6 18.7 %collective-permute-start.1 = (f32[64,64]{1,0:T(8,128)S(1)}, f32[64,64]{1,0:T(8,128)S(1)}, u32[]{:S(2)}, u32[]{:S(2)}) collective-permute-start(f32[64,64]{1,0:T(8,128)S(1)} %get-tuple-element.16), channel_id=1, source_target_pairs={{0,3},{1,5},{2,10},{3,14},{4,2},{5,4},{6,9},{7,12},{8,0},{9,6},{10... | collective-permute-start | bytes 49160 | tf_op jit(solution)/shard_map/ppermute | solution.py:254
  10.5 13.8 %collective-permute-start = (f32[64,64]{1,0:T(8,128)S(1)}, f32[64,64]{1,0:T(8,128)S(1)}, u32[]{:S(2)}, u32[]{:S(2)}) collective-permute-start(f32[64,64]{1,0:T(8,128)S(1)} %get-tuple-element.16), channel_id=1, source_target_pairs={{0,0},{1,6},{2,8},{3,12},{4,1},{5,5},{6,11},{7,15},{8,3},{9,7},{10... | collective-permute-start | bytes 49160 | tf_op jit(solution)/shard_map/ppermute | solution.py:254
  11.2 13.1 %copy-start = (bf16[1,64,3072]{2,1,0:T(8,128)(2,1)S(1)}, bf16[1,64,3072]{2,1,0:T(8,128)(2,1)}, u32[]{:S(2)}) copy-start(bf16[1,64,3072]{2,1,0:T(8,128)(2,1)} %param.10) | copy-start | bytes 1179652
  11.2 13.1 %copy-start.2 = (s32[64]{0:T(128)S(1)}, s32[64]{0:T(128)}, u32[]{:S(2)}) copy-start(s32[64]{0:T(128)} %param.7) | copy-start | bytes 772
  24.7 8.6 %collective-permute-start.4 = (bf16[32,2304]{1,0:T(8,128)(2,1)S(1)}, bf16[32,2304]{1,0:T(8,128)(2,1)S(1)}, u32[]{:S(2)}, u32[]{:S(2)}) collective-permute-start(bf16[32,2304]{1,0:T(8,128)(2,1)S(1)} %get-tuple-element.19), channel_id=1, source_target_pairs={{0,4},{4,0},{8,12},{12,8},{1,5},{5,1},{9,13},{13,9},{2,6},{6,2},{1... | collective-permute-start | bytes 442376 | tf_op jit(solution)/shard_map/ppermute | solution.py:244
  27.8 14.9 %copy-start.1 = (bf16[16,3072]{1,0:T(8,128)(2,1)S(1)}, bf16[16,3072]{1,0:T(8,128)(2,1)}, u32[]{:S(2)}) copy-start(bf16[16,3072]{1,0:T(8,128)(2,1)} %residual.1) | copy-start | bytes 294916
  33.2 4.6 %collective-permute-start.6 = (bf16[32,768]{1,0:T(8,128)(2,1)S(1)}, bf16[32,768]{1,0:T(8,128)(2,1)S(1)}, u32[]{:S(2)}, u32[]{:S(2)}) collective-permute-start(bf16[32,768]{1,0:T(8,128)(2,1)S(1)} %get-tuple-element.24), channel_id=1, source_target_pairs={{0,4},{4,0},{8,12},{12,8},{1,5},{5,1},{9,13},{13,9},{2,6},{6,2},{1... | collective-permute-start | bytes 147464 | tf_op jit(solution)/shard_map/ppermute | solution.py:244
  33.4 9.3 %collective-permute-start.5 = (bf16[16,2304]{1,0:T(8,128)(2,1)S(1)}, bf16[16,2304]{1,0:T(8,128)(2,1)S(1)}, u32[]{:S(2)}, u32[]{:S(2)}) collective-permute-start(bf16[16,2304]{1,0:T(8,128)(2,1)S(1)} %get-tuple-element.21), channel_id=1, source_target_pairs={{0,8},{4,12},{8,0},{12,4},{1,9},{5,13},{9,1},{13,5},{2,10},{6,14},... | collective-permute-start | bytes 221192 | tf_op jit(solution)/shard_map/ppermute | solution.py:244
  37.9 4.8 %collective-permute-start.7 = (bf16[16,768]{1,0:T(8,128)(2,1)S(1)}, bf16[16,768]{1,0:T(8,128)(2,1)S(1)}, u32[]{:S(2)}, u32[]{:S(2)}) collective-permute-start(bf16[16,768]{1,0:T(8,128)(2,1)S(1)} %get-tuple-element.26), channel_id=1, source_target_pairs={{0,8},{4,12},{8,0},{12,4},{1,9},{5,13},{9,1},{13,5},{2,10},{6,14},... | collective-permute-start | bytes 73736 | tf_op jit(solution)/shard_map/ppermute | solution.py:244

commit v15 on v12

--- a/solution.py
+++ b/solution.py
@@ -9,6 +9,7 @@
 
 WIDTHS = (2304, 768)
 DEPTH = 768
+THIRDS = 3
 PS = ("page", "sub")
 VMEM = pl.BlockSpec(memory_space=pltpu.VMEM)
 HBM = pl.BlockSpec(memory_space=pltpu.HBM)
@@ -38,20 +39,30 @@
 
 
 def low_kernel(hidden, rank_down, low, hidden_here, down_here, got):
-    copies = [
-        pltpu.make_async_copy(hidden, hidden_here, got.at[0]),
-        pltpu.make_async_copy(rank_down, down_here, got.at[1]),
-    ]
-    for copy in copies:
-        copy.start()
-    for copy in copies:
-        copy.wait()
-    low[...] = lax.dot_general(
-        hidden_here[...],
-        down_here[...],
-        (((1,), (1,)), ((), ())),
-        preferred_element_type=jnp.float32,
-    )
+    depth = hidden.shape[1] // THIRDS
+    copies = []
+    for third in range(THIRDS):
+        at = slice(third * depth, (third + 1) * depth)
+        pair = [(hidden, hidden_here), (rank_down, down_here)]
+        copies.append(
+            [
+                pltpu.make_async_copy(source.at[:, at], here.at[:, at], got.at[2 * third + index])
+                for index, (source, here) in enumerate(pair)
+            ]
+        )
+        for copy in copies[third]:
+            copy.start()
+    for third in range(THIRDS):
+        for copy in copies[third]:
+            copy.wait()
+        at = slice(third * depth, (third + 1) * depth)
+        product = lax.dot_general(
+            hidden_here[:, at],
+            down_here[:, at],
+            (((1,), (1,)), ((), ())),
+            preferred_element_type=jnp.float32,
+        )
+        low[...] = product if third == 0 else low[...] + product
 
 
 def low_phase(hidden, rank_down):
@@ -67,7 +78,7 @@
         out_specs=(VMEM,) * 2,
         scratch_shapes=[
             pltpu.VMEM(rank_down.shape, rank_down.dtype),
-            pltpu.SemaphoreType.DMA((2,)),
+            pltpu.SemaphoreType.DMA((2 * THIRDS,)),
         ],
         compiler_params=pltpu.CompilerParams(vmem_limit_bytes=52 << 20),
         cost_estimate=pl.CostEstimate(
@@ -299,6 +310,7 @@
         and rank_up.shape[0] == 1
         and residual.shape == (16, sum(WIDTHS))
         and hidden_units.shape[1] % DEPTH == 0
+        and hidden_units.shape[1] % (THIRDS * 128) == 0
     )
     form = four_by_four if fits else any_size
     return form(hidden_units, adapter_ids, down_projection_weight, rank_down, rank_up, residual)

time: 41.1 us -> 41.1 us (level)
  no operation moved by 1% of the time
where the time goes in v15:
time: 41.1 us; the launch traced here: 41 us
  Pallas kernels  21.6 us (53%)
  starting transfers between devices  16.1 us (39%)
  waiting for transfers between devices  3.13 us (8%)
    pallas_call x1, Pallas kernels, base_phase(): pl.pallas_call(functools.partial(base_kernel, start), out_shape=jax.Shape...  13 us
    ppermute x4, starting transfers between devices, swap(): lax.ppermute(value, 'tp', [(i, i ^ bit) for i in range(lax.axis_size('tp'...  9.79 us
    ppermute x4, starting transfers between devices, four_by_four(): lows.append(lax.ppermute(low, ('tp',) + PS, pairs))  6.32 us
    pallas_call x1, Pallas kernels, last_phase(): pl.pallas_call(functools.partial(last_kernel, start), out_shape=(jax.Shap...  5.42 us
    ppermute x4, waiting for transfers between devices, swap(): lax.ppermute(value, 'tp', [(i, i ^ bit) for i in range(lax.axis_size('tp'...  3.11 us
    pallas_call x1, Pallas kernels, low_phase(): pl.pallas_call(low_kernel, out_shape=(jax.ShapeDtypeStruct((rows, rank),...  2.03 us
  transfers between devices with their start and end apart: 8, of which 2 were waited for; matrix products, arithmetic and copies ran while one was open for 0% of the time, Pallas kernels for 45%

profile of v15, /device:TPU:0, one launch (start us, length us, event | category | flops | bytes accessed | tf_op | source)
XLA Modules:
  0.0 41.0 jit_solution(12531548106430334811)
XLA Ops:
  0.0 2.0 %low_rank.1 = (f32[64,64]{1,0:T(8,128)S(1)}, bf16[64,8448]{1,0:T(8,128)(2,1)S(1)}) custom-call(bf16[64,8448]{1,0:T(8,128)(2,1)} %hidden.1, bf16[64,8448]{1,0:T(8,128)(2,1)} %bitcast.8), custom_call_target="tpu_custom_call" | custom-call | flops 69206016 | bytes 2162688 | tf_op jit(solution)/shard_map/low_rank/pallas_call | solution.py:71
  2.0 2.4 %collective-permute-start.3 = (f32[64,64]{1,0:T(8,128)S(1)}, f32[64,64]{1,0:T(8,128)S(1)}, u32[]{:S(2)}, u32[]{:S(2)}) collective-permute-start(f32[64,64]{1,0:T(8,128)S(1)} %get-tuple-element.16), channel_id=1, source_target_pairs={{0,3},{1,7},{2,11},{3,15},{4,0},{5,4},{6,8},{7,12},{8,1},{9,5},{10... | collective-permute-start | bytes 49160 | tf_op jit(solution)/shard_map/ppermute | solution.py:259
  4.5 2.6 %collective-permute-start.2 = (f32[64,64]{1,0:T(8,128)S(1)}, f32[64,64]{1,0:T(8,128)S(1)}, u32[]{:S(2)}, u32[]{:S(2)}) collective-permute-start(f32[64,64]{1,0:T(8,128)S(1)} %get-tuple-element.16), channel_id=1, source_target_pairs={{0,2},{1,6},{2,10},{3,14},{4,3},{5,7},{6,11},{7,15},{8,0},{9,4},{1... | collective-permute-start | bytes 49160 | tf_op jit(solution)/shard_map/ppermute | solution.py:259
  7.1 0.6 %collective-permute-start.1 = (f32[64,64]{1,0:T(8,128)S(1)}, f32[64,64]{1,0:T(8,128)S(1)}, u32[]{:S(2)}, u32[]{:S(2)}) collective-permute-start(f32[64,64]{1,0:T(8,128)S(1)} %get-tuple-element.16), channel_id=1, source_target_pairs={{0,1},{1,5},{2,9},{3,13},{4,2},{5,6},{6,10},{7,14},{8,3},{9,7},{10... | collective-permute-start | bytes 49160 | tf_op jit(solution)/shard_map/ppermute | solution.py:259
  7.7 0.7 %collective-permute-start = (f32[64,64]{1,0:T(8,128)S(1)}, f32[64,64]{1,0:T(8,128)S(1)}, u32[]{:S(2)}, u32[]{:S(2)}) collective-permute-start(f32[64,64]{1,0:T(8,128)S(1)} %get-tuple-element.16), channel_id=1, source_target_pairs={{0,0},{1,4},{2,8},{3,12},{4,1},{5,5},{6,9},{7,13},{8,2},{9,6},{10,... | collective-permute-start | bytes 49160 | tf_op jit(solution)/shard_map/ppermute | solution.py:259
  8.4 0.0 copy-start
  8.4 0.0 copy-start.2
  8.4 13.0 %base.1 = f32[64,2304]{1,0:T(8,128)S(1)} custom-call(bf16[64,8448]{1,0:T(8,128)(2,1)S(1)} %get-tuple-element.17.hidden, bf16[8448,3072]{1,0:T(8,128)(2,1)} %weight.3), custom_call_target="tpu_custom_call" | custom-call | flops 2491416576 | bytes 38928384 | tf_op jit(solution)/shard_map/base/pallas_call | solution.py:115
  21.4 0.0 collective-permute-done.3.low_d
  21.5 0.0 collective-permute-done.2.low_c
  21.5 0.0 collective-permute-done.1.low_b
  21.5 0.0 collective-permute-done.low_a
  21.5 0.0 copy-done
  21.5 0.0 copy-done.2
  21.5 0.4 adapter_term.1
  21.9 4.0 %collective-permute-start.4 = (bf16[32,2304]{1,0:T(8,128)(2,1)S(1)}, bf16[32,2304]{1,0:T(8,128)(2,1)S(1)}, u32[]{:S(2)}, u32[]{:S(2)}) collective-permute-start(bf16[32,2304]{1,0:T(8,128)(2,1)S(1)} %get-tuple-element.19), channel_id=1, source_target_pairs={{0,4},{4,0},{8,12},{12,8},{1,5},{5,1},{9,13},{13,9},{2,6},{6,2},{1... | collective-permute-start | bytes 442376 | tf_op jit(solution)/shard_map/ppermute | solution.py:249
  25.9 0.0 copy-start.1
  25.9 5.4 %last_base.1 = (bf16[32,768]{1,0:T(8,128)(2,1)S(1)}, f32[32,768]{1,0:T(8,128)S(1)}) custom-call(bf16[64,8448]{1,0:T(8,128)(2,1)S(1)} %get-tuple-element.17.hidden, bf16[8448,3072]{1,0:T(8,128)(2,1)} %weight.3, f32[64,64]{1,0:T(8,128)S(1)} %get-tuple-element.22.low, bf16[64,3072]{1,0:T(8,128)(2,1)S(1)} %bitcast.6), custom_call_target="tpu_custom_call" | custom-call | flops 830472192 | bytes 12976128 | tf_op jit(solution)/shard_map/last_base/pallas_call | solution.py:182
  31.3 0.1 collective-permute-start.6
  31.4 0.0 collective-permute-done.4.got
  31.4 2.9 %collective-permute-start.5 = (bf16[16,2304]{1,0:T(8,128)(2,1)S(1)}, bf16[16,2304]{1,0:T(8,128)(2,1)S(1)}, u32[]{:S(2)}, u32[]{:S(2)}) collective-permute-start(bf16[16,2304]{1,0:T(8,128)(2,1)S(1)} %get-tuple-element.21), channel_id=1, source_target_pairs={{0,8},{4,12},{8,0},{12,4},{1,9},{5,13},{9,1},{13,5},{2,10},{6,14},... | collective-permute-start | bytes 221192 | tf_op jit(solution)/shard_map/ppermute | solution.py:249
  34.3 1.1 %collective-permute-done.6.got = bf16[32,768]{1,0:T(8,128)(2,1)S(1)} collective-permute-done((bf16[32,768]{1,0:T(8,128)(2,1)S(1)}, bf16[32,768]{1,0:T(8,128)(2,1)S(1)}, u32[]{:S(2)}, u32[]{:S(2)}) %collective-permute-start.6) | collective-permute-done | bytes 49184 | tf_op jit(solution)/shard_map/ppermute | solution.py:249
  35.5 2.8 %collective-permute-start.7 = (bf16[16,768]{1,0:T(8,128)(2,1)S(1)}, bf16[16,768]{1,0:T(8,128)(2,1)S(1)}, u32[]{:S(2)}, u32[]{:S(2)}) collective-permute-start(bf16[16,768]{1,0:T(8,128)(2,1)S(1)} %get-tuple-element.26), channel_id=1, source_target_pairs={{0,8},{4,12},{8,0},{12,4},{1,9},{5,13},{9,1},{13,5},{2,10},{6,14},... | collective-permute-start | bytes 73736 | tf_op jit(solution)/shard_map/ppermute | solution.py:249
  38.3 2.0 %collective-permute-done.7.got_two = bf16[16,768]{1,0:T(8,128)(2,1)S(1)} collective-permute-done((bf16[16,768]{1,0:T(8,128)(2,1)S(1)}, bf16[16,768]{1,0:T(8,128)(2,1)S(1)}, u32[]{:S(2)}, u32[]{:S(2)}) %collective-permute-start.7) | collective-permute-done | bytes 24608 | tf_op jit(solution)/shard_map/ppermute | solution.py:249
  40.3 0.0 collective-permute-done.5.got_one
  40.3 0.0 copy-done.1
  40.3 0.7 %finish.1 = bf16[16,3072]{1,0:T(8,128)(2,1)} custom-call(bf16[16,3072]{1,0:T(8,128)(2,1)S(1)} %copy-done.1, f32[16,2304]{1,0:T(8,128)S(1)} %get-tuple-element.20.total_one, bf16[16,2304]{1,0:T(8,128)(2,1)S(1)} %collective-permute-done.5.got_one, f32[16,768]{1,0:T(8,128)S(1)} %get-tuple-element.25.total_two, bf16[16,768]{1,0:T(8,128)(2,1)S(1)} %collective-permute-done.7.got_two), custom_call_target="tpu_custom_call" | custom-call | tf_op jit(solution)/shard_map/finish/pallas_call | solution.py:238
  (2 shorter events, 0.0 us)
Async XLA Ops:
  2.0 19.4 %collective-permute-start.3 = (f32[64,64]{1,0:T(8,128)S(1)}, f32[64,64]{1,0:T(8,128)S(1)}, u32[]{:S(2)}, u32[]{:S(2)}) collective-permute-start(f32[64,64]{1,0:T(8,128)S(1)} %get-tuple-element.16), channel_id=1, source_target_pairs={{0,3},{1,7},{2,11},{3,15},{4,0},{5,4},{6,8},{7,12},{8,1},{9,5},{10... | collective-permute-start | bytes 49160 | tf_op jit(solution)/shard_map/ppermute | solution.py:259
  4.5 17.0 %collective-permute-start.2 = (f32[64,64]{1,0:T(8,128)S(1)}, f32[64,64]{1,0:T(8,128)S(1)}, u32[]{:S(2)}, u32[]{:S(2)}) collective-permute-start(f32[64,64]{1,0:T(8,128)S(1)} %get-tuple-element.16), channel_id=1, source_target_pairs={{0,2},{1,6},{2,10},{3,14},{4,3},{5,7},{6,11},{7,15},{8,0},{9,4},{1... | collective-permute-start | bytes 49160 | tf_op jit(solution)/shard_map/ppermute | solution.py:259
  7.1 14.4 %collective-permute-start.1 = (f32[64,64]{1,0:T(8,128)S(1)}, f32[64,64]{1,0:T(8,128)S(1)}, u32[]{:S(2)}, u32[]{:S(2)}) collective-permute-start(f32[64,64]{1,0:T(8,128)S(1)} %get-tuple-element.16), channel_id=1, source_target_pairs={{0,1},{1,5},{2,9},{3,13},{4,2},{5,6},{6,10},{7,14},{8,3},{9,7},{10... | collective-permute-start | bytes 49160 | tf_op jit(solution)/shard_map/ppermute | solution.py:259
  7.7 13.8 %collective-permute-start = (f32[64,64]{1,0:T(8,128)S(1)}, f32[64,64]{1,0:T(8,128)S(1)}, u32[]{:S(2)}, u32[]{:S(2)}) collective-permute-start(f32[64,64]{1,0:T(8,128)S(1)} %get-tuple-element.16), channel_id=1, source_target_pairs={{0,0},{1,4},{2,8},{3,12},{4,1},{5,5},{6,9},{7,13},{8,2},{9,6},{10,... | collective-permute-start | bytes 49160 | tf_op jit(solution)/shard_map/ppermute | solution.py:259
  8.4 13.1 %copy-start = (bf16[1,64,3072]{2,1,0:T(8,128)(2,1)S(1)}, bf16[1,64,3072]{2,1,0:T(8,128)(2,1)}, u32[]{:S(2)}) copy-start(bf16[1,64,3072]{2,1,0:T(8,128)(2,1)} %param.10) | copy-start | bytes 1179652
  8.4 13.1 %copy-start.2 = (s32[64]{0:T(128)S(1)}, s32[64]{0:T(128)}, u32[]{:S(2)}) copy-start(s32[64]{0:T(128)} %param.7) | copy-start | bytes 772
  21.9 9.5 %collective-permute-start.4 = (bf16[32,2304]{1,0:T(8,128)(2,1)S(1)}, bf16[32,2304]{1,0:T(8,128)(2,1)S(1)}, u32[]{:S(2)}, u32[]{:S(2)}) collective-permute-start(bf16[32,2304]{1,0:T(8,128)(2,1)S(1)} %get-tuple-element.19), channel_id=1, source_target_pairs={{0,4},{4,0},{8,12},{12,8},{1,5},{5,1},{9,13},{13,9},{2,6},{6,2},{1... | collective-permute-start | bytes 442376 | tf_op jit(solution)/shard_map/ppermute | solution.py:249
  25.9 14.4 %copy-start.1 = (bf16[16,3072]{1,0:T(8,128)(2,1)S(1)}, bf16[16,3072]{1,0:T(8,128)(2,1)}, u32[]{:S(2)}) copy-start(bf16[16,3072]{1,0:T(8,128)(2,1)} %residual.1) | copy-start | bytes 294916
  31.3 4.2 %collective-permute-start.6 = (bf16[32,768]{1,0:T(8,128)(2,1)S(1)}, bf16[32,768]{1,0:T(8,128)(2,1)S(1)}, u32[]{:S(2)}, u32[]{:S(2)}) collective-permute-start(bf16[32,768]{1,0:T(8,128)(2,1)S(1)} %get-tuple-element.24), channel_id=1, source_target_pairs={{0,4},{4,0},{8,12},{12,8},{1,5},{5,1},{9,13},{13,9},{2,6},{6,2},{1... | collective-permute-start | bytes 147464 | tf_op jit(solution)/shard_map/ppermute | solution.py:249
  31.4 8.8 %collective-permute-start.5 = (bf16[16,2304]{1,0:T(8,128)(2,1)S(1)}, bf16[16,2304]{1,0:T(8,128)(2,1)S(1)}, u32[]{:S(2)}, u32[]{:S(2)}) collective-permute-start(bf16[16,2304]{1,0:T(8,128)(2,1)S(1)} %get-tuple-element.21), channel_id=1, source_target_pairs={{0,8},{4,12},{8,0},{12,4},{1,9},{5,13},{9,1},{13,5},{2,10},{6,14},... | collective-permute-start | bytes 221192 | tf_op jit(solution)/shard_map/ppermute | solution.py:249
  35.5 4.8 %collective-permute-start.7 = (bf16[16,768]{1,0:T(8,128)(2,1)S(1)}, bf16[16,768]{1,0:T(8,128)(2,1)S(1)}, u32[]{:S(2)}, u32[]{:S(2)}) collective-permute-start(bf16[16,768]{1,0:T(8,128)(2,1)S(1)} %get-tuple-element.26), channel_id=1, source_target_pairs={{0,8},{4,12},{8,0},{12,4},{1,9},{5,13},{9,1},{13,5},{2,10},{6,14},... | collective-permute-start | bytes 73736 | tf_op jit(solution)/shard_map/ppermute | solution.py:249
